TPU v7x, 32 devices: a whole 2x2x4 slice. The times are simulated.
32 devices in a mesh: dp: 2 (over x), expert: 16 (over z, y, core).
Axes of the slice: x: 2, y: 2, z: 4, core: 2. Of those that a mesh axis runs over, the one named last changes fastest.
Arguments:
- grad_out: bfloat16 [2048, 4096], P('expert', 'dp'), may hold values from -6 to 6
- routing: int32 [2048, 6], P('expert'), may hold values from 0 to 15, all different within a row; in each aligned block of 128 rows (0 to 127, 128 to 255, ...) at most 56 rows name the same one
- gates: float32 [2048, 6], P('expert'), may hold values from 0.05 to 1
- scales: float32 [2048], P('expert'), may hold values from 0.25 to 4
- saved_gate: bfloat16 [16, 1408, 896], P('expert'), may hold values from -6 to 6
- saved_up: bfloat16 [16, 1408, 896], P('expert'), may hold values from -6 to 6
- w_gate: bfloat16 [16, 4096, 1408], P('expert', 'dp'), may hold values from -0.09375 to 0.09375
- w_up: bfloat16 [16, 4096, 1408], P('expert', 'dp'), may hold values from -0.09375 to 0.09375
- w_down: bfloat16 [16, 1408, 4096], P('expert', None, 'dp'), may hold values from -0.15625 to 0.15625
Outputs:
- grad_x: bfloat16 [2048, 4096], P('expert', 'dp')
- grad_down: bfloat16 [16, 1408, 4096], P('expert', None, 'dp')
Inputs may be any that keep to these rules, and one draw needn't show every extreme that they name: `routing`: each row names 6 different experts; within each token group of 128 rows no expert is named more than 56 times, a bound that some block reaches.
All inputs are finite; a program needn't handle non-finite values.
Results may differ from a plain program's by a relative error of at most 0.027.
Values may be sent and summed in bfloat16 or wider, within the bound.
No kernel may reach another device: no remote copies, remote signals or barrier semaphores. Data moves between devices by JAX's collectives and lax.ppermute only.
A program may use at most 128 MiB of HBM per device.

v0:
```python
import functools

import jax
import jax.numpy as jnp
import numpy as np
from jax import lax
from jax.experimental import pallas as pl
from jax.experimental.pallas import tpu as pltpu
from jax.sharding import PartitionSpec as P

LANES = 128
PIECES = 4
NT = (((1,), (1,)), ((), ()))
TN = (((0,), (0,)), ((), ()))
VMEM = pl.BlockSpec(memory_space=pltpu.VMEM)
ANY = pl.BlockSpec(memory_space=pl.ANY)
FREE = pl.CostEstimate(flops=0, bytes_accessed=0, transcendentals=0)


def activation_grad(hidden_grad, gate_pre, up_pre):
    g = gate_pre.astype(jnp.float32)
    u = up_pre.astype(jnp.float32)
    sig = jax.nn.sigmoid(g)
    dh = hidden_grad.astype(jnp.float32)
    gate_grad = (dh * u * sig * (1.0 + g * (1.0 - sig))).astype(jnp.bfloat16)
    up_grad = (dh * g * sig).astype(jnp.bfloat16)
    return (gate_grad, up_grad)


def contract(left, weights):
    return lax.dot_general(
        left, weights, (((0,), (1,)), ((), ())), preferred_element_type=jnp.float32
    )


def exchange_local(grad_out, routing, gates, scales, saved_gate, saved_up, w_gate, w_up, w_down):
    tok_rows, dcols = grad_out.shape
    topk = routing.shape[1]
    groups = lax.axis_size("expert")
    experts = groups * w_gate.shape[0]
    slots = saved_gate.shape[2]
    capacity = slots // groups
    flat_route = routing.reshape(-1)
    hot = (flat_route[:, None] == jnp.arange(experts, dtype=jnp.int32)[None, :]).astype(jnp.int32)
    position = jnp.sum(hot * (jnp.cumsum(hot, axis=0) - 1), axis=1)
    target = flat_route * capacity + position
    select = jnp.arange(experts * capacity, dtype=jnp.int32)[:, None] == target[None, :]
    weight = (gates * scales[:, None]).reshape(-1)
    slot_factor = jnp.sum(jnp.where(select, weight[None, :], 0.0), axis=1)
    collect = jnp.any(select.reshape(experts * capacity, tok_rows, topk), axis=2).astype(
        jnp.bfloat16
    )
    owned_rows = jnp.dot(collect, grad_out, preferred_element_type=jnp.float32)
    sending = (
        (slot_factor[:, None] * owned_rows).astype(jnp.bfloat16).reshape(experts, capacity, dcols)
    )
    arrived = lax.all_to_all(sending, "expert", split_axis=0, concat_axis=0, tiled=True).reshape(
        slots, dcols
    )
    wdown = w_down[0]
    wgate = w_gate[0]
    wup = w_up[0]
    sgate = saved_gate[0]
    sup = saved_up[0]
    partial_value = lax.dot_general(
        wdown, arrived, (((1,), (1,)), ((), ())), preferred_element_type=jnp.float32
    )
    reduced = lax.psum_scatter(
        partial_value.astype(jnp.bfloat16), "dp", scatter_dimension=0, tiled=True
    )
    hidden_grad = lax.all_gather(reduced, "dp", axis=0, tiled=True)
    gate_grad, up_grad = activation_grad(hidden_grad, sgate, sup)
    slot_grad = contract(gate_grad, wgate) + contract(up_grad, wup)
    gate_full = sgate.astype(jnp.float32)
    hidden = (gate_full * jax.nn.sigmoid(gate_full) * sup.astype(jnp.float32)).astype(jnp.bfloat16)
    grad_down = jnp.dot(hidden, arrived, preferred_element_type=jnp.float32).astype(jnp.bfloat16)
    returning = slot_grad.astype(jnp.bfloat16).reshape(groups, capacity, dcols)
    back = lax.all_to_all(returning, "expert", split_axis=0, concat_axis=0, tiled=True).reshape(
        experts * capacity, dcols
    )
    grad_x = lax.dot_general(
        collect, back, (((0,), (0,)), ((), ())), preferred_element_type=jnp.float32
    )
    return (grad_x.astype(jnp.bfloat16), grad_down[None])


def ring_of(chips):
    return list(range(0, chips, 2)) + list(range(1, chips, 2))[::-1]


def pack_kernel(experts, rows_ref, routing_ref, gates_ref, scales_ref, out_ref):
    topk, tok = routing_ref.shape
    dcols = rows_ref.shape[1]
    lanes = out_ref.shape[1] - dcols
    out_ref[:, :dcols] = rows_ref[...]
    line = lax.broadcasted_iota(jnp.int32, (lanes, tok), 0)
    expert = line % experts
    piece = line // experts
    hot = jnp.zeros((lanes, tok), jnp.float32)
    factor = jnp.zeros((lanes, tok), jnp.float32)
    for k in range(topk):
        same = routing_ref[k : k + 1] == expert
        hot += jnp.where(same, 1.0, 0.0)
        factor += jnp.where(same, gates_ref[k : k + 1] * scales_ref[...], 0.0)
    row = lax.broadcasted_iota(jnp.int32, (tok, tok), 0)
    column = lax.broadcasted_iota(jnp.int32, (tok, tok), 1)
    earlier = jnp.where(row < column, 1.0, 0.0).astype(jnp.bfloat16)
    before = jnp.dot(hot.astype(jnp.bfloat16), earlier, preferred_element_type=jnp.float32)
    high = factor.astype(jnp.bfloat16)
    rest = factor - high.astype(jnp.float32)
    middle = rest.astype(jnp.bfloat16)
    low = rest - middle.astype(jnp.float32)
    meta = jnp.where(piece == 0, hot * (before + 1.0), 0.0)
    meta = jnp.where(piece == 1, high.astype(jnp.float32), meta)
    meta = jnp.where(piece == 2, middle.astype(jnp.float32), meta)
    meta = jnp.where(piece == 3, low, meta)
    out_ref[:, dcols:] = meta.T.astype(jnp.bfloat16)


def whole(shape):
    return pl.BlockSpec(shape, lambda i: (0,) * len(shape))


def pack(rows, routing, gates, scales, experts):
    tok, dcols = rows.shape
    lanes = -(-PIECES * experts // LANES) * LANES
    operands = [
        pltpu.with_memory_space_constraint(a, pltpu.HBM)
        for a in (rows, routing.T, gates.T, scales[None])
    ]
    return pl.pallas_call(
        functools.partial(pack_kernel, experts),
        grid=(1,),
        in_specs=[whole(a.shape) for a in operands],
        out_specs=whole((tok, dcols + lanes)),
        out_shape=jax.ShapeDtypeStruct((tok, dcols + lanes), jnp.bfloat16),
        compiler_params=pltpu.CompilerParams(vmem_limit_bytes=8 << 20),
        cost_estimate=FREE,
        name="pack",
    )(*operands)


def prep_kernel(capacity, ids_ref, gate_ref, up_ref, to_gate_ref, to_up_ref, hidden_ref, turned):
    g = gate_ref[...].astype(jnp.float32)
    u = up_ref[...].astype(jnp.float32)
    sig = jax.nn.sigmoid(g)
    swish = g * sig
    hidden_ref[...] = (swish * u).astype(jnp.bfloat16)
    turned[0] = (u * sig * (1.0 + g * (1.0 - sig))).T
    turned[1] = swish.T
    for i in range(to_gate_ref.shape[0]):
        start = pl.multiple_of(ids_ref[i] * capacity, 8)
        for k, ref in enumerate((to_gate_ref, to_up_ref)):
            ref[i] = turned[k, pl.ds(start, capacity)].astype(jnp.bfloat16)


def prep(ids, gate, up, capacity):
    ff, slots = gate.shape
    groups = slots // capacity
    tile = LANES
    out = jax.ShapeDtypeStruct((groups, capacity, ff), jnp.bfloat16)
    spec = pl.BlockSpec((tile, slots), lambda i, ids: (i, 0))
    out_spec = pl.BlockSpec((groups, capacity, tile), lambda i, ids: (0, 0, i))
    operands = [pltpu.with_memory_space_constraint(a, pltpu.HBM) for a in (gate, up)]
    return pl.pallas_call(
        functools.partial(prep_kernel, capacity),
        grid_spec=pltpu.PrefetchScalarGridSpec(
            num_scalar_prefetch=1,
            grid=(ff // tile,),
            in_specs=[spec, spec],
            out_specs=[out_spec, out_spec, spec],
            scratch_shapes=[pltpu.VMEM((2, slots, tile), jnp.float32)],
        ),
        out_shape=[out, out, jax.ShapeDtypeStruct(gate.shape, jnp.bfloat16)],
        compiler_params=pltpu.CompilerParams(vmem_limit_bytes=12 << 20),
        cost_estimate=pl.CostEstimate(
            flops=10 * ff * slots, bytes_accessed=10 * ff * slots, transcendentals=ff * slots
        ),
        name="prep",
    )(ids, *operands)


def hold_kernel(*refs):
    count = (len(refs) - 2) // 2
    copies = [
        pltpu.make_async_copy(refs[i], refs[count + 1 + i], refs[-1].at[i]) for i in range(count)
    ]
    for copy in copies:
        copy.start()
    for copy in copies:
        copy.wait()


def hold(weights, after):
    operands = [pltpu.with_memory_space_constraint(w, pltpu.HBM) for w in weights]
    return pl.pallas_call(
        hold_kernel,
        in_specs=[ANY] * (len(weights) + 1),
        out_specs=[VMEM] * len(weights),
        out_shape=[pltpu.VMEM(w.shape, w.dtype) for w in weights],
        scratch_shapes=[pltpu.SemaphoreType.DMA((len(weights),))],
        compiler_params=pltpu.CompilerParams(vmem_limit_bytes=1 << 20),
        cost_estimate=FREE,
        name="hold",
    )(*operands, after)


def take_kernel(experts, count, me_ref, wdown_ref, *refs):
    rows, arrived_ref, partial_ref, leads = refs[:count], refs[count], refs[count + 1], refs[count + 2 :]
    groups, capacity, dcols = arrived_ref.shape
    me = me_ref[0]
    picked = []
    for i, (ref, to_ref) in enumerate(zip(rows, leads)):
        meta = ref[:, dcols:].astype(jnp.float32)
        tok, lanes = meta.shape
        lane = lax.broadcasted_iota(jnp.int32, (tok, lanes), 1)
        mine = lane % experts == me
        places = jnp.where(mine & (lane < experts), meta, 0.0)
        share = jnp.where(mine & (lane >= experts), meta, 0.0)
        position = jnp.sum(places, axis=1, keepdims=True) - 1.0
        factor = jnp.sum(share, axis=1, keepdims=True)
        slot = lax.broadcasted_iota(jnp.int32, (tok, capacity), 1).astype(jnp.float32)
        select = jnp.where(slot == position, 1.0, 0.0).astype(jnp.bfloat16)
        to_ref[...] = select
        scaled = (factor * ref[:, :dcols].astype(jnp.float32)).astype(jnp.bfloat16)
        picked.append(lax.dot_general(select, scaled, TN, preferred_element_type=jnp.float32))
        arrived_ref[i] = picked[i].astype(jnp.bfloat16)
    partial_ref[...] = lax.dot_general(
        jnp.concatenate(picked, axis=0).astype(jnp.bfloat16),
        wdown_ref[...],
        NT,
        preferred_element_type=jnp.float32,
    ).astype(jnp.bfloat16)


def take_rows(me, wdown, rows, capacity, experts):
    count, tok = len(rows), rows[0].shape[0]
    ff, dcols = wdown.shape
    lead = jax.ShapeDtypeStruct((tok, capacity), jnp.bfloat16)
    return pl.pallas_call(
        functools.partial(take_kernel, experts, count),
        in_specs=[pl.BlockSpec(memory_space=pltpu.SMEM)] + [VMEM] * (1 + count),
        out_shape=[
            jax.ShapeDtypeStruct((count, capacity, dcols), jnp.bfloat16),
            jax.ShapeDtypeStruct((count * capacity, ff), jnp.bfloat16),
        ]
        + [lead] * count,
        compiler_params=pltpu.CompilerParams(vmem_limit_bytes=18 << 20),
        cost_estimate=FREE,
        name="take",
    )(me, wdown, *rows)


def give_kernel(count, mine_ref, theirs_ref, to_gate_ref, to_up_ref, wgate_ref, wup_ref, *refs):
    leads, outs = refs[:count], refs[count:]
    capacity = to_gate_ref.shape[1]
    dh = mine_ref[...].astype(jnp.float32) + theirs_ref[...].astype(jnp.float32)
    dh = dh.astype(jnp.bfloat16).astype(jnp.float32)

    def scaled(ref):
        return (dh * ref[...].astype(jnp.float32).reshape(dh.shape)).astype(jnp.bfloat16)

    slot_grad = lax.dot_general(
        scaled(to_gate_ref), wgate_ref[...], NT, preferred_element_type=jnp.float32
    )
    slot_grad += lax.dot_general(
        scaled(to_up_ref), wup_ref[...], NT, preferred_element_type=jnp.float32
    )
    for i, (lead, out) in enumerate(zip(leads, outs)):
        part = slot_grad[i * capacity : (i + 1) * capacity].astype(jnp.bfloat16)
        out[...] = jnp.dot(lead[...], part, preferred_element_type=jnp.float32).astype(jnp.bfloat16)


def give_rows(first, mine, theirs, to_gate, to_up, wgate, wup, leads):
    count, tok = len(leads), leads[0].shape[0]
    capacity, ff = to_gate.shape[1:]
    factors = pl.BlockSpec((count, capacity, ff), lambda i: (first // count, 0, 0))
    out = jax.ShapeDtypeStruct((tok, wgate.shape[0]), jnp.bfloat16)
    return pl.pallas_call(
        functools.partial(give_kernel, count),
        grid=(1,),
        in_specs=[VMEM, VMEM, factors, factors] + [VMEM] * (2 + count),
        out_specs=[VMEM] * count,
        out_shape=[out] * count,
        compiler_params=pltpu.CompilerParams(vmem_limit_bytes=20 << 20),
        cost_estimate=FREE,
        name="give",
    )(mine, theirs, to_gate, to_up, wgate, wup, *leads)


def add_kernel(*refs):
    total = refs[0][...].astype(jnp.float32)
    for ref in refs[1:-1]:
        total += ref[...].astype(jnp.float32)
    refs[-1][...] = total.astype(refs[-1].dtype)


def add(*parts):
    return pl.pallas_call(
        add_kernel,
        in_specs=[VMEM] * len(parts),
        out_specs=VMEM,
        out_shape=jax.ShapeDtypeStruct(parts[0].shape, parts[0].dtype),
        compiler_params=pltpu.CompilerParams(vmem_limit_bytes=8 << 20),
        cost_estimate=FREE,
        name="add",
    )(*parts)


def sort_kernel(ids_ref, *refs):
    parts, out_ref, done = refs[:-2], refs[-2], refs[-1]
    copies, n = [], 0
    for part in parts:
        for i in range(part.shape[0]):
            copies.append(pltpu.make_async_copy(part.at[i], out_ref.at[ids_ref[n]], done.at[n]))
            n += 1
    for copy in copies:
        copy.start()
    for copy in copies:
        copy.wait()


def sort(ids, parts):
    groups = ids.shape[0]
    return pl.pallas_call(
        sort_kernel,
        in_specs=[pl.BlockSpec(memory_space=pltpu.SMEM)] + [ANY] * len(parts),
        out_specs=ANY,
        out_shape=jax.ShapeDtypeStruct((groups,) + parts[0].shape[1:], jnp.bfloat16),
        scratch_shapes=[pltpu.SemaphoreType.DMA((groups,))],
        compiler_params=pltpu.CompilerParams(vmem_limit_bytes=1 << 20),
        cost_estimate=FREE,
        name="sort",
    )(ids, *parts)


def ring_local(grad_out, routing, gates, scales, saved_gate, saved_up, w_gate, w_up, w_down):
    tok_rows, dcols = grad_out.shape
    groups = lax.axis_size("expert")
    slots = saved_gate.shape[2]
    capacity = slots // groups
    chips = groups // 2
    order = ring_of(chips)
    place = np.argsort(np.array(order))
    after = {order[i]: order[(i + 1) % chips] for i in range(chips)}
    ring = [(2 * j, 2 * after[j]) for j in range(chips)]
    ring += [(2 * after[j] + 1, 2 * j + 1) for j in range(chips)]
    sibling = [(i, i ^ 1) for i in range(groups)]
    swap = [(0, 1), (1, 0)]
    me = lax.axis_index("expert")
    back = [(b, a) for a, b in ring]
    stages = [(s, chips - s) for s in range(1, chips // 2)] + [(chips // 2,)]
    steps = [s for stage in stages for s in stage] + [0]
    table = np.zeros((groups, groups), np.int32)
    for device in range(groups):
        spot = place[device // 2]
        for i, step in enumerate(steps):
            down = 2 * order[(spot - step) % chips]
            up = 2 * order[(spot + step) % chips] + 1
            table[device, 2 * i : 2 * i + 2] = (down, up) if device % 2 == 0 else (up, down)
    ids = lax.dynamic_slice(jnp.asarray(table), (me, 0), (1, groups)).reshape(-1)
    me = me.reshape(1)

    payload = pack(grad_out, routing, gates, scales, groups)
    to_gate, to_up, hidden = prep(ids, saved_gate[0], saved_up[0], capacity)
    (wdown,) = hold([w_down[0]], hidden)

    tie = lax.optimization_barrier
    rows, others = {0: payload}, {}
    arrived, leads, partial, theirs, own, given, totals = {}, {}, {}, {}, {}, {}, {}

    def pass_on(stage):
        for s in stage:
            if s <= chips // 2:
                rows[s] = lax.ppermute(rows[s - 1], "expert", ring)
            else:
                rows[s] = lax.ppermute(rows[(s + 1) % chips], "expert", back)

    def share(stage):
        for s in stage:
            others[s] = lax.ppermute(rows[s], "expert", sibling)

    def take(stage):
        near_far = [a for s in stage for a in (rows[s], others[s])]
        arrived[stage], partial[stage], *leads[stage] = take_rows(
            me, wdown, near_far, capacity, groups
        )

    def trade(stage):
        theirs[stage] = lax.ppermute(partial[stage], "dp", swap)

    def give(stage, then=None):
        first = 2 * steps.index(stage[0])
        parts = give_rows(
            first, partial[stage], theirs[stage], to_gate, to_up, *held, leads[stage]
        )
        if then is not None:
            theirs[then], *parts = tie((theirs[then], *parts))
        for i, s in enumerate(stage):
            own[s] = parts[2 * i]
            given[s] = lax.ppermute(parts[2 * i + 1], "expert", sibling)

    def collect(s, before):
        parts = [own[s], given[s]]
        if before is not None:
            parts.append(lax.ppermute(totals[before], "expert", ring).astype(jnp.float32))
        totals[s] = add(*parts)

    def after(values, keys, guard, key):
        *kept, guard[key] = tie(tuple(values[k] for k in keys) + (guard[key],))
        for k, v in zip(keys, kept):
            values[k] = v

    last = (0,)
    pass_on(stages[0])
    share(last)
    take(last)
    trade(last)
    rows[1], hidden = tie((rows[1], hidden))
    after(rows, stages[0], partial, last)
    held = hold([w_gate[0], w_up[0]], leads[last][0])
    before = last
    for i, stage in enumerate(stages):
        if i + 1 < len(stages):
            pass_on(stages[i + 1])
        share(stage)
        take(stage)
        trade(stage)
        after(theirs, [before], partial, stage)
        give(before, stage if i + 1 == len(stages) else None)
        if i + 1 < len(stages):
            after(rows, stages[i + 1], own, before[0])
        if i > 0:
            collect(before[0], before[0] - 1 if before[0] > 1 else None)
        before = stage
    after(theirs, [before], totals, before[0] - 1)
    give(before)
    for s in list(range(before[0], chips)) + [0]:
        collect(s, (s - 1) % chips)
    parts = [arrived[stage] for stage in stages + [last]]
    every = sort(ids, parts)
    grad_down = jnp.dot(
        hidden, every.reshape(slots, dcols), preferred_element_type=jnp.float32
    ).astype(jnp.bfloat16)
    return (totals[0], grad_down[None])


def solution(mesh):
    paired = mesh.shape["dp"] == 2 and mesh.shape["expert"] % 4 == 0
    return jax.shard_map(
        ring_local if paired else exchange_local,
        mesh=mesh,
        in_specs=(
            P("expert", "dp"),
            P("expert", None),
            P("expert", None),
            P("expert"),
            P("expert", None, None),
            P("expert", None, None),
            P("expert", "dp", None),
            P("expert", "dp", None),
            P("expert", None, "dp"),
        ),
        out_specs=(P("expert", "dp"), P("expert", None, "dp")),
        check_vma=False,
    )
```

profile of v0, /device:TPU:0, one launch (start us, length us, event | category | flops | bytes accessed | tf_op | source)
XLA Modules:
  0.0 140.9 jit_solution(7811453824286266271)
XLA Ops:
  0.6 1.3 pack.1.refs_0_
  2.0 3.1 %collective-permute-start = (bf16[128,2176]{1,0:T(8,128)(2,1)S(1)}, bf16[128,2176]{1,0:T(8,128)(2,1)S(1)}, u32[]{:S(2)}, u32[]{:S(2)}) collective-permute-start(bf16[128,2176]{1,0:T(8,128)(2,1)S(1)} %pack.1.refs_0_), channel_id=1, source_target_pairs={{0,4},{2,0},{4,8},{6,2},{8,12},{10,6},{12,14},{14,10},{5,1},{1,3},... | collective-permute-start | bytes 1671176 | tf_op jit(solution)/shard_map/ppermute | solution.py:375
  5.0 1.1 collective-permute-start.1
  6.1 0.7 dynamic-slice_bitcast_fusion.ids_ref
  6.8 9.9 %prep.1 = (bf16[16,56,1408]{2,1,0:T(8,128)(2,1)S(1)}, bf16[16,56,1408]{2,1,0:T(8,128)(2,1)S(1)}, bf16[1408,896]{1,0:T(8,128)(2,1)S(1)}) custom-call(s32[16]{0:T(128)S(1)} %dynamic-slice_bitcast_fusion.ids_ref, bf16[1408,896]{1,0:T(8,128)(2,1)} %bitcast.20, bf16[1408,896]{1,0:T(8,128)(2,1)} %bitcast.21), custom_call_target="tpu_custom_call" | custom-call | flops 12615680 | bytes 12615680 | tf_op jit(solution)/shard_map/prep/pallas_call | solution.py:165
  16.7 2.6 %hold.2.wdown_ref = bf16[1408,2048]{1,0:T(8,128)(2,1)S(1)} custom-call(bf16[1408,2048]{1,0:T(8,128)(2,1)} %bitcast.17, bf16[1408,896]{1,0:T(8,128)(2,1)S(1)} %get-tuple-element.146.refs_1_), custom_call_target="tpu_custom_call" | custom-call | tf_op jit(solution)/shard_map/hold/pallas_call | solution.py:196
  19.4 2.2 %take.5 = (bf16[2,56,2048]{2,1,0:T(8,128)(2,1)S(1)}, bf16[112,1408]{1,0:T(8,128)(2,1)S(1)}, bf16[128,56]{1,0:T(8,128)(2,1)S(1)}, bf16[128,56]{1,0:T(8,128)(2,1)S(1)}) custom-call(s32[1]{0:T(128)} %bitcast.6.me_ref, bf16[1408,2048]{1,0:T(8,128)(2,1)S(1)} %hold.2.wdown_ref, bf16[128,2176]{1,0:T(8,128)(2,1)S(1)} %pack.1.refs_0_, ...), custom_call_target="tpu_custom_call" | custom-call | tf_op jit(solution)/shard_map/take/pallas_call | solution.py:240
  21.7 0.8 collective-permute-start.6
  22.5 1.6 %collective-permute-start.3 = (bf16[128,2176]{1,0:T(8,128)(2,1)S(1)}, bf16[128,2176]{1,0:T(8,128)(2,1)S(1)}, u32[]{:S(2)}, u32[]{:S(2)}) collective-permute-start(bf16[128,2176]{1,0:T(8,128)(2,1)S(1)} %collective-permute-done.refs_0_), channel_id=1, source_target_pairs={{0,4},{2,0},{4,8},{6,2},{8,12},{10,6},{12,14},{14,10},{5,1},{1,3},... | collective-permute-start | bytes 1671176 | tf_op jit(solution)/shard_map/ppermute | solution.py:375
  24.1 0.4 collective-permute-start.4
  24.6 1.5 %collective-permute-start.5 = (bf16[112,1408]{1,0:T(8,128)(2,1)S(1)}, bf16[112,1408]{1,0:T(8,128)(2,1)S(1)}, u32[]{:S(2)}, u32[]{:S(2)}) collective-permute-start(bf16[112,1408]{1,0:T(8,128)(2,1)S(1)} %get-tuple-element.82.mine_ref), channel_id=1, source_target_pairs={{0,16},{16,0},{1,17},{17,1},{2,18},{18,2},{3,19},{19,3},{4,20},{20... | collective-permute-start | bytes 946184 | tf_op jit(solution)/shard_map/ppermute | solution.py:390
  26.1 4.3 %hold.3 = (bf16[2048,1408]{1,0:T(8,128)(2,1)S(1)}, bf16[2048,1408]{1,0:T(8,128)(2,1)S(1)}) custom-call(bf16[2048,1408]{1,0:T(8,128)(2,1)} %bitcast.18, bf16[2048,1408]{1,0:T(8,128)(2,1)} %bitcast.19, bf16[128,56]{1,0:T(8,128)(2,1)S(1)} %get-tuple-element.87.refs_2_.refs_0_), custom_call_target="tpu_custom_call" | custom-call | tf_op jit(solution)/shard_map/hold/pallas_call | solution.py:196
  30.4 2.4 %take.6 = (bf16[4,56,2048]{2,1,0:T(8,128)(2,1)S(1)}, bf16[224,1408]{1,0:T(8,128)(2,1)S(1)}, bf16[128,56]{1,0:T(8,128)(2,1)S(1)}, bf16[128,56]{1,0:T(8,128)(2,1)S...) custom-call(s32[1]{0:T(128)} %bitcast.6.me_ref, bf16[1408,2048]{1,0:T(8,128)(2,1)S(1)} %hold.2.wdown_ref, ...), custom_call_target="tpu_custom_call" | custom-call | tf_op jit(solution)/shard_map/take/pallas_call | solution.py:240
  32.8 0.6 collective-permute-start.9
  33.4 0.4 collective-permute-done.5.theirs_ref
  33.8 3.9 %give.5 = (bf16[128,2048]{1,0:T(8,128)(2,1)S(1)}, bf16[128,2048]{1,0:T(8,128)(2,1)S(1)}) custom-call(bf16[112,1408]{1,0:T(8,128)(2,1)S(1)} %get-tuple-element.82.mine_ref, bf16[112,1408]{1,0:T(8,128)(2,1)S(1)} %collective-permute-done.5.theirs_ref, bf16[16,56,1408]{2,1,0:T(8,128)(2,1)S(1)} %get-tuple-element.85.to_gate_ref, ...), custom_call_target="tpu_custom_call" | custom-call | tf_op jit(solution)/shard_map/give/pallas_call | solution.py:279
  37.7 0.2 collective-permute-done.3.refs_0_
  37.9 0.2 collective-permute-start.10
  38.2 0.3 collective-permute-start.11
  38.4 1.4 %collective-permute-start.14 = (bf16[128,2176]{1,0:T(8,128)(2,1)S(1)}, bf16[128,2176]{1,0:T(8,128)(2,1)S(1)}, u32[]{:S(2)}, u32[]{:S(2)}) collective-permute-start(bf16[128,2176]{1,0:T(8,128)(2,1)S(1)} %collective-permute-done.3.refs_0_), channel_id=1, source_target_pairs={{0,4},{2,0},{4,8},{6,2},{8,12},{10,6},{12,14},{14,10},{5,1},{1,3},... | collective-permute-start | bytes 1671176 | tf_op jit(solution)/shard_map/ppermute | solution.py:375
  39.9 0.6 collective-permute-start.15
  40.5 0.2 collective-permute-done.11.refs_3_
  40.7 2.4 %take.7 = (bf16[4,56,2048]{2,1,0:T(8,128)(2,1)S(1)}, bf16[224,1408]{1,0:T(8,128)(2,1)S(1)}, bf16[128,56]{1,0:T(8,128)(2,1)S(1)}, bf16[128,56]{1,0:T(8,128)(2,1)S...) custom-call(s32[1]{0:T(128)} %bitcast.6.me_ref, bf16[1408,2048]{1,0:T(8,128)(2,1)S(1)} %hold.2.wdown_ref, ...), custom_call_target="tpu_custom_call" | custom-call | tf_op jit(solution)/shard_map/take/pallas_call | solution.py:240
  43.1 1.6 %collective-permute-start.13 = (bf16[224,1408]{1,0:T(8,128)(2,1)S(1)}, bf16[224,1408]{1,0:T(8,128)(2,1)S(1)}, u32[]{:S(2)}, u32[]{:S(2)}) collective-permute-start(bf16[224,1408]{1,0:T(8,128)(2,1)S(1)} %get-tuple-element.105.mine_ref), channel_id=1, source_target_pairs={{0,16},{16,0},{1,17},{17,1},{2,18},{18,2},{3,19},{19,3},{4,20},{20... | collective-permute-start | bytes 1892360 | tf_op jit(solution)/shard_map/ppermute | solution.py:390
  44.6 5.4 %collective-permute-done.9.theirs_ref = bf16[224,1408]{1,0:T(8,128)(2,1)S(1)} collective-permute-done((bf16[224,1408]{1,0:T(8,128)(2,1)S(1)}, bf16[224,1408]{1,0:T(8,128)(2,1)S(1)}, u32[]{:S(2)}, u32[]{:S(2)}) %collective-permute-start.9) | collective-permute-done | bytes 630816 | tf_op jit(solution)/shard_map/ppermute | solution.py:390
  50.0 4.3 %give.6 = (bf16[128,2048]{1,0:T(8,128)(2,1)S(1)}, bf16[128,2048]{1,0:T(8,128)(2,1)S(1)}, bf16[128,2048]{1,0:T(8,128)(2,1)S(1)}, bf16[128,2048]{1,0:T(8,128)(2,1)S(1)}) custom-call(bf16[224,1408]{1,0:T(8,128)(2,1)S(1)} %get-tuple-element.94.mine_ref, bf16[224,1408]{1,0:T(8,128)(2,1)S(1)} %collective-permute-done.9.theirs_ref, ...), custom_call_target="tpu_custom_call" | custom-call | tf_op jit(solution)/shard_map/give/pallas_call | solution.py:279
  54.4 0.5 collective-permute-start.17
  54.9 1.6 %collective-permute-start.19 = (bf16[128,2176]{1,0:T(8,128)(2,1)S(1)}, bf16[128,2176]{1,0:T(8,128)(2,1)S(1)}, u32[]{:S(2)}, u32[]{:S(2)}) collective-permute-start(bf16[128,2176]{1,0:T(8,128)(2,1)S(1)} %collective-permute-done.14.refs_0_), channel_id=1, source_target_pairs={{0,4},{2,0},{4,8},{6,2},{8,12},{10,6},{12,14},{14,10},{5,1},{1,3},... | collective-permute-start | bytes 1671176 | tf_op jit(solution)/shard_map/ppermute | solution.py:375
  56.5 0.7 collective-permute-done.17.refs_3_
  57.1 2.4 %take.8 = (bf16[4,56,2048]{2,1,0:T(8,128)(2,1)S(1)}, bf16[224,1408]{1,0:T(8,128)(2,1)S(1)}, bf16[128,56]{1,0:T(8,128)(2,1)S(1)}, bf16[128,56]{1,0:T(8,128)(2,1)S...) custom-call(s32[1]{0:T(128)} %bitcast.6.me_ref, bf16[1408,2048]{1,0:T(8,128)(2,1)S(1)} %hold.2.wdown_ref, ...), custom_call_target="tpu_custom_call" | custom-call | tf_op jit(solution)/shard_map/take/pallas_call | solution.py:240
  59.5 2.6 %collective-permute-done.13.theirs_ref = bf16[224,1408]{1,0:T(8,128)(2,1)S(1)} collective-permute-done((bf16[224,1408]{1,0:T(8,128)(2,1)S(1)}, bf16[224,1408]{1,0:T(8,128)(2,1)S(1)}, u32[]{:S(2)}, u32[]{:S(2)}) %collective-permute-start.13) | collective-permute-done | bytes 630816 | tf_op jit(solution)/shard_map/ppermute | solution.py:390
  62.1 4.3 %give.7 = (bf16[128,2048]{1,0:T(8,128)(2,1)S(1)}, bf16[128,2048]{1,0:T(8,128)(2,1)S(1)}, bf16[128,2048]{1,0:T(8,128)(2,1)S(1)}, bf16[128,2048]{1,0:T(8,128)(2,1)S(1)}) custom-call(bf16[224,1408]{1,0:T(8,128)(2,1)S(1)} %get-tuple-element.105.mine_ref, bf16[224,1408]{1,0:T(8,128)(2,1)S(1)} %collective-permute-done.13.theirs_ref, ...), custom_call_target="tpu_custom_call" | custom-call | tf_op jit(solution)/shard_map/give/pallas_call | solution.py:279
  66.5 0.6 collective-permute-start.22
  67.1 0.1 add.12
  67.2 1.9 %collective-permute-start.27 = (bf16[128,2048]{1,0:T(8,128)(2,1)S(1)}, bf16[128,2048]{1,0:T(8,128)(2,1)S(1)}, u32[]{:S(2)}, u32[]{:S(2)}) collective-permute-start(bf16[128,2048]{1,0:T(8,128)(2,1)S(1)} %add.12), channel_id=1, source_target_pairs={{0,4},{2,0},{4,8},{6,2},{8,12},{10,6},{12,14},{14,10},{5,1},{1,3},... | collective-permute-start | bytes 1572872 | tf_op jit(solution)/shard_map/ppermute | solution.py:406
  69.1 2.2 %take.9 = (bf16[2,56,2048]{2,1,0:T(8,128)(2,1)S(1)}, bf16[112,1408]{1,0:T(8,128)(2,1)S(1)}, bf16[128,56]{1,0:T(8,128)(2,1)S(1)}, bf16[128,56]{1,0:T(8,128)(2,1)S(1)}) custom-call(s32[1]{0:T(128)} %bitcast.6.me_ref, bf16[1408,2048]{1,0:T(8,128)(2,1)S(1)} %hold.2.wdown_ref, bf16[128,2176]{1,0:T(8,128)(2,1)S(1)} %collective-permute-done.19.refs_0_, ...), custom_call_target="tpu_custom_call" | custom-call | tf_op jit(solution)/shard_map/take/pallas_call | solution.py:240
  71.3 1.6 %collective-permute-start.21 = (bf16[112,1408]{1,0:T(8,128)(2,1)S(1)}, bf16[112,1408]{1,0:T(8,128)(2,1)S(1)}, u32[]{:S(2)}, u32[]{:S(2)}) collective-permute-start(bf16[112,1408]{1,0:T(8,128)(2,1)S(1)} %get-tuple-element.132.mine_ref), channel_id=1, source_target_pairs={{0,16},{16,0},{1,17},{17,1},{2,18},{18,2},{3,19},{19,3},{4,20},{20... | collective-permute-start | bytes 946184 | tf_op jit(solution)/shard_map/ppermute | solution.py:390
  72.9 3.8 %collective-permute-done.27 = bf16[128,2048]{1,0:T(8,128)(2,1)S(1)} collective-permute-done((bf16[128,2048]{1,0:T(8,128)(2,1)S(1)}, bf16[128,2048]{1,0:T(8,128)(2,1)S(1)}, u32[]{:S(2)}, u32[]{:S(2)}) %collective-permute-start.27) | collective-permute-done | bytes 524320 | tf_op jit(solution)/shard_map/ppermute | solution.py:406
  76.8 0.2 add.13
  77.0 1.6 %collective-permute-start.28 = (bf16[128,2048]{1,0:T(8,128)(2,1)S(1)}, bf16[128,2048]{1,0:T(8,128)(2,1)S(1)}, u32[]{:S(2)}, u32[]{:S(2)}) collective-permute-start(bf16[128,2048]{1,0:T(8,128)(2,1)S(1)} %add.13), channel_id=1, source_target_pairs={{0,4},{2,0},{4,8},{6,2},{8,12},{10,6},{12,14},{14,10},{5,1},{1,3},... | collective-permute-start | bytes 1572872 | tf_op jit(solution)/shard_map/ppermute | solution.py:406
  78.6 4.9 %collective-permute-done.22.theirs_ref = bf16[224,1408]{1,0:T(8,128)(2,1)S(1)} collective-permute-done((bf16[224,1408]{1,0:T(8,128)(2,1)S(1)}, bf16[224,1408]{1,0:T(8,128)(2,1)S(1)}, u32[]{:S(2)}, u32[]{:S(2)}) %collective-permute-start.22) | collective-permute-done | bytes 630816 | tf_op jit(solution)/shard_map/ppermute | solution.py:390
  83.5 4.3 %give.8 = (bf16[128,2048]{1,0:T(8,128)(2,1)S(1)}, bf16[128,2048]{1,0:T(8,128)(2,1)S(1)}, bf16[128,2048]{1,0:T(8,128)(2,1)S(1)}, bf16[128,2048]{1,0:T(8,128)(2,1)S(1)}) custom-call(bf16[224,1408]{1,0:T(8,128)(2,1)S(1)} %get-tuple-element.120.mine_ref, bf16[224,1408]{1,0:T(8,128)(2,1)S(1)} %collective-permute-done.22.theirs_ref, ...), custom_call_target="tpu_custom_call" | custom-call | tf_op jit(solution)/shard_map/give/pallas_call | solution.py:279
  87.8 2.0 %collective-permute-done.21.theirs_ref = bf16[112,1408]{1,0:T(8,128)(2,1)S(1)} collective-permute-done((bf16[112,1408]{1,0:T(8,128)(2,1)S(1)}, bf16[112,1408]{1,0:T(8,128)(2,1)S(1)}, u32[]{:S(2)}, u32[]{:S(2)}) %collective-permute-start.21) | collective-permute-done | bytes 315424 | tf_op jit(solution)/shard_map/ppermute | solution.py:390
  90.0 1.8 %collective-permute-done.24.refs_1_ = bf16[128,2048]{1,0:T(8,128)(2,1)S(1)} collective-permute-done((bf16[128,2048]{1,0:T(8,128)(2,1)S(1)}, bf16[128,2048]{1,0:T(8,128)(2,1)S(1)}, u32[]{:S(2)}, u32[]{:S(2)}) %collective-permute-start.24) | collective-permute-done | bytes 524320 | tf_op jit(solution)/shard_map/ppermute | solution.py:401
  91.8 0.2 add.14
  92.0 1.6 %collective-permute-start.30 = (bf16[128,2048]{1,0:T(8,128)(2,1)S(1)}, bf16[128,2048]{1,0:T(8,128)(2,1)S(1)}, u32[]{:S(2)}, u32[]{:S(2)}) collective-permute-start(bf16[128,2048]{1,0:T(8,128)(2,1)S(1)} %add.14), channel_id=1, source_target_pairs={{0,4},{2,0},{4,8},{6,2},{8,12},{10,6},{12,14},{14,10},{5,1},{1,3},... | collective-permute-start | bytes 1572872 | tf_op jit(solution)/shard_map/ppermute | solution.py:406
  93.6 3.9 %give.9 = (bf16[128,2048]{1,0:T(8,128)(2,1)S(1)}, bf16[128,2048]{1,0:T(8,128)(2,1)S(1)}) custom-call(bf16[112,1408]{1,0:T(8,128)(2,1)S(1)} %get-tuple-element.132.mine_ref, bf16[112,1408]{1,0:T(8,128)(2,1)S(1)} %collective-permute-done.21.theirs_ref, bf16[16,56,1408]{2,1,0:T(8,128)(2,1)S(1)} %get-tuple-element.85.to_gate_ref, ...), custom_call_target="tpu_custom_call" | custom-call | tf_op jit(solution)/shard_map/give/pallas_call | solution.py:279
  97.6 3.6 %collective-permute-done.30 = bf16[128,2048]{1,0:T(8,128)(2,1)S(1)} collective-permute-done((bf16[128,2048]{1,0:T(8,128)(2,1)S(1)}, bf16[128,2048]{1,0:T(8,128)(2,1)S(1)}, u32[]{:S(2)}, u32[]{:S(2)}) %collective-permute-start.30) | collective-permute-done | bytes 524320 | tf_op jit(solution)/shard_map/ppermute | solution.py:406
  101.2 0.1 convert_element_type.26.refs_2_
  101.3 0.2 add.15
  101.5 1.6 %collective-permute-start.31 = (bf16[128,2048]{1,0:T(8,128)(2,1)S(1)}, bf16[128,2048]{1,0:T(8,128)(2,1)S(1)}, u32[]{:S(2)}, u32[]{:S(2)}) collective-permute-start(bf16[128,2048]{1,0:T(8,128)(2,1)S(1)} %add.15), channel_id=1, source_target_pairs={{0,4},{2,0},{4,8},{6,2},{8,12},{10,6},{12,14},{14,10},{5,1},{1,3},... | collective-permute-start | bytes 1572872 | tf_op jit(solution)/shard_map/ppermute | solution.py:406
  103.1 7.6 %collective-permute-done.31 = bf16[128,2048]{1,0:T(8,128)(2,1)S(1)} collective-permute-done((bf16[128,2048]{1,0:T(8,128)(2,1)S(1)}, bf16[128,2048]{1,0:T(8,128)(2,1)S(1)}, u32[]{:S(2)}, u32[]{:S(2)}) %collective-permute-start.31) | collective-permute-done | bytes 524320 | tf_op jit(solution)/shard_map/ppermute | solution.py:406
  110.8 0.2 add.16
  111.0 1.6 %collective-permute-start.32 = (bf16[128,2048]{1,0:T(8,128)(2,1)S(1)}, bf16[128,2048]{1,0:T(8,128)(2,1)S(1)}, u32[]{:S(2)}, u32[]{:S(2)}) collective-permute-start(bf16[128,2048]{1,0:T(8,128)(2,1)S(1)} %add.16), channel_id=1, source_target_pairs={{0,4},{2,0},{4,8},{6,2},{8,12},{10,6},{12,14},{14,10},{5,1},{1,3},... | collective-permute-start | bytes 1572872 | tf_op jit(solution)/shard_map/ppermute | solution.py:406
  112.7 7.6 %collective-permute-done.32 = bf16[128,2048]{1,0:T(8,128)(2,1)S(1)} collective-permute-done((bf16[128,2048]{1,0:T(8,128)(2,1)S(1)}, bf16[128,2048]{1,0:T(8,128)(2,1)S(1)}, u32[]{:S(2)}, u32[]{:S(2)}) %collective-permute-start.32) | collective-permute-done | bytes 524320 | tf_op jit(solution)/shard_map/ppermute | solution.py:406
  120.4 0.2 add.17
  120.5 1.6 %collective-permute-start.33 = (bf16[128,2048]{1,0:T(8,128)(2,1)S(1)}, bf16[128,2048]{1,0:T(8,128)(2,1)S(1)}, u32[]{:S(2)}, u32[]{:S(2)}) collective-permute-start(bf16[128,2048]{1,0:T(8,128)(2,1)S(1)} %add.17), channel_id=1, source_target_pairs={{0,4},{2,0},{4,8},{6,2},{8,12},{10,6},{12,14},{14,10},{5,1},{1,3},... | collective-permute-start | bytes 1572872 | tf_op jit(solution)/shard_map/ppermute | solution.py:406
  122.2 0.5 collective-permute-start.8
  122.7 5.7 %sort.1 = bf16[16,56,2048]{2,1,0:T(8,128)(2,1)S(1)} custom-call(s32[16]{0:T(128)S(1)} %dynamic-slice_bitcast_fusion.ids_ref, bf16[4,56,2048]{2,1,0:T(8,128)(2,1)S(1)} %get-tuple-element.147.refs_0_, bf16[4,56,2048]{2,1,0:T(8,128)(2,1)S(1)} %get-tuple-element.148.refs_1_, bf16[4,56,2048]{2,1,0:T(8,128)(2,1)S(1)} %get-tuple-element.149.refs_2_, ...), custom_call_target="tpu_custom_call" | custom-call | tf_op jit(solution)/shard_map/sort/pallas_call | solution.py:325
  128.4 1.4 collective-permute-done.33
  129.9 0.2 add.18
  130.0 1.9 %collective-permute-start.34 = (bf16[128,2048]{1,0:T(8,128)(2,1)S(1)}, bf16[128,2048]{1,0:T(8,128)(2,1)S(1)}, u32[]{:S(2)}, u32[]{:S(2)}) collective-permute-start(bf16[128,2048]{1,0:T(8,128)(2,1)S(1)} %add.18), channel_id=1, source_target_pairs={{0,4},{2,0},{4,8},{6,2},{8,12},{10,6},{12,14},{14,10},{5,1},{1,3},... | collective-permute-start | bytes 1572872 | tf_op jit(solution)/shard_map/ppermute | solution.py:406
  131.9 7.9 %fusion = bf16[1,1408,2048]{2,1,0:T(8,128)(2,1)} fusion(bf16[1408,896]{1,0:T(8,128)(2,1)S(1)} %get-tuple-element.146.refs_1_, bf16[896,2048]{1,0:T(8,128)(2,1)S(1)} %bitcast.16), kind=kOutput, calls=%fused_computation.1 | convolution fusion | flops 5170266112 | bytes 11960320 | tf_op jit(solution)/shard_map/dot_general | solution.py:442
  139.9 1.0 add.19
  (38 shorter events, 0.9 us)
Async XLA Ops:
  2.0 17.4 %collective-permute-start = (bf16[128,2176]{1,0:T(8,128)(2,1)S(1)}, bf16[128,2176]{1,0:T(8,128)(2,1)S(1)}, u32[]{:S(2)}, u32[]{:S(2)}) collective-permute-start(bf16[128,2176]{1,0:T(8,128)(2,1)S(1)} %pack.1.refs_0_), channel_id=1, source_target_pairs={{0,4},{2,0},{4,8},{6,2},{8,12},{10,6},{12,14},{14,10},{5,1},{1,3},... | collective-permute-start | bytes 1671176 | tf_op jit(solution)/shard_map/ppermute | solution.py:375
  5.0 14.4 %collective-permute-start.2 = (bf16[128,2176]{1,0:T(8,128)(2,1)S(1)}, bf16[128,2176]{1,0:T(8,128)(2,1)S(1)}, u32[]{:S(2)}, u32[]{:S(2)}) collective-permute-start(bf16[128,2176]{1,0:T(8,128)(2,1)S(1)} %pack.1.refs_0_), channel_id=1, source_target_pairs={{0,1},{1,0},{2,3},{3,2},{4,5},{5,4},{6,7},{7,6},{8,9},{9,8},{10,11... | collective-permute-start | bytes 1671176 | tf_op jit(solution)/shard_map/ppermute | solution.py:381
  5.0 16.6 %collective-permute-start.1 = (bf16[128,2176]{1,0:T(8,128)(2,1)S(1)}, bf16[128,2176]{1,0:T(8,128)(2,1)S(1)}, u32[]{:S(2)}, u32[]{:S(2)}) collective-permute-start(bf16[128,2176]{1,0:T(8,128)(2,1)S(1)} %pack.1.refs_0_), channel_id=1, source_target_pairs={{4,0},{0,2},{8,4},{2,6},{12,8},{6,10},{14,12},{10,14},{1,5},{3,1},... | collective-permute-start | bytes 1671176 | tf_op jit(solution)/shard_map/ppermute | solution.py:377
  21.7 8.7 %collective-permute-start.6 = (bf16[128,2176]{1,0:T(8,128)(2,1)S(1)}, bf16[128,2176]{1,0:T(8,128)(2,1)S(1)}, u32[]{:S(2)}, u32[]{:S(2)}) collective-permute-start(bf16[128,2176]{1,0:T(8,128)(2,1)S(1)} %collective-permute-done.refs_0_), channel_id=1, source_target_pairs={{0,1},{1,0},{2,3},{3,2},{4,5},{5,4},{6,7},{7,6},{8,9},{9,8},{10,11... | collective-permute-start | bytes 1671176 | tf_op jit(solution)/shard_map/ppermute | solution.py:381
  22.5 8.0 %collective-permute-start.7 = (bf16[128,2176]{1,0:T(8,128)(2,1)S(1)}, bf16[128,2176]{1,0:T(8,128)(2,1)S(1)}, u32[]{:S(2)}, u32[]{:S(2)}) collective-permute-start(bf16[128,2176]{1,0:T(8,128)(2,1)S(1)} %collective-permute-done.1.refs_2_), channel_id=1, source_target_pairs={{0,1},{1,0},{2,3},{3,2},{4,5},{5,4},{6,7},{7,6},{8,9},{9,8},{10,11... | collective-permute-start | bytes 1671176 | tf_op jit(solution)/shard_map/ppermute | solution.py:381
  22.5 15.4 %collective-permute-start.3 = (bf16[128,2176]{1,0:T(8,128)(2,1)S(1)}, bf16[128,2176]{1,0:T(8,128)(2,1)S(1)}, u32[]{:S(2)}, u32[]{:S(2)}) collective-permute-start(bf16[128,2176]{1,0:T(8,128)(2,1)S(1)} %collective-permute-done.refs_0_), channel_id=1, source_target_pairs={{0,4},{2,0},{4,8},{6,2},{8,12},{10,6},{12,14},{14,10},{5,1},{1,3},... | collective-permute-start | bytes 1671176 | tf_op jit(solution)/shard_map/ppermute | solution.py:375
  24.1 13.8 %collective-permute-start.4 = (bf16[128,2176]{1,0:T(8,128)(2,1)S(1)}, bf16[128,2176]{1,0:T(8,128)(2,1)S(1)}, u32[]{:S(2)}, u32[]{:S(2)}) collective-permute-start(bf16[128,2176]{1,0:T(8,128)(2,1)S(1)} %collective-permute-done.1.refs_2_), channel_id=1, source_target_pairs={{4,0},{0,2},{8,4},{2,6},{12,8},{6,10},{14,12},{10,14},{1,5},{3,1},... | collective-permute-start | bytes 1671176 | tf_op jit(solution)/shard_map/ppermute | solution.py:377
  24.6 9.2 %collective-permute-start.5 = (bf16[112,1408]{1,0:T(8,128)(2,1)S(1)}, bf16[112,1408]{1,0:T(8,128)(2,1)S(1)}, u32[]{:S(2)}, u32[]{:S(2)}) collective-permute-start(bf16[112,1408]{1,0:T(8,128)(2,1)S(1)} %get-tuple-element.82.mine_ref), channel_id=1, source_target_pairs={{0,16},{16,0},{1,17},{17,1},{2,18},{18,2},{3,19},{19,3},{4,20},{20... | collective-permute-start | bytes 946184 | tf_op jit(solution)/shard_map/ppermute | solution.py:390
  32.8 17.2 %collective-permute-start.9 = (bf16[224,1408]{1,0:T(8,128)(2,1)S(1)}, bf16[224,1408]{1,0:T(8,128)(2,1)S(1)}, u32[]{:S(2)}, u32[]{:S(2)}) collective-permute-start(bf16[224,1408]{1,0:T(8,128)(2,1)S(1)} %get-tuple-element.94.mine_ref), channel_id=1, source_target_pairs={{0,16},{16,0},{1,17},{17,1},{2,18},{18,2},{3,19},{19,3},{4,20},{20... | collective-permute-start | bytes 1892360 | tf_op jit(solution)/shard_map/ppermute | solution.py:390
  37.9 2.5 %collective-permute-start.10 = (bf16[128,2176]{1,0:T(8,128)(2,1)S(1)}, bf16[128,2176]{1,0:T(8,128)(2,1)S(1)}, u32[]{:S(2)}, u32[]{:S(2)}) collective-permute-start(bf16[128,2176]{1,0:T(8,128)(2,1)S(1)} %collective-permute-done.3.refs_0_), channel_id=1, source_target_pairs={{0,1},{1,0},{2,3},{3,2},{4,5},{5,4},{6,7},{7,6},{8,9},{9,8},{10,11... | collective-permute-start | bytes 1671176 | tf_op jit(solution)/shard_map/ppermute | solution.py:381
  38.2 2.5 %collective-permute-start.11 = (bf16[128,2176]{1,0:T(8,128)(2,1)S(1)}, bf16[128,2176]{1,0:T(8,128)(2,1)S(1)}, u32[]{:S(2)}, u32[]{:S(2)}) collective-permute-start(bf16[128,2176]{1,0:T(8,128)(2,1)S(1)} %collective-permute-done.4.refs_2_), channel_id=1, source_target_pairs={{0,1},{1,0},{2,3},{3,2},{4,5},{5,4},{6,7},{7,6},{8,9},{9,8},{10,11... | collective-permute-start | bytes 1671176 | tf_op jit(solution)/shard_map/ppermute | solution.py:381
  38.4 15.8 %collective-permute-start.14 = (bf16[128,2176]{1,0:T(8,128)(2,1)S(1)}, bf16[128,2176]{1,0:T(8,128)(2,1)S(1)}, u32[]{:S(2)}, u32[]{:S(2)}) collective-permute-start(bf16[128,2176]{1,0:T(8,128)(2,1)S(1)} %collective-permute-done.3.refs_0_), channel_id=1, source_target_pairs={{0,4},{2,0},{4,8},{6,2},{8,12},{10,6},{12,14},{14,10},{5,1},{1,3},... | collective-permute-start | bytes 1671176 | tf_op jit(solution)/shard_map/ppermute | solution.py:375
  39.9 14.4 %collective-permute-start.15 = (bf16[128,2176]{1,0:T(8,128)(2,1)S(1)}, bf16[128,2176]{1,0:T(8,128)(2,1)S(1)}, u32[]{:S(2)}, u32[]{:S(2)}) collective-permute-start(bf16[128,2176]{1,0:T(8,128)(2,1)S(1)} %collective-permute-done.4.refs_2_), channel_id=1, source_target_pairs={{4,0},{0,2},{8,4},{2,6},{12,8},{6,10},{14,12},{10,14},{1,5},{3,1},... | collective-permute-start | bytes 1671176 | tf_op jit(solution)/shard_map/ppermute | solution.py:377
  43.1 19.0 %collective-permute-start.13 = (bf16[224,1408]{1,0:T(8,128)(2,1)S(1)}, bf16[224,1408]{1,0:T(8,128)(2,1)S(1)}, u32[]{:S(2)}, u32[]{:S(2)}) collective-permute-start(bf16[224,1408]{1,0:T(8,128)(2,1)S(1)} %get-tuple-element.105.mine_ref), channel_id=1, source_target_pairs={{0,16},{16,0},{1,17},{17,1},{2,18},{18,2},{3,19},{19,3},{4,20},{20... | collective-permute-start | bytes 1892360 | tf_op jit(solution)/shard_map/ppermute | solution.py:390
  54.3 2.2 %collective-permute-start.16 = (bf16[128,2176]{1,0:T(8,128)(2,1)S(1)}, bf16[128,2176]{1,0:T(8,128)(2,1)S(1)}, u32[]{:S(2)}, u32[]{:S(2)}) collective-permute-start(bf16[128,2176]{1,0:T(8,128)(2,1)S(1)} %collective-permute-done.14.refs_0_), channel_id=1, source_target_pairs={{0,1},{1,0},{2,3},{3,2},{4,5},{5,4},{6,7},{7,6},{8,9},{9,8},{10,11... | collective-permute-start | bytes 1671176 | tf_op jit(solution)/shard_map/ppermute | solution.py:381
  54.4 2.7 %collective-permute-start.17 = (bf16[128,2176]{1,0:T(8,128)(2,1)S(1)}, bf16[128,2176]{1,0:T(8,128)(2,1)S(1)}, u32[]{:S(2)}, u32[]{:S(2)}) collective-permute-start(bf16[128,2176]{1,0:T(8,128)(2,1)S(1)} %collective-permute-done.15.refs_2_), channel_id=1, source_target_pairs={{0,1},{1,0},{2,3},{3,2},{4,5},{5,4},{6,7},{7,6},{8,9},{9,8},{10,11... | collective-permute-start | bytes 1671176 | tf_op jit(solution)/shard_map/ppermute | solution.py:381
  54.9 11.5 %collective-permute-start.19 = (bf16[128,2176]{1,0:T(8,128)(2,1)S(1)}, bf16[128,2176]{1,0:T(8,128)(2,1)S(1)}, u32[]{:S(2)}, u32[]{:S(2)}) collective-permute-start(bf16[128,2176]{1,0:T(8,128)(2,1)S(1)} %collective-permute-done.14.refs_0_), channel_id=1, source_target_pairs={{0,4},{2,0},{4,8},{6,2},{8,12},{10,6},{12,14},{14,10},{5,1},{1,3},... | collective-permute-start | bytes 1671176 | tf_op jit(solution)/shard_map/ppermute | solution.py:375
  56.5 10.6 %collective-permute-start.26 = (bf16[128,2048]{1,0:T(8,128)(2,1)S(1)}, bf16[128,2048]{1,0:T(8,128)(2,1)S(1)}, u32[]{:S(2)}, u32[]{:S(2)}) collective-permute-start(bf16[128,2048]{1,0:T(8,128)(2,1)S(1)} %get-tuple-element.139), channel_id=1, source_target_pairs={{0,1},{1,0},{2,3},{3,2},{4,5},{5,4},{6,7},{7,6},{8,9},{9,8},{10,11... | collective-permute-start | bytes 1572872 | tf_op jit(solution)/shard_map/ppermute | solution.py:401
  66.4 2.7 %collective-permute-start.20 = (bf16[128,2176]{1,0:T(8,128)(2,1)S(1)}, bf16[128,2176]{1,0:T(8,128)(2,1)S(1)}, u32[]{:S(2)}, u32[]{:S(2)}) collective-permute-start(bf16[128,2176]{1,0:T(8,128)(2,1)S(1)} %collective-permute-done.19.refs_0_), channel_id=1, source_target_pairs={{0,1},{1,0},{2,3},{3,2},{4,5},{5,4},{6,7},{7,6},{8,9},{9,8},{10,11... | collective-permute-start | bytes 1671176 | tf_op jit(solution)/shard_map/ppermute | solution.py:381
  66.5 17.1 %collective-permute-start.22 = (bf16[224,1408]{1,0:T(8,128)(2,1)S(1)}, bf16[224,1408]{1,0:T(8,128)(2,1)S(1)}, u32[]{:S(2)}, u32[]{:S(2)}) collective-permute-start(bf16[224,1408]{1,0:T(8,128)(2,1)S(1)} %get-tuple-element.120.mine_ref), channel_id=1, source_target_pairs={{0,16},{16,0},{1,17},{17,1},{2,18},{18,2},{3,19},{19,3},{4,20},{20... | collective-permute-start | bytes 1892360 | tf_op jit(solution)/shard_map/ppermute | solution.py:390
  67.2 9.5 %collective-permute-start.27 = (bf16[128,2048]{1,0:T(8,128)(2,1)S(1)}, bf16[128,2048]{1,0:T(8,128)(2,1)S(1)}, u32[]{:S(2)}, u32[]{:S(2)}) collective-permute-start(bf16[128,2048]{1,0:T(8,128)(2,1)S(1)} %add.12), channel_id=1, source_target_pairs={{0,4},{2,0},{4,8},{6,2},{8,12},{10,6},{12,14},{14,10},{5,1},{1,3},... | collective-permute-start | bytes 1572872 | tf_op jit(solution)/shard_map/ppermute | solution.py:406
  69.1 7.7 %collective-permute-start.25 = (bf16[128,2048]{1,0:T(8,128)(2,1)S(1)}, bf16[128,2048]{1,0:T(8,128)(2,1)S(1)}, u32[]{:S(2)}, u32[]{:S(2)}) collective-permute-start(bf16[128,2048]{1,0:T(8,128)(2,1)S(1)} %get-tuple-element.137), channel_id=1, source_target_pairs={{0,1},{1,0},{2,3},{3,2},{4,5},{5,4},{6,7},{7,6},{8,9},{9,8},{10,11... | collective-permute-start | bytes 1572872 | tf_op jit(solution)/shard_map/ppermute | solution.py:401
  71.3 18.5 %collective-permute-start.21 = (bf16[112,1408]{1,0:T(8,128)(2,1)S(1)}, bf16[112,1408]{1,0:T(8,128)(2,1)S(1)}, u32[]{:S(2)}, u32[]{:S(2)}) collective-permute-start(bf16[112,1408]{1,0:T(8,128)(2,1)S(1)} %get-tuple-element.132.mine_ref), channel_id=1, source_target_pairs={{0,16},{16,0},{1,17},{17,1},{2,18},{18,2},{3,19},{19,3},{4,20},{20... | collective-permute-start | bytes 946184 | tf_op jit(solution)/shard_map/ppermute | solution.py:390
  77.0 12.9 %collective-permute-start.28 = (bf16[128,2048]{1,0:T(8,128)(2,1)S(1)}, bf16[128,2048]{1,0:T(8,128)(2,1)S(1)}, u32[]{:S(2)}, u32[]{:S(2)}) collective-permute-start(bf16[128,2048]{1,0:T(8,128)(2,1)S(1)} %add.13), channel_id=1, source_target_pairs={{0,4},{2,0},{4,8},{6,2},{8,12},{10,6},{12,14},{14,10},{5,1},{1,3},... | collective-permute-start | bytes 1572872 | tf_op jit(solution)/shard_map/ppermute | solution.py:406
  89.8 1.9 %collective-permute-start.24 = (bf16[128,2048]{1,0:T(8,128)(2,1)S(1)}, bf16[128,2048]{1,0:T(8,128)(2,1)S(1)}, u32[]{:S(2)}, u32[]{:S(2)}) collective-permute-start(bf16[128,2048]{1,0:T(8,128)(2,1)S(1)} %get-tuple-element.135), channel_id=1, source_target_pairs={{0,1},{1,0},{2,3},{3,2},{4,5},{5,4},{6,7},{7,6},{8,9},{9,8},{10,11... | collective-permute-start | bytes 1572872 | tf_op jit(solution)/shard_map/ppermute | solution.py:401
  92.0 9.2 %collective-permute-start.30 = (bf16[128,2048]{1,0:T(8,128)(2,1)S(1)}, bf16[128,2048]{1,0:T(8,128)(2,1)S(1)}, u32[]{:S(2)}, u32[]{:S(2)}) collective-permute-start(bf16[128,2048]{1,0:T(8,128)(2,1)S(1)} %add.14), channel_id=1, source_target_pairs={{0,4},{2,0},{4,8},{6,2},{8,12},{10,6},{12,14},{14,10},{5,1},{1,3},... | collective-permute-start | bytes 1572872 | tf_op jit(solution)/shard_map/ppermute | solution.py:406
  97.5 3.8 %collective-permute-start.29 = (bf16[128,2048]{1,0:T(8,128)(2,1)S(1)}, bf16[128,2048]{1,0:T(8,128)(2,1)S(1)}, u32[]{:S(2)}, u32[]{:S(2)}) collective-permute-start(bf16[128,2048]{1,0:T(8,128)(2,1)S(1)} %get-tuple-element.144), channel_id=1, source_target_pairs={{0,1},{1,0},{2,3},{3,2},{4,5},{5,4},{6,7},{7,6},{8,9},{9,8},{10,11... | collective-permute-start | bytes 1572872 | tf_op jit(solution)/shard_map/ppermute | solution.py:401
  101.5 9.2 %collective-permute-start.31 = (bf16[128,2048]{1,0:T(8,128)(2,1)S(1)}, bf16[128,2048]{1,0:T(8,128)(2,1)S(1)}, u32[]{:S(2)}, u32[]{:S(2)}) collective-permute-start(bf16[128,2048]{1,0:T(8,128)(2,1)S(1)} %add.15), channel_id=1, source_target_pairs={{0,4},{2,0},{4,8},{6,2},{8,12},{10,6},{12,14},{14,10},{5,1},{1,3},... | collective-permute-start | bytes 1572872 | tf_op jit(solution)/shard_map/ppermute | solution.py:406
  103.1 7.7 %collective-permute-start.23 = (bf16[128,2048]{1,0:T(8,128)(2,1)S(1)}, bf16[128,2048]{1,0:T(8,128)(2,1)S(1)}, u32[]{:S(2)}, u32[]{:S(2)}) collective-permute-start(bf16[128,2048]{1,0:T(8,128)(2,1)S(1)} %get-tuple-element.131), channel_id=1, source_target_pairs={{0,1},{1,0},{2,3},{3,2},{4,5},{5,4},{6,7},{7,6},{8,9},{9,8},{10,11... | collective-permute-start | bytes 1572872 | tf_op jit(solution)/shard_map/ppermute | solution.py:401
  111.0 9.2 %collective-permute-start.32 = (bf16[128,2048]{1,0:T(8,128)(2,1)S(1)}, bf16[128,2048]{1,0:T(8,128)(2,1)S(1)}, u32[]{:S(2)}, u32[]{:S(2)}) collective-permute-start(bf16[128,2048]{1,0:T(8,128)(2,1)S(1)} %add.16), channel_id=1, source_target_pairs={{0,4},{2,0},{4,8},{6,2},{8,12},{10,6},{12,14},{14,10},{5,1},{1,3},... | collective-permute-start | bytes 1572872 | tf_op jit(solution)/shard_map/ppermute | solution.py:406
  112.6 7.7 %collective-permute-start.18 = (bf16[128,2048]{1,0:T(8,128)(2,1)S(1)}, bf16[128,2048]{1,0:T(8,128)(2,1)S(1)}, u32[]{:S(2)}, u32[]{:S(2)}) collective-permute-start(bf16[128,2048]{1,0:T(8,128)(2,1)S(1)} %get-tuple-element.116), channel_id=1, source_target_pairs={{0,1},{1,0},{2,3},{3,2},{4,5},{5,4},{6,7},{7,6},{8,9},{9,8},{10,11... | collective-permute-start | bytes 1572872 | tf_op jit(solution)/shard_map/ppermute | solution.py:401
  120.5 9.2 %collective-permute-start.33 = (bf16[128,2048]{1,0:T(8,128)(2,1)S(1)}, bf16[128,2048]{1,0:T(8,128)(2,1)S(1)}, u32[]{:S(2)}, u32[]{:S(2)}) collective-permute-start(bf16[128,2048]{1,0:T(8,128)(2,1)S(1)} %add.17), channel_id=1, source_target_pairs={{0,4},{2,0},{4,8},{6,2},{8,12},{10,6},{12,14},{14,10},{5,1},{1,3},... | collective-permute-start | bytes 1572872 | tf_op jit(solution)/shard_map/ppermute | solution.py:406
  122.2 7.7 %collective-permute-start.12 = (bf16[128,2048]{1,0:T(8,128)(2,1)S(1)}, bf16[128,2048]{1,0:T(8,128)(2,1)S(1)}, u32[]{:S(2)}, u32[]{:S(2)}) collective-permute-start(bf16[128,2048]{1,0:T(8,128)(2,1)S(1)} %get-tuple-element.104), channel_id=1, source_target_pairs={{0,1},{1,0},{2,3},{3,2},{4,5},{5,4},{6,7},{7,6},{8,9},{9,8},{10,11... | collective-permute-start | bytes 1572872 | tf_op jit(solution)/shard_map/ppermute | solution.py:401
  122.2 17.8 %collective-permute-start.8 = (bf16[128,2048]{1,0:T(8,128)(2,1)S(1)}, bf16[128,2048]{1,0:T(8,128)(2,1)S(1)}, u32[]{:S(2)}, u32[]{:S(2)}) collective-permute-start(bf16[128,2048]{1,0:T(8,128)(2,1)S(1)} %get-tuple-element.93), channel_id=1, source_target_pairs={{0,1},{1,0},{2,3},{3,2},{4,5},{5,4},{6,7},{7,6},{8,9},{9,8},{10,11... | collective-permute-start | bytes 1572872 | tf_op jit(solution)/shard_map/ppermute | solution.py:401
  130.0 9.8 %collective-permute-start.34 = (bf16[128,2048]{1,0:T(8,128)(2,1)S(1)}, bf16[128,2048]{1,0:T(8,128)(2,1)S(1)}, u32[]{:S(2)}, u32[]{:S(2)}) collective-permute-start(bf16[128,2048]{1,0:T(8,128)(2,1)S(1)} %add.18), channel_id=1, source_target_pairs={{0,4},{2,0},{4,8},{6,2},{8,12},{10,6},{12,14},{14,10},{5,1},{1,3},... | collective-permute-start | bytes 1572872 | tf_op jit(solution)/shard_map/ppermute | solution.py:406
where the time goes:
time: 141 us
  Pallas kernels  58.4 us (41%)
  waiting for transfers between devices  42.2 us (30%)
  starting transfers between devices  30.1 us (21%)
  matrix products  7.91 us (6%)
    ppermute x7, waiting for transfers between devices, collect(): lax.ppermute(totals[before], 'expert', ring).astype(jnp.float32)  24 us
    pallas_call x5, Pallas kernels, give_rows(): pl.pallas_call(functools.partial(give_kernel, count), grid=(1,), in_specs...  20.6 us
    ppermute x5, waiting for transfers between devices, trade(): theirs[stage] = lax.ppermute(partial[stage], 'dp', swap)  15.3 us
    ppermute x7, starting transfers between devices, collect(): lax.ppermute(totals[before], 'expert', ring).astype(jnp.float32)  11.9 us
    pallas_call x5, Pallas kernels, take_rows(): pl.pallas_call(functools.partial(take_kernel, experts, count), in_specs=[...  11.6 us
    pallas_call x1, Pallas kernels, prep(): pl.pallas_call(functools.partial(prep_kernel, capacity), grid_spec=pltpu....  9.93 us
    dot_general x1, matrix products, ring_local(): jnp.dot(hidden, every.reshape(slots, dcols), preferred_element_type=jnp.f...  7.91 us
    ppermute x4, starting transfers between devices, pass_on(): rows[s] = lax.ppermute(rows[s - 1], 'expert', ring)  7.67 us
  transfers between devices with their start and end apart: 35, of which 14 were waited for; matrix products, arithmetic and copies ran while one was open for 7% of the time, Pallas kernels for 39%

commit v1 on v0

--- a/solution.py
+++ b/solution.py
@@ -10,10 +10,13 @@
 
 LANES = 128
 PIECES = 4
+HALVES = 4
+SPLIT = 6
 NT = (((1,), (1,)), ((), ()))
 TN = (((0,), (0,)), ((), ()))
 VMEM = pl.BlockSpec(memory_space=pltpu.VMEM)
 ANY = pl.BlockSpec(memory_space=pl.ANY)
+TOKEN = jax.ShapeDtypeStruct((8, LANES), jnp.float32)
 FREE = pl.CostEstimate(flops=0, bytes_accessed=0, transcendentals=0)
 
 
@@ -140,77 +143,85 @@
     )(*operands)
 
 
-def prep_kernel(capacity, ids_ref, gate_ref, up_ref, to_gate_ref, to_up_ref, hidden_ref, turned):
+def prep_kernel(capacity, first, ids_ref, gate_ref, up_ref, *refs):
+    to_gate_ref, to_up_ref, hidden_ref, token_ref, turned = refs[-5:]
     g = gate_ref[...].astype(jnp.float32)
     u = up_ref[...].astype(jnp.float32)
     sig = jax.nn.sigmoid(g)
     swish = g * sig
-    hidden_ref[...] = (swish * u).astype(jnp.bfloat16)
     turned[0] = (u * sig * (1.0 + g * (1.0 - sig))).T
     turned[1] = swish.T
-    for i in range(to_gate_ref.shape[0]):
-        start = pl.multiple_of(ids_ref[i] * capacity, 8)
-        for k, ref in enumerate((to_gate_ref, to_up_ref)):
-            ref[i] = turned[k, pl.ds(start, capacity)].astype(jnp.bfloat16)
-
-
-def prep(ids, gate, up, capacity):
+    turned[2] = (swish * u).T
+
+    def in_order(k):
+        groups = gate_ref.shape[1] // capacity
+        starts = [pl.multiple_of(ids_ref[i] * capacity, 8) for i in range(groups)]
+        return jnp.concatenate([turned[k, pl.ds(start, capacity)] for start in starts], axis=0)
+
+    span = pl.ds(pl.multiple_of((first + pl.program_id(0)) * LANES, LANES), LANES)
+    to_gate_ref[:, span] = in_order(0).astype(jnp.bfloat16)
+    to_up_ref[:, span] = in_order(1).astype(jnp.bfloat16)
+    hidden_ref[span] = in_order(2).T.astype(jnp.bfloat16)
+    token_ref[...] = jnp.zeros(token_ref.shape, token_ref.dtype)
+
+
+def prep(ids, gate, up, capacity, tiles, old=()):
     ff, slots = gate.shape
-    groups = slots // capacity
-    tile = LANES
-    out = jax.ShapeDtypeStruct((groups, capacity, ff), jnp.bfloat16)
-    spec = pl.BlockSpec((tile, slots), lambda i, ids: (i, 0))
-    out_spec = pl.BlockSpec((groups, capacity, tile), lambda i, ids: (0, 0, i))
+    spec = pl.BlockSpec((LANES, slots), lambda i, ids: (tiles[0] + i, 0))
     operands = [pltpu.with_memory_space_constraint(a, pltpu.HBM) for a in (gate, up)]
-    return pl.pallas_call(
-        functools.partial(prep_kernel, capacity),
+    count = (tiles[1] - tiles[0]) * LANES
+    return pl.pallas_call(
+        functools.partial(prep_kernel, capacity, tiles[0]),
         grid_spec=pltpu.PrefetchScalarGridSpec(
             num_scalar_prefetch=1,
-            grid=(ff // tile,),
-            in_specs=[spec, spec],
-            out_specs=[out_spec, out_spec, spec],
-            scratch_shapes=[pltpu.VMEM((2, slots, tile), jnp.float32)],
+            grid=(tiles[1] - tiles[0],),
+            in_specs=[spec, spec] + [VMEM] * len(old),
+            out_specs=[VMEM] * 3 + [pl.BlockSpec(TOKEN.shape, lambda i, ids: (0, 0))],
+            scratch_shapes=[pltpu.VMEM((3, slots, LANES), jnp.float32)],
         ),
-        out_shape=[out, out, jax.ShapeDtypeStruct(gate.shape, jnp.bfloat16)],
-        compiler_params=pltpu.CompilerParams(vmem_limit_bytes=12 << 20),
+        out_shape=[
+            pltpu.VMEM((slots, ff), jnp.bfloat16),
+            pltpu.VMEM((slots, ff), jnp.bfloat16),
+            pltpu.VMEM((ff, slots), jnp.bfloat16),
+            TOKEN,
+        ],
+        input_output_aliases={3 + i: i for i in range(len(old))},
+        compiler_params=pltpu.CompilerParams(vmem_limit_bytes=8 << 20),
         cost_estimate=pl.CostEstimate(
-            flops=10 * ff * slots, bytes_accessed=10 * ff * slots, transcendentals=ff * slots
+            flops=10 * count * slots, bytes_accessed=10 * count * slots, transcendentals=count * slots
         ),
         name="prep",
-    )(ids, *operands)
-
-
-def hold_kernel(*refs):
-    count = (len(refs) - 2) // 2
-    copies = [
-        pltpu.make_async_copy(refs[i], refs[count + 1 + i], refs[-1].at[i]) for i in range(count)
-    ]
-    for copy in copies:
-        copy.start()
-    for copy in copies:
-        copy.wait()
-
-
-def hold(weights, after):
-    operands = [pltpu.with_memory_space_constraint(w, pltpu.HBM) for w in weights]
+    )(ids, *operands, *old)
+
+
+def hold_kernel(weights_ref, *refs):
+    out_ref, token_ref, done = refs[-3:]
+    copy = pltpu.make_async_copy(weights_ref, out_ref, done)
+    copy.start()
+    token_ref[...] = jnp.zeros(token_ref.shape, token_ref.dtype)
+    copy.wait()
+
+
+def hold(weights, *after):
     return pl.pallas_call(
         hold_kernel,
-        in_specs=[ANY] * (len(weights) + 1),
-        out_specs=[VMEM] * len(weights),
-        out_shape=[pltpu.VMEM(w.shape, w.dtype) for w in weights],
-        scratch_shapes=[pltpu.SemaphoreType.DMA((len(weights),))],
+        in_specs=[ANY] * (1 + len(after)),
+        out_specs=[VMEM, VMEM],
+        out_shape=[pltpu.VMEM(weights.shape, weights.dtype), TOKEN],
+        scratch_shapes=[pltpu.SemaphoreType.DMA(())],
         compiler_params=pltpu.CompilerParams(vmem_limit_bytes=1 << 20),
         cost_estimate=FREE,
         name="hold",
-    )(*operands, after)
-
-
-def take_kernel(experts, count, me_ref, wdown_ref, *refs):
-    rows, arrived_ref, partial_ref, leads = refs[:count], refs[count], refs[count + 1], refs[count + 2 :]
-    groups, capacity, dcols = arrived_ref.shape
+    )(pltpu.with_memory_space_constraint(weights, pltpu.HBM), *after)
+
+
+def take_kernel(experts, count, first, me_ref, wdown_ref, *refs):
+    rows, (every_ref, partial_ref, *leads) = refs[:count], refs[-2 - count :]
+    dcols = every_ref.shape[1]
+    capacity = every_ref.shape[0] // experts
     me = me_ref[0]
     picked = []
-    for i, (ref, to_ref) in enumerate(zip(rows, leads)):
+    for ref, to_ref in zip(rows, leads):
         meta = ref[:, dcols:].astype(jnp.float32)
         tok, lanes = meta.shape
         lane = lax.broadcasted_iota(jnp.int32, (tok, lanes), 1)
@@ -224,41 +235,45 @@
         to_ref[...] = select
         scaled = (factor * ref[:, :dcols].astype(jnp.float32)).astype(jnp.bfloat16)
         picked.append(lax.dot_general(select, scaled, TN, preferred_element_type=jnp.float32))
-        arrived_ref[i] = picked[i].astype(jnp.bfloat16)
+    slots = jnp.concatenate(picked, axis=0).astype(jnp.bfloat16)
+    every_ref[first * capacity : (first + count) * capacity] = slots
     partial_ref[...] = lax.dot_general(
-        jnp.concatenate(picked, axis=0).astype(jnp.bfloat16),
-        wdown_ref[...],
-        NT,
-        preferred_element_type=jnp.float32,
+        slots, wdown_ref[...], NT, preferred_element_type=jnp.float32
     ).astype(jnp.bfloat16)
 
 
-def take_rows(me, wdown, rows, capacity, experts):
+def take_rows(first, me, wdown, rows, every, total, experts):
     count, tok = len(rows), rows[0].shape[0]
     ff, dcols = wdown.shape
+    capacity = total // experts
+    smem = pl.BlockSpec(memory_space=pltpu.SMEM)
+    old = [] if every is None else [every]
     lead = jax.ShapeDtypeStruct((tok, capacity), jnp.bfloat16)
     return pl.pallas_call(
-        functools.partial(take_kernel, experts, count),
-        in_specs=[pl.BlockSpec(memory_space=pltpu.SMEM)] + [VMEM] * (1 + count),
+        functools.partial(take_kernel, experts, count, first),
+        in_specs=[smem] + [VMEM] * (1 + count + len(old)),
+        out_specs=[VMEM] * (2 + count),
         out_shape=[
-            jax.ShapeDtypeStruct((count, capacity, dcols), jnp.bfloat16),
+            pltpu.VMEM((total, dcols), jnp.bfloat16),
             jax.ShapeDtypeStruct((count * capacity, ff), jnp.bfloat16),
         ]
         + [lead] * count,
-        compiler_params=pltpu.CompilerParams(vmem_limit_bytes=18 << 20),
+        input_output_aliases={2 + count: 0} if old else {},
+        compiler_params=pltpu.CompilerParams(vmem_limit_bytes=14 << 20),
         cost_estimate=FREE,
         name="take",
-    )(me, wdown, *rows)
-
-
-def give_kernel(count, mine_ref, theirs_ref, to_gate_ref, to_up_ref, wgate_ref, wup_ref, *refs):
+    )(me, wdown, *rows, *old)
+
+
+def give_kernel(count, first, mine_ref, theirs_ref, to_gate_ref, to_up_ref, wgate_ref, wup_ref, *refs):
     leads, outs = refs[:count], refs[count:]
-    capacity = to_gate_ref.shape[1]
+    capacity = mine_ref.shape[0] // count
+    span = slice(first * capacity, (first + count) * capacity)
     dh = mine_ref[...].astype(jnp.float32) + theirs_ref[...].astype(jnp.float32)
     dh = dh.astype(jnp.bfloat16).astype(jnp.float32)
 
     def scaled(ref):
-        return (dh * ref[...].astype(jnp.float32).reshape(dh.shape)).astype(jnp.bfloat16)
+        return (dh * ref[span].astype(jnp.float32)).astype(jnp.bfloat16)
 
     slot_grad = lax.dot_general(
         scaled(to_gate_ref), wgate_ref[...], NT, preferred_element_type=jnp.float32
@@ -273,38 +288,93 @@
 
 def give_rows(first, mine, theirs, to_gate, to_up, wgate, wup, leads):
     count, tok = len(leads), leads[0].shape[0]
-    capacity, ff = to_gate.shape[1:]
-    factors = pl.BlockSpec((count, capacity, ff), lambda i: (first // count, 0, 0))
     out = jax.ShapeDtypeStruct((tok, wgate.shape[0]), jnp.bfloat16)
     return pl.pallas_call(
-        functools.partial(give_kernel, count),
-        grid=(1,),
-        in_specs=[VMEM, VMEM, factors, factors] + [VMEM] * (2 + count),
+        functools.partial(give_kernel, count, first),
+        in_specs=[VMEM] * (6 + count),
         out_specs=[VMEM] * count,
         out_shape=[out] * count,
-        compiler_params=pltpu.CompilerParams(vmem_limit_bytes=20 << 20),
+        compiler_params=pltpu.CompilerParams(vmem_limit_bytes=16 << 20),
         cost_estimate=FREE,
         name="give",
     )(mine, theirs, to_gate, to_up, wgate, wup, *leads)
 
 
-def add_kernel(*refs):
-    total = refs[0][...].astype(jnp.float32)
-    for ref in refs[1:-1]:
-        total += ref[...].astype(jnp.float32)
-    refs[-1][...] = total.astype(refs[-1].dtype)
-
-
-def add(*parts):
-    return pl.pallas_call(
-        add_kernel,
+def add_kernel(span, own_ref, given_ref, *refs):
+    out_ref = refs[-1]
+    total = own_ref[:, span].astype(jnp.float32) + given_ref[:, span].astype(jnp.float32)
+    if len(refs) > 1:
+        received = jnp.concatenate([ref[...] for ref in refs[:-1]], axis=1)
+        if received.shape != total.shape:
+            received = received[:, span]
+        total += received.astype(jnp.float32)
+    out_ref[...] = total.astype(out_ref.dtype)
+
+
+def add(span, own, given, received):
+    parts = (own, given, *received)
+    return pl.pallas_call(
+        functools.partial(add_kernel, span),
         in_specs=[VMEM] * len(parts),
         out_specs=VMEM,
-        out_shape=jax.ShapeDtypeStruct(parts[0].shape, parts[0].dtype),
+        out_shape=jax.ShapeDtypeStruct((own.shape[0], span.stop - span.start), own.dtype),
         compiler_params=pltpu.CompilerParams(vmem_limit_bytes=8 << 20),
         cost_estimate=FREE,
         name="add",
     )(*parts)
+
+
+def grad_kernel(hidden_ref, every_ref, after_ref, *refs):
+    refs[-1][...] = jnp.dot(
+        hidden_ref[...], every_ref[...], preferred_element_type=jnp.float32
+    ).astype(jnp.bfloat16)
+
+
+def grad_rows(hidden, every, after, part, old):
+    (ff, slots), dcols = hidden.shape, every.shape[1]
+    rows = ff // 4
+    return pl.pallas_call(
+        grad_kernel,
+        grid=(2,),
+        in_specs=[pl.BlockSpec((rows, slots), lambda i: (2 * part + i, 0)), VMEM]
+        + [ANY] * (1 + len(old)),
+        out_specs=pl.BlockSpec((rows, dcols), lambda i: (2 * part + i, 0)),
+        out_shape=jax.ShapeDtypeStruct((ff, dcols), jnp.bfloat16),
+        input_output_aliases={3: 0} if old else {},
+        compiler_params=pltpu.CompilerParams(vmem_limit_bytes=14 << 20),
+        cost_estimate=FREE,
+        name="grad_down",
+    )(hidden, every, after, *old)
+
+
+def mark(array, us):
+    return pl.pallas_call(
+        lambda old_ref, new_ref: None,
+        in_specs=[ANY],
+        out_specs=ANY,
+        out_shape=jax.ShapeDtypeStruct(array.shape, array.dtype),
+        input_output_aliases={0: 0},
+        compiler_params=pltpu.CompilerParams(vmem_limit_bytes=1 << 20),
+        cost_estimate=pl.CostEstimate(
+            flops=int(us * 1.1e9), bytes_accessed=int(us * 3.6e6), transcendentals=0
+        ),
+        name="mark",
+    )(array)
+
+
+def mark(array, us):
+    return pl.pallas_call(
+        lambda old_ref, new_ref: None,
+        in_specs=[ANY],
+        out_specs=ANY,
+        out_shape=jax.ShapeDtypeStruct(array.shape, array.dtype),
+        input_output_aliases={0: 0},
+        compiler_params=pltpu.CompilerParams(vmem_limit_bytes=1 << 20),
+        cost_estimate=pl.CostEstimate(
+            flops=int(us * 1.1e9), bytes_accessed=int(us * 3.6e6), transcendentals=0
+        ),
+        name="mark",
+    )(array)
 
 
 def sort_kernel(ids_ref, *refs):
@@ -362,12 +432,13 @@
     me = me.reshape(1)
 
     payload = pack(grad_out, routing, gates, scales, groups)
-    to_gate, to_up, hidden = prep(ids, saved_gate[0], saved_up[0], capacity)
-    (wdown,) = hold([w_down[0]], hidden)
+    tiles = -(-saved_gate.shape[1] // LANES)
+    *factors, token = prep(ids, saved_gate[0], saved_up[0], capacity, (0, SPLIT))
+    wdown, _ = hold(w_down[0], token)
 
     tie = lax.optimization_barrier
     rows, others = {0: payload}, {}
-    arrived, leads, partial, theirs, own, given, totals = {}, {}, {}, {}, {}, {}, {}
+    leads, partial, theirs, own, given, totals = {}, {}, {}, {}, {}, {}
 
     def pass_on(stage):
         for s in stage:
@@ -380,31 +451,35 @@
         for s in stage:
             others[s] = lax.ppermute(rows[s], "expert", sibling)
 
-    def take(stage):
+    def take(stage, every=None):
         near_far = [a for s in stage for a in (rows[s], others[s])]
-        arrived[stage], partial[stage], *leads[stage] = take_rows(
-            me, wdown, near_far, capacity, groups
+        every, partial[stage], *leads[stage] = take_rows(
+            2 * steps.index(stage[0]), me, wdown, near_far, every, slots, groups
         )
+        return every
 
     def trade(stage):
-        theirs[stage] = lax.ppermute(partial[stage], "dp", swap)
-
-    def give(stage, then=None):
+        theirs[stage] = mark(lax.ppermute(partial[stage], "dp", swap), 10.0)
+
+    def give(stage):
         first = 2 * steps.index(stage[0])
         parts = give_rows(
             first, partial[stage], theirs[stage], to_gate, to_up, *held, leads[stage]
         )
-        if then is not None:
-            theirs[then], *parts = tie((theirs[then], *parts))
         for i, s in enumerate(stage):
             own[s] = parts[2 * i]
             given[s] = lax.ppermute(parts[2 * i + 1], "expert", sibling)
 
     def collect(s, before):
-        parts = [own[s], given[s]]
-        if before is not None:
-            parts.append(lax.ppermute(totals[before], "expert", ring).astype(jnp.float32))
-        totals[s] = add(*parts)
+        received = [] if before is None else totals[before]
+        received = [mark(lax.ppermute(part, "expert", ring), 8.0) for part in received]
+        pieces = 2 if s >= HALVES else 1
+        width = dcols // pieces
+        totals[s] = []
+        for p in range(pieces):
+            mine = received[p : p + 1] if len(received) == pieces else received
+            span = slice(p * width, (p + 1) * width)
+            totals[s].append(add(span, own[s], given[s], mine))
 
     def after(values, keys, guard, key):
         *kept, guard[key] = tie(tuple(values[k] for k in keys) + (guard[key],))
@@ -414,35 +489,50 @@
     last = (0,)
     pass_on(stages[0])
     share(last)
-    take(last)
+    every = take(last)
     trade(last)
-    rows[1], hidden = tie((rows[1], hidden))
     after(rows, stages[0], partial, last)
-    held = hold([w_gate[0], w_up[0]], leads[last][0])
     before = last
     for i, stage in enumerate(stages):
-        if i + 1 < len(stages):
+        final = i + 1 == len(stages)
+        if not final:
             pass_on(stages[i + 1])
         share(stage)
-        take(stage)
+        every = take(stage, every)
         trade(stage)
-        after(theirs, [before], partial, stage)
-        give(before, stage if i + 1 == len(stages) else None)
-        if i + 1 < len(stages):
-            after(rows, stages[i + 1], own, before[0])
-        if i > 0:
+        if i == 0:
+            ids, partial[stage] = tie((ids, partial[stage]))
+            to_gate, to_up, hidden, token = prep(
+                ids, saved_gate[0], saved_up[0], capacity, (SPLIT, tiles), factors
+            )
+            wgate, token = hold(w_gate[0], token)
+            tokens = [token]
+            after(rows, stages[1], tokens, 0)
+        else:
+            if i == 1:
+                wup, _ = hold(w_up[0], leads[stage][0], *tokens)
+                held = (wgate, wup)
+            after(theirs, [before], partial, stage)
+            give(before)
+            if not final:
+                after(rows, stages[i + 1], own, before[0])
+            if i == 2:
+                after(theirs, [last], own, before[0])
+                give(last)
+                after(given, [before[0]], own, 0)
             collect(before[0], before[0] - 1 if before[0] > 1 else None)
         before = stage
-    after(theirs, [before], totals, before[0] - 1)
+    after(theirs, [before], totals[before[0] - 1], 0)
     give(before)
-    for s in list(range(before[0], chips)) + [0]:
-        collect(s, (s - 1) % chips)
-    parts = [arrived[stage] for stage in stages + [last]]
-    every = sort(ids, parts)
-    grad_down = jnp.dot(
-        hidden, every.reshape(slots, dcols), preferred_element_type=jnp.float32
-    ).astype(jnp.bfloat16)
-    return (totals[0], grad_down[None])
+    grads = [grad_rows(hidden, every, own[before[0]], 0, [])]
+    after(given, [before[0]], grads, 0)
+    for s in range(before[0], chips):
+        collect(s, s - 1)
+    grads = [grad_rows(hidden, every, totals[chips - 1][0], 1, grads)]
+    received = [mark(lax.ppermute(part, "expert", ring), 8.0) for part in totals[chips - 1]]
+    grad_x = add(slice(0, dcols), own[0], given[0], received)
+    (grad_down,) = grads
+    return (grad_x, grad_down[None])
 
 
 def solution(mesh):

time: 141 us -> 130 us (0.922)
  waiting for transfers between devices: 42.2 us -> 30.8 us
  matrix products: 7.91 us -> 0 us
  Pallas kernels: 58.4 us -> 66 us
  starting transfers between devices: 30.1 us -> 31.6 us
    ppermute x12 -> x16, waiting for transfers between devices: 39.3 us -> 27.9 us  [the longest x9 21.8 us: collect(): lax.ppermute(part, 'expert', ring)]
    dot_general x1 -> x0, matrix products: 7.91 us -> none  [ring_local(): jnp.dot(hidden, every.reshape(slots, dcols), preferred_element_type=jnp.f...]
    pallas_call x22 -> x45, Pallas kernels: 57 us -> 64.7 us  [the longest x5 20.7 us: give_rows(): pl.pallas_call(functools.partial(give_kernel, count, first), in_specs=[VM...]
    ppermute x8, waiting for transfers between devices: 1.82 us -> 0.02 us  [give(): given[s] = lax.ppermute(parts[2 * i + 1], 'expert', sibling)]
    ppermute x4, waiting for transfers between devices: 0.23 us -> 2.02 us  [pass_on(): rows[s] = lax.ppermute(rows[s - 1], 'expert', ring)]
    ppermute x12 -> x16, starting transfers between devices: 17.7 us -> 19.2 us  [the longest x9 10.3 us: collect(): lax.ppermute(part, 'expert', ring)]
  transfers between devices with their start and end apart: 35 -> 39, of which waited for: 14 -> 14; matrix products, arithmetic and copies ran while one was open for 7% -> 1% of each run, Pallas kernels for 39% -> 46%
where the time goes in v1:
time: 130 us
  Pallas kernels  66 us (51%)
  starting transfers between devices  31.6 us (24%)
  waiting for transfers between devices  30.8 us (24%)
    ppermute x9, waiting for transfers between devices, collect(): lax.ppermute(part, 'expert', ring)  21.8 us
    pallas_call x5, Pallas kernels, give_rows(): pl.pallas_call(functools.partial(give_kernel, count, first), in_specs=[VM...  20.7 us
    pallas_call x2, Pallas kernels, prep(): pl.pallas_call(functools.partial(prep_kernel, capacity, tiles[0]), grid_s...  12 us
    pallas_call x5, Pallas kernels, take_rows(): pl.pallas_call(functools.partial(take_kernel, experts, count, first), in_...  11.6 us
    ppermute x9, starting transfers between devices, collect(): lax.ppermute(part, 'expert', ring)  10.3 us
    pallas_call x3, Pallas kernels, hold(): pl.pallas_call(hold_kernel, in_specs=[ANY] * (1 + len(after)), out_specs=...  9.12 us
    pallas_call x2, Pallas kernels, grad_rows(): pl.pallas_call(grad_kernel, grid=(2,), in_specs=[pl.BlockSpec((rows, slot...  8.9 us
    ppermute x5, starting transfers between devices, trade(): theirs[stage] = mark(lax.ppermute(partial[stage], 'dp', swap), 10.0)  7.34 us
  transfers between devices with their start and end apart: 39, of which 14 were waited for; matrix products, arithmetic and copies ran while one was open for 1% of the time, Pallas kernels for 46%

profile of v1, /device:TPU:0, one launch (start us, length us, event | category | flops | bytes accessed | tf_op | source)
XLA Modules:
  0.0 130.0 jit_solution(4442341948785576277)
XLA Ops:
  0.6 1.3 %pack.1.refs_0_ = bf16[128,2176]{1,0:T(8,128)(2,1)S(1)} custom-call(bf16[128,2048]{1,0:T(8,128)(2,1)} %rows_ref.1, s32[6,128]{1,0:T(8,128)} %bitcast.20, f32[6,128]{1,0:T(8,128)} %bitcast.21, f32[1,128]{1,0:T(1,128)} %bitcast.22), custom_call_target="tpu_custom_call" | custom-call | tf_op jit(solution)/shard_map/pack/pallas_call | solution.py:134
  2.0 0.5 collective-permute-start.2
  2.5 2.6 %collective-permute-start = (bf16[128,2176]{1,0:T(8,128)(2,1)S(1)}, bf16[128,2176]{1,0:T(8,128)(2,1)S(1)}, u32[]{:S(2)}, u32[]{:S(2)}) collective-permute-start(bf16[128,2176]{1,0:T(8,128)(2,1)S(1)} %pack.1.refs_0_), channel_id=1, source_target_pairs={{0,4},{2,0},{4,8},{6,2},{8,12},{10,6},{12,14},{14,10},{5,1},{1,3},... | collective-permute-start | bytes 1671176 | tf_op jit(solution)/shard_map/ppermute | solution.py:446
  5.1 0.7 dynamic-slice_bitcast_fusion.ids_ref
  5.8 6.4 %prep.2 = (bf16[896,1408]{1,0:T(8,128)(2,1)S(1)}, bf16[896,1408]{1,0:T(8,128)(2,1)S(1)}, bf16[1408,896]{1,0:T(8,128)(2,1)S(1)}, f32[8,128]{1,0:T(8,128)S(1)}) custom-call(s32[16]{0:T(128)S(1)} %dynamic-slice_bitcast_fusion.ids_ref, bf16[1408,896]{1,0:T(8,128)(2,1)} %bitcast.13, bf16[1408,896]{1,0:T(8,128)(2,1)} %bitcast.15), custom_call_target="tpu_custom_call" | custom-call | flops 6881280 | bytes 6881280 | tf_op jit(solution)/shard_map/prep/pallas_call | solution.py:173
  12.2 3.2 %hold.3 = (bf16[1408,2048]{1,0:T(8,128)(2,1)S(1)}, f32[8,128]{1,0:T(8,128)}) custom-call(bf16[1408,2048]{1,0:T(8,128)(2,1)} %bitcast.17, f32[8,128]{1,0:T(8,128)S(1)} %get-tuple-element.83.refs_0_), custom_call_target="tpu_custom_call" | custom-call | tf_op jit(solution)/shard_map/hold/pallas_call | solution.py:206
  15.5 2.2 %take.5 = (bf16[896,2048]{1,0:T(8,128)(2,1)S(1)}, bf16[112,1408]{1,0:T(8,128)(2,1)S(1)}, bf16[128,56]{1,0:T(8,128)(2,1)S(1)}, bf16[128,56]{1,0:T(8,128)(2,1)S(1)}) custom-call(s32[1]{0:T(128)} %bitcast.me_ref, bf16[1408,2048]{1,0:T(8,128)(2,1)S(1)} %get-tuple-element.84.wdown_ref, bf16[128,2176]{1,0:T(8,128)(2,1)S(1)} %pack.1.refs_0_, ...), custom_call_target="tpu_custom_call" | custom-call | tf_op jit(solution)/shard_map/take/pallas_call | solution.py:252
  17.7 0.6 collective-permute-done.1.refs_2_
  18.5 0.4 collective-permute-start.4
  18.9 1.8 %collective-permute-start.6 = (bf16[128,2176]{1,0:T(8,128)(2,1)S(1)}, bf16[128,2176]{1,0:T(8,128)(2,1)S(1)}, u32[]{:S(2)}, u32[]{:S(2)}) collective-permute-start(bf16[128,2176]{1,0:T(8,128)(2,1)S(1)} %collective-permute-done.refs_0_), channel_id=1, source_target_pairs={{0,4},{2,0},{4,8},{6,2},{8,12},{10,6},{12,14},{14,10},{5,1},{1,3},... | collective-permute-start | bytes 1671176 | tf_op jit(solution)/shard_map/ppermute | solution.py:446
  20.6 0.3 collective-permute-start.7
  20.9 0.2 collective-permute-done.4.refs_3_
  21.1 2.4 %take.6 = (bf16[896,2048]{1,0:T(8,128)(2,1)S(1)}, bf16[224,1408]{1,0:T(8,128)(2,1)S(1)}, bf16[128,56]{1,0:T(8,128)(2,1)S(1)}, bf16[128,56]{1,0:T(8,128)(2,1)S(1)...) custom-call(s32[1]{0:T(128)} %bitcast.me_ref, ...), custom_call_target="tpu_custom_call", output_to_operand_aliasing={{0}: (6, {})} | custom-call | tf_op jit(solution)/shard_map/take/pallas_call | solution.py:252
  23.5 1.7 %collective-permute-start.5 = (bf16[224,1408]{1,0:T(8,128)(2,1)S(1)}, bf16[224,1408]{1,0:T(8,128)(2,1)S(1)}, u32[]{:S(2)}, u32[]{:S(2)}) collective-permute-start(bf16[224,1408]{1,0:T(8,128)(2,1)S(1)} %get-tuple-element.101.mine_ref), channel_id=1, source_target_pairs={{0,16},{16,0},{1,17},{17,1},{2,18},{18,2},{3,19},{19,3},{4,20},{20... | collective-permute-start | bytes 1892360 | tf_op jit(solution)/shard_map/ppermute | solution.py:462
  25.2 5.6 %prep.3 = (bf16[896,1408]{1,0:T(8,128)(2,1)S(1)}, bf16[896,1408]{1,0:T(8,128)(2,1)S(1)}, bf16[1408,896]{1,0:T(8,128)(2,1)S(1)}, f32[8,128]{1,0:T(8,128)S(1)}) custom-call(s32[16]{0:T(128)S(1)} %dynamic-slice_bitcast_fusion.ids_ref, bf16[1408,896]{1,0:T(8,128)(2,1)} %bitcast.14, ...), custom_call_target="tpu_custom_call", output_to_operand_aliasing={{0}: (3, {}), {1}: (4, {}), {2}: (5, {})} | custom-call | flops 5734400 | bytes 5734400 | tf_op jit(solution)/shard_map/prep/pallas_call | solution.py:173
  30.9 2.6 %hold.4 = (bf16[2048,1408]{1,0:T(8,128)(2,1)S(1)}, f32[8,128]{1,0:T(8,128)S(1)}) custom-call(bf16[2048,1408]{1,0:T(8,128)(2,1)} %bitcast.18, f32[8,128]{1,0:T(8,128)S(1)} %get-tuple-element.94.refs_0_), custom_call_target="tpu_custom_call" | custom-call | tf_op jit(solution)/shard_map/hold/pallas_call | solution.py:206
  33.6 0.9 collective-permute-start.8
  34.5 1.7 %collective-permute-start.16 = (bf16[112,1408]{1,0:T(8,128)(2,1)S(1)}, bf16[112,1408]{1,0:T(8,128)(2,1)S(1)}, u32[]{:S(2)}, u32[]{:S(2)}) collective-permute-start(bf16[112,1408]{1,0:T(8,128)(2,1)S(1)} %get-tuple-element.123.mine_ref), channel_id=1, source_target_pairs={{0,16},{16,0},{1,17},{17,1},{2,18},{18,2},{3,19},{19,3},{4,20},{20... | collective-permute-start | bytes 946184 | tf_op jit(solution)/shard_map/ppermute | solution.py:462
  36.1 1.5 %collective-permute-start.11 = (bf16[128,2176]{1,0:T(8,128)(2,1)S(1)}, bf16[128,2176]{1,0:T(8,128)(2,1)S(1)}, u32[]{:S(2)}, u32[]{:S(2)}) collective-permute-start(bf16[128,2176]{1,0:T(8,128)(2,1)S(1)} %collective-permute-done.6.refs_0_), channel_id=1, source_target_pairs={{0,4},{2,0},{4,8},{6,2},{8,12},{10,6},{12,14},{14,10},{5,1},{1,3},... | collective-permute-start | bytes 1671176 | tf_op jit(solution)/shard_map/ppermute | solution.py:446
  37.7 0.5 collective-permute-start.12
  38.2 2.4 %take.7 = (bf16[896,2048]{1,0:T(8,128)(2,1)S(1)}, bf16[224,1408]{1,0:T(8,128)(2,1)S(1)}, bf16[128,56]{1,0:T(8,128)(2,1)S(1)}, bf16[128,56]{1,0:T(8,128)(2,1)S(1)...) custom-call(s32[1]{0:T(128)} %bitcast.me_ref, ...), custom_call_target="tpu_custom_call", output_to_operand_aliasing={{0}: (6, {})} | custom-call | tf_op jit(solution)/shard_map/take/pallas_call | solution.py:252
  40.6 1.1 collective-permute-start.10
  41.7 3.2 %hold.5 = (bf16[2048,1408]{1,0:T(8,128)(2,1)S(1)}, f32[8,128]{1,0:T(8,128)}) custom-call(bf16[2048,1408]{1,0:T(8,128)(2,1)} %bitcast.19, bf16[128,56]{1,0:T(8,128)(2,1)S(1)} %get-tuple-element.106.refs_0_, f32[8,128]{1,0:T(8,128)S(1)} %get-tuple-element.107.refs_1_), custom_call_target="tpu_custom_call" | custom-call | tf_op jit(solution)/shard_map/hold/pallas_call | solution.py:206
  44.9 4.3 %give.5 = (bf16[128,2048]{1,0:T(8,128)(2,1)S(1)}, bf16[128,2048]{1,0:T(8,128)(2,1)S(1)}, bf16[128,2048]{1,0:T(8,128)(2,1)S(1)}, bf16[128,2048]{1,0:T(8,128)(2,1)S(1)}) custom-call(bf16[224,1408]{1,0:T(8,128)(2,1)S(1)} %get-tuple-element.101.mine_ref, bf16[224,1408]{1,0:T(8,128)(2,1)S(1)} %mark.16.theirs_ref, ...), custom_call_target="tpu_custom_call" | custom-call | tf_op jit(solution)/shard_map/give/pallas_call | solution.py:292
  49.3 1.9 %collective-permute-done.11.refs_0_ = bf16[128,2176]{1,0:T(8,128)(2,1)S(1)} collective-permute-done((bf16[128,2176]{1,0:T(8,128)(2,1)S(1)}, bf16[128,2176]{1,0:T(8,128)(2,1)S(1)}, u32[]{:S(2)}, u32[]{:S(2)}) %collective-permute-start.11) | collective-permute-done | bytes 557088 | tf_op jit(solution)/shard_map/ppermute | solution.py:446
  51.2 0.5 collective-permute-start.13
  51.8 1.4 %collective-permute-start.17 = (bf16[128,2176]{1,0:T(8,128)(2,1)S(1)}, bf16[128,2176]{1,0:T(8,128)(2,1)S(1)}, u32[]{:S(2)}, u32[]{:S(2)}) collective-permute-start(bf16[128,2176]{1,0:T(8,128)(2,1)S(1)} %collective-permute-done.11.refs_0_), channel_id=1, source_target_pairs={{0,4},{2,0},{4,8},{6,2},{8,12},{10,6},{12,14},{14,10},{5,1},{1,3},... | collective-permute-start | bytes 1671176 | tf_op jit(solution)/shard_map/ppermute | solution.py:446
  53.3 1.2 collective-permute-start.27
  54.6 2.4 %take.8 = (bf16[896,2048]{1,0:T(8,128)(2,1)S(1)}, bf16[224,1408]{1,0:T(8,128)(2,1)S(1)}, bf16[128,56]{1,0:T(8,128)(2,1)S(1)}, bf16[128,56]{1,0:T(8,128)(2,1)S(1)...) custom-call(s32[1]{0:T(128)} %bitcast.me_ref, ...), custom_call_target="tpu_custom_call", output_to_operand_aliasing={{0}: (6, {})} | custom-call | tf_op jit(solution)/shard_map/take/pallas_call | solution.py:252
  57.0 1.1 collective-permute-start.21
  58.1 2.1 %collective-permute-done.10.old_ref = bf16[224,1408]{1,0:T(8,128)(2,1)S(1)} collective-permute-done((bf16[224,1408]{1,0:T(8,128)(2,1)S(1)}, bf16[224,1408]{1,0:T(8,128)(2,1)S(1)}, u32[]{:S(2)}, u32[]{:S(2)}) %collective-permute-start.10) | collective-permute-done | bytes 630816 | tf_op jit(solution)/shard_map/ppermute | solution.py:462
  60.2 4.3 %give.6 = (bf16[128,2048]{1,0:T(8,128)(2,1)S(1)}, bf16[128,2048]{1,0:T(8,128)(2,1)S(1)}, bf16[128,2048]{1,0:T(8,128)(2,1)S(1)}, bf16[128,2048]{1,0:T(8,128)(2,1)S(1)}) custom-call(bf16[224,1408]{1,0:T(8,128)(2,1)S(1)} %get-tuple-element.100.mine_ref, bf16[224,1408]{1,0:T(8,128)(2,1)S(1)} %mark.17.theirs_ref, ...), custom_call_target="tpu_custom_call" | custom-call | tf_op jit(solution)/shard_map/give/pallas_call | solution.py:292
  64.6 0.5 collective-permute-start.22
  65.1 3.9 %give.7 = (bf16[128,2048]{1,0:T(8,128)(2,1)S(1)}, bf16[128,2048]{1,0:T(8,128)(2,1)S(1)}) custom-call(bf16[112,1408]{1,0:T(8,128)(2,1)S(1)} %get-tuple-element.123.mine_ref, bf16[112,1408]{1,0:T(8,128)(2,1)S(1)} %mark.18.theirs_ref, bf16[896,1408]{1,0:T(8,128)(2,1)S(1)} %get-tuple-element.103.to_gate_ref, bf16[896,1408]{1,0:T(8,128)(2,1)S(1)} %get-tuple-element.104.to_up_ref, ...), custom_call_target="tpu_custom_call" | custom-call | tf_op jit(solution)/shard_map/give/pallas_call | solution.py:292
  69.0 0.2 add.17
  69.3 2.7 %collective-permute-start.28 = (bf16[128,2048]{1,0:T(8,128)(2,1)S(1)}, bf16[128,2048]{1,0:T(8,128)(2,1)S(1)}, u32[]{:S(2)}, u32[]{:S(2)}) collective-permute-start(bf16[128,2048]{1,0:T(8,128)(2,1)S(1)} %add.17), channel_id=1, source_target_pairs={{0,4},{2,0},{4,8},{6,2},{8,12},{10,6},{12,14},{14,10},{5,1},{1,3},... | collective-permute-start | bytes 1572872 | tf_op jit(solution)/shard_map/ppermute | solution.py:475
  71.9 2.2 %take.9 = (bf16[896,2048]{1,0:T(8,128)(2,1)S(1)}, bf16[112,1408]{1,0:T(8,128)(2,1)S(1)}, bf16[128,56]{1,0:T(8,128)(2,1)S(1)}, bf16[128,56]{1,0:T(8,128)(2,1)S(1)}) custom-call(s32[1]{0:T(128)} %bitcast.me_ref, bf16[1408,2048]{1,0:T(8,128)(2,1)S(1)} %get-tuple-element.84.wdown_ref, ...), custom_call_target="tpu_custom_call", output_to_operand_aliasing={{0}: (4, {})} | custom-call | tf_op jit(solution)/shard_map/take/pallas_call | solution.py:252
  74.2 1.7 %collective-permute-start.24 = (bf16[112,1408]{1,0:T(8,128)(2,1)S(1)}, bf16[112,1408]{1,0:T(8,128)(2,1)S(1)}, u32[]{:S(2)}, u32[]{:S(2)}) collective-permute-start(bf16[112,1408]{1,0:T(8,128)(2,1)S(1)} %get-tuple-element.147.mine_ref), channel_id=1, source_target_pairs={{0,16},{16,0},{1,17},{17,1},{2,18},{18,2},{3,19},{19,3},{4,20},{20... | collective-permute-start | bytes 946184 | tf_op jit(solution)/shard_map/ppermute | solution.py:462
  75.9 4.3 %give.8 = (bf16[128,2048]{1,0:T(8,128)(2,1)S(1)}, bf16[128,2048]{1,0:T(8,128)(2,1)S(1)}, bf16[128,2048]{1,0:T(8,128)(2,1)S(1)}, bf16[128,2048]{1,0:T(8,128)(2,1)S(1)}) custom-call(bf16[224,1408]{1,0:T(8,128)(2,1)S(1)} %get-tuple-element.136.mine_ref, bf16[224,1408]{1,0:T(8,128)(2,1)S(1)} %mark.19.theirs_ref, ...), custom_call_target="tpu_custom_call" | custom-call | tf_op jit(solution)/shard_map/give/pallas_call | solution.py:292
  80.3 2.8 %collective-permute-done.24.old_ref = bf16[112,1408]{1,0:T(8,128)(2,1)S(1)} collective-permute-done((bf16[112,1408]{1,0:T(8,128)(2,1)S(1)}, bf16[112,1408]{1,0:T(8,128)(2,1)S(1)}, u32[]{:S(2)}, u32[]{:S(2)}) %collective-permute-start.24) | collective-permute-done | bytes 315424 | tf_op jit(solution)/shard_map/ppermute | solution.py:462
  83.1 0.2 add.18
  83.3 3.9 %give.9 = (bf16[128,2048]{1,0:T(8,128)(2,1)S(1)}, bf16[128,2048]{1,0:T(8,128)(2,1)S(1)}) custom-call(bf16[112,1408]{1,0:T(8,128)(2,1)S(1)} %get-tuple-element.147.mine_ref, bf16[112,1408]{1,0:T(8,128)(2,1)S(1)} %mark.20.theirs_ref, bf16[896,1408]{1,0:T(8,128)(2,1)S(1)} %get-tuple-element.103.to_gate_ref, bf16[896,1408]{1,0:T(8,128)(2,1)S(1)} %get-tuple-element.104.to_up_ref, ...), custom_call_target="tpu_custom_call" | custom-call | tf_op jit(solution)/shard_map/give/pallas_call | solution.py:292
  87.3 0.8 collective-permute-start.30
  88.1 4.4 %grad_down.2.refs_0_ = bf16[1408,2048]{1,0:T(8,128)(2,1)} custom-call(bf16[1408,896]{1,0:T(8,128)(2,1)S(1)} %get-tuple-element.159.hidden_ref, bf16[896,2048]{1,0:T(8,128)(2,1)S(1)} %get-tuple-element.160.every_ref, bf16[128,2048]{1,0:T(8,128)(2,1)S(1)} %get-tuple-element.157.after_ref.own_ref), custom_call_target="tpu_custom_call" | custom-call | tf_op jit(solution)/shard_map/grad_down/pallas_call | solution.py:336
  92.5 4.0 %collective-permute-done.30.old_ref = bf16[128,2048]{1,0:T(8,128)(2,1)S(1)} collective-permute-done((bf16[128,2048]{1,0:T(8,128)(2,1)S(1)}, bf16[128,2048]{1,0:T(8,128)(2,1)S(1)}, u32[]{:S(2)}, u32[]{:S(2)}) %collective-permute-start.30) | collective-permute-done | bytes 524320 | tf_op jit(solution)/shard_map/ppermute | solution.py:475
  96.6 0.8 collective-permute-start.35
  97.4 0.5 collective-permute-start.20
  97.9 0.5 collective-permute-start.23
  98.5 4.5 %collective-permute-done.35.old_ref = bf16[128,1024]{1,0:T(8,128)(2,1)S(1)} collective-permute-done((bf16[128,1024]{1,0:T(8,128)(2,1)S(1)}, bf16[128,1024]{1,0:T(8,128)(2,1)S(1)}, u32[]{:S(2)}, u32[]{:S(2)}) %collective-permute-start.35) | collective-permute-done | bytes 262176 | tf_op jit(solution)/shard_map/ppermute | solution.py:475
  103.1 0.7 collective-permute-start.31
  103.9 1.7 %collective-permute-start.36 = (bf16[128,1024]{1,0:T(8,128)(2,1)S(1)}, bf16[128,1024]{1,0:T(8,128)(2,1)S(1)}, u32[]{:S(2)}, u32[]{:S(2)}) collective-permute-start(bf16[128,1024]{1,0:T(8,128)(2,1)S(1)} %add.24), channel_id=1, source_target_pairs={{0,4},{2,0},{4,8},{6,2},{8,12},{10,6},{12,14},{14,10},{5,1},{1,3},... | collective-permute-start | bytes 786440 | tf_op jit(solution)/shard_map/ppermute | solution.py:475
  105.6 3.9 %collective-permute-done.31.old_ref = bf16[128,1024]{1,0:T(8,128)(2,1)S(1)} collective-permute-done((bf16[128,1024]{1,0:T(8,128)(2,1)S(1)}, bf16[128,1024]{1,0:T(8,128)(2,1)S(1)}, u32[]{:S(2)}, u32[]{:S(2)}) %collective-permute-start.31) | collective-permute-done | bytes 262176 | tf_op jit(solution)/shard_map/ppermute | solution.py:475
  109.5 0.8 collective-permute-start.32
  110.3 1.9 %collective-permute-done.36.old_ref = bf16[128,1024]{1,0:T(8,128)(2,1)S(1)} collective-permute-done((bf16[128,1024]{1,0:T(8,128)(2,1)S(1)}, bf16[128,1024]{1,0:T(8,128)(2,1)S(1)}, u32[]{:S(2)}, u32[]{:S(2)}) %collective-permute-start.36) | collective-permute-done | bytes 262176 | tf_op jit(solution)/shard_map/ppermute | solution.py:475
  112.3 0.8 collective-permute-start.37
  113.1 2.8 %collective-permute-done.32.old_ref = bf16[128,1024]{1,0:T(8,128)(2,1)S(1)} collective-permute-done((bf16[128,1024]{1,0:T(8,128)(2,1)S(1)}, bf16[128,1024]{1,0:T(8,128)(2,1)S(1)}, u32[]{:S(2)}, u32[]{:S(2)}) %collective-permute-start.32) | collective-permute-done | bytes 262176 | tf_op jit(solution)/shard_map/ppermute | solution.py:475
  116.1 0.8 collective-permute-start.33
  116.9 1.9 %collective-permute-done.37.old_ref = bf16[128,1024]{1,0:T(8,128)(2,1)S(1)} collective-permute-done((bf16[128,1024]{1,0:T(8,128)(2,1)S(1)}, bf16[128,1024]{1,0:T(8,128)(2,1)S(1)}, u32[]{:S(2)}, u32[]{:S(2)}) %collective-permute-start.37) | collective-permute-done | bytes 262176 | tf_op jit(solution)/shard_map/ppermute | solution.py:475
  118.9 0.8 collective-permute-start.38
  119.7 2.8 %collective-permute-done.33.old_ref = bf16[128,1024]{1,0:T(8,128)(2,1)S(1)} collective-permute-done((bf16[128,1024]{1,0:T(8,128)(2,1)S(1)}, bf16[128,1024]{1,0:T(8,128)(2,1)S(1)}, u32[]{:S(2)}, u32[]{:S(2)}) %collective-permute-start.33) | collective-permute-done | bytes 262176 | tf_op jit(solution)/shard_map/ppermute | solution.py:475
  122.6 0.8 collective-permute-start.34
  123.4 4.4 %grad_down.3 = bf16[1408,2048]{1,0:T(8,128)(2,1)} custom-call(bf16[1408,896]{1,0:T(8,128)(2,1)S(1)} %get-tuple-element.159.hidden_ref, bf16[896,2048]{1,0:T(8,128)(2,1)S(1)} %get-tuple-element.160.every_ref, bf16[128,1024]{1,0:T(8,128)(2,1)S(1)} %add.22.after_ref, bf16[1408,2048]{1,0:T(8,128)(2,1)} %grad_down.2.refs_0_), custom_call_target="tpu_custom_call", output_to_operand_aliasing={{}: (3, {})} | custom-call | tf_op jit(solution)/shard_map/grad_down/pallas_call | solution.py:336
  127.8 1.2 collective-permute-done.34.old_ref
  129.0 1.0 add.27
  (61 shorter events, 1.5 us)
Async XLA Ops:
  2.0 13.5 %collective-permute-start.2 = (bf16[128,2176]{1,0:T(8,128)(2,1)S(1)}, bf16[128,2176]{1,0:T(8,128)(2,1)S(1)}, u32[]{:S(2)}, u32[]{:S(2)}) collective-permute-start(bf16[128,2176]{1,0:T(8,128)(2,1)S(1)} %pack.1.refs_0_), channel_id=1, source_target_pairs={{0,1},{1,0},{2,3},{3,2},{4,5},{5,4},{6,7},{7,6},{8,9},{9,8},{10,11... | collective-permute-start | bytes 1671176 | tf_op jit(solution)/shard_map/ppermute | solution.py:452
  2.5 15.2 %collective-permute-start = (bf16[128,2176]{1,0:T(8,128)(2,1)S(1)}, bf16[128,2176]{1,0:T(8,128)(2,1)S(1)}, u32[]{:S(2)}, u32[]{:S(2)}) collective-permute-start(bf16[128,2176]{1,0:T(8,128)(2,1)S(1)} %pack.1.refs_0_), channel_id=1, source_target_pairs={{0,4},{2,0},{4,8},{6,2},{8,12},{10,6},{12,14},{14,10},{5,1},{1,3},... | collective-permute-start | bytes 1671176 | tf_op jit(solution)/shard_map/ppermute | solution.py:446
  5.1 13.2 %collective-permute-start.1 = (bf16[128,2176]{1,0:T(8,128)(2,1)S(1)}, bf16[128,2176]{1,0:T(8,128)(2,1)S(1)}, u32[]{:S(2)}, u32[]{:S(2)}) collective-permute-start(bf16[128,2176]{1,0:T(8,128)(2,1)S(1)} %pack.1.refs_0_), channel_id=1, source_target_pairs={{4,0},{0,2},{8,4},{2,6},{12,8},{6,10},{14,12},{10,14},{1,5},{3,1},... | collective-permute-start | bytes 1671176 | tf_op jit(solution)/shard_map/ppermute | solution.py:448
  18.4 2.5 %collective-permute-start.3 = (bf16[128,2176]{1,0:T(8,128)(2,1)S(1)}, bf16[128,2176]{1,0:T(8,128)(2,1)S(1)}, u32[]{:S(2)}, u32[]{:S(2)}) collective-permute-start(bf16[128,2176]{1,0:T(8,128)(2,1)S(1)} %collective-permute-done.refs_0_), channel_id=1, source_target_pairs={{0,1},{1,0},{2,3},{3,2},{4,5},{5,4},{6,7},{7,6},{8,9},{9,8},{10,11... | collective-permute-start | bytes 1671176 | tf_op jit(solution)/shard_map/ppermute | solution.py:452
  18.5 2.6 %collective-permute-start.4 = (bf16[128,2176]{1,0:T(8,128)(2,1)S(1)}, bf16[128,2176]{1,0:T(8,128)(2,1)S(1)}, u32[]{:S(2)}, u32[]{:S(2)}) collective-permute-start(bf16[128,2176]{1,0:T(8,128)(2,1)S(1)} %collective-permute-done.1.refs_2_), channel_id=1, source_target_pairs={{0,1},{1,0},{2,3},{3,2},{4,5},{5,4},{6,7},{7,6},{8,9},{9,8},{10,11... | collective-permute-start | bytes 1671176 | tf_op jit(solution)/shard_map/ppermute | solution.py:452
  18.9 14.7 %collective-permute-start.6 = (bf16[128,2176]{1,0:T(8,128)(2,1)S(1)}, bf16[128,2176]{1,0:T(8,128)(2,1)S(1)}, u32[]{:S(2)}, u32[]{:S(2)}) collective-permute-start(bf16[128,2176]{1,0:T(8,128)(2,1)S(1)} %collective-permute-done.refs_0_), channel_id=1, source_target_pairs={{0,4},{2,0},{4,8},{6,2},{8,12},{10,6},{12,14},{14,10},{5,1},{1,3},... | collective-permute-start | bytes 1671176 | tf_op jit(solution)/shard_map/ppermute | solution.py:446
  20.6 13.0 %collective-permute-start.7 = (bf16[128,2176]{1,0:T(8,128)(2,1)S(1)}, bf16[128,2176]{1,0:T(8,128)(2,1)S(1)}, u32[]{:S(2)}, u32[]{:S(2)}) collective-permute-start(bf16[128,2176]{1,0:T(8,128)(2,1)S(1)} %collective-permute-done.1.refs_2_), channel_id=1, source_target_pairs={{4,0},{0,2},{8,4},{2,6},{12,8},{6,10},{14,12},{10,14},{1,5},{3,1},... | collective-permute-start | bytes 1671176 | tf_op jit(solution)/shard_map/ppermute | solution.py:448
  23.5 21.5 %collective-permute-start.5 = (bf16[224,1408]{1,0:T(8,128)(2,1)S(1)}, bf16[224,1408]{1,0:T(8,128)(2,1)S(1)}, u32[]{:S(2)}, u32[]{:S(2)}) collective-permute-start(bf16[224,1408]{1,0:T(8,128)(2,1)S(1)} %get-tuple-element.101.mine_ref), channel_id=1, source_target_pairs={{0,16},{16,0},{1,17},{17,1},{2,18},{18,2},{3,19},{19,3},{4,20},{20... | collective-permute-start | bytes 1892360 | tf_op jit(solution)/shard_map/ppermute | solution.py:462
  33.6 4.0 %collective-permute-start.8 = (bf16[128,2176]{1,0:T(8,128)(2,1)S(1)}, bf16[128,2176]{1,0:T(8,128)(2,1)S(1)}, u32[]{:S(2)}, u32[]{:S(2)}) collective-permute-start(bf16[128,2176]{1,0:T(8,128)(2,1)S(1)} %collective-permute-done.6.refs_0_), channel_id=1, source_target_pairs={{0,1},{1,0},{2,3},{3,2},{4,5},{5,4},{6,7},{7,6},{8,9},{9,8},{10,11... | collective-permute-start | bytes 1671176 | tf_op jit(solution)/shard_map/ppermute | solution.py:452
  34.5 3.7 %collective-permute-start.9 = (bf16[128,2176]{1,0:T(8,128)(2,1)S(1)}, bf16[128,2176]{1,0:T(8,128)(2,1)S(1)}, u32[]{:S(2)}, u32[]{:S(2)}) collective-permute-start(bf16[128,2176]{1,0:T(8,128)(2,1)S(1)} %collective-permute-done.7.refs_2_), channel_id=1, source_target_pairs={{0,1},{1,0},{2,3},{3,2},{4,5},{5,4},{6,7},{7,6},{8,9},{9,8},{10,11... | collective-permute-start | bytes 1671176 | tf_op jit(solution)/shard_map/ppermute | solution.py:452
  34.5 17.3 %collective-permute-start.16 = (bf16[112,1408]{1,0:T(8,128)(2,1)S(1)}, bf16[112,1408]{1,0:T(8,128)(2,1)S(1)}, u32[]{:S(2)}, u32[]{:S(2)}) collective-permute-start(bf16[112,1408]{1,0:T(8,128)(2,1)S(1)} %get-tuple-element.123.mine_ref), channel_id=1, source_target_pairs={{0,16},{16,0},{1,17},{17,1},{2,18},{18,2},{3,19},{19,3},{4,20},{20... | collective-permute-start | bytes 946184 | tf_op jit(solution)/shard_map/ppermute | solution.py:462
  36.1 15.1 %collective-permute-start.11 = (bf16[128,2176]{1,0:T(8,128)(2,1)S(1)}, bf16[128,2176]{1,0:T(8,128)(2,1)S(1)}, u32[]{:S(2)}, u32[]{:S(2)}) collective-permute-start(bf16[128,2176]{1,0:T(8,128)(2,1)S(1)} %collective-permute-done.6.refs_0_), channel_id=1, source_target_pairs={{0,4},{2,0},{4,8},{6,2},{8,12},{10,6},{12,14},{14,10},{5,1},{1,3},... | collective-permute-start | bytes 1671176 | tf_op jit(solution)/shard_map/ppermute | solution.py:446
  37.7 13.5 %collective-permute-start.12 = (bf16[128,2176]{1,0:T(8,128)(2,1)S(1)}, bf16[128,2176]{1,0:T(8,128)(2,1)S(1)}, u32[]{:S(2)}, u32[]{:S(2)}) collective-permute-start(bf16[128,2176]{1,0:T(8,128)(2,1)S(1)} %collective-permute-done.7.refs_2_), channel_id=1, source_target_pairs={{4,0},{0,2},{8,4},{2,6},{12,8},{6,10},{14,12},{10,14},{1,5},{3,1},... | collective-permute-start | bytes 1671176 | tf_op jit(solution)/shard_map/ppermute | solution.py:448
  40.6 19.6 %collective-permute-start.10 = (bf16[224,1408]{1,0:T(8,128)(2,1)S(1)}, bf16[224,1408]{1,0:T(8,128)(2,1)S(1)}, u32[]{:S(2)}, u32[]{:S(2)}) collective-permute-start(bf16[224,1408]{1,0:T(8,128)(2,1)S(1)} %get-tuple-element.100.mine_ref), channel_id=1, source_target_pairs={{0,16},{16,0},{1,17},{17,1},{2,18},{18,2},{3,19},{19,3},{4,20},{20... | collective-permute-start | bytes 1892360 | tf_op jit(solution)/shard_map/ppermute | solution.py:462
  49.2 3.9 %collective-permute-start.26 = (bf16[128,2048]{1,0:T(8,128)(2,1)S(1)}, bf16[128,2048]{1,0:T(8,128)(2,1)S(1)}, u32[]{:S(2)}, u32[]{:S(2)}) collective-permute-start(bf16[128,2048]{1,0:T(8,128)(2,1)S(1)} %get-tuple-element.153), channel_id=1, source_target_pairs={{0,1},{1,0},{2,3},{3,2},{4,5},{5,4},{6,7},{7,6},{8,9},{9,8},{10,11... | collective-permute-start | bytes 1572872 | tf_op jit(solution)/shard_map/ppermute | solution.py:471
  51.2 3.3 %collective-permute-start.13 = (bf16[128,2176]{1,0:T(8,128)(2,1)S(1)}, bf16[128,2176]{1,0:T(8,128)(2,1)S(1)}, u32[]{:S(2)}, u32[]{:S(2)}) collective-permute-start(bf16[128,2176]{1,0:T(8,128)(2,1)S(1)} %collective-permute-done.11.refs_0_), channel_id=1, source_target_pairs={{0,1},{1,0},{2,3},{3,2},{4,5},{5,4},{6,7},{7,6},{8,9},{9,8},{10,11... | collective-permute-start | bytes 1671176 | tf_op jit(solution)/shard_map/ppermute | solution.py:452
  51.8 2.8 %collective-permute-start.14 = (bf16[128,2176]{1,0:T(8,128)(2,1)S(1)}, bf16[128,2176]{1,0:T(8,128)(2,1)S(1)}, u32[]{:S(2)}, u32[]{:S(2)}) collective-permute-start(bf16[128,2176]{1,0:T(8,128)(2,1)S(1)} %collective-permute-done.12.refs_2_), channel_id=1, source_target_pairs={{0,1},{1,0},{2,3},{3,2},{4,5},{5,4},{6,7},{7,6},{8,9},{9,8},{10,11... | collective-permute-start | bytes 1671176 | tf_op jit(solution)/shard_map/ppermute | solution.py:452
  51.8 12.7 %collective-permute-start.17 = (bf16[128,2176]{1,0:T(8,128)(2,1)S(1)}, bf16[128,2176]{1,0:T(8,128)(2,1)S(1)}, u32[]{:S(2)}, u32[]{:S(2)}) collective-permute-start(bf16[128,2176]{1,0:T(8,128)(2,1)S(1)} %collective-permute-done.11.refs_0_), channel_id=1, source_target_pairs={{0,4},{2,0},{4,8},{6,2},{8,12},{10,6},{12,14},{14,10},{5,1},{1,3},... | collective-permute-start | bytes 1671176 | tf_op jit(solution)/shard_map/ppermute | solution.py:446
  53.3 15.7 %collective-permute-start.27 = (bf16[128,2048]{1,0:T(8,128)(2,1)S(1)}, bf16[128,2048]{1,0:T(8,128)(2,1)S(1)}, u32[]{:S(2)}, u32[]{:S(2)}) collective-permute-start(bf16[128,2048]{1,0:T(8,128)(2,1)S(1)} %add.16), channel_id=1, source_target_pairs={{0,4},{2,0},{4,8},{6,2},{8,12},{10,6},{12,14},{14,10},{5,1},{1,3},... | collective-permute-start | bytes 1572872 | tf_op jit(solution)/shard_map/ppermute | solution.py:475
  57.0 19.0 %collective-permute-start.21 = (bf16[224,1408]{1,0:T(8,128)(2,1)S(1)}, bf16[224,1408]{1,0:T(8,128)(2,1)S(1)}, u32[]{:S(2)}, u32[]{:S(2)}) collective-permute-start(bf16[224,1408]{1,0:T(8,128)(2,1)S(1)} %get-tuple-element.136.mine_ref), channel_id=1, source_target_pairs={{0,16},{16,0},{1,17},{17,1},{2,18},{18,2},{3,19},{19,3},{4,20},{20... | collective-permute-start | bytes 1892360 | tf_op jit(solution)/shard_map/ppermute | solution.py:462
  64.5 4.5 %collective-permute-start.15 = (bf16[128,2048]{1,0:T(8,128)(2,1)S(1)}, bf16[128,2048]{1,0:T(8,128)(2,1)S(1)}, u32[]{:S(2)}, u32[]{:S(2)}) collective-permute-start(bf16[128,2048]{1,0:T(8,128)(2,1)S(1)} %get-tuple-element.122), channel_id=1, source_target_pairs={{0,1},{1,0},{2,3},{3,2},{4,5},{5,4},{6,7},{7,6},{8,9},{9,8},{10,11... | collective-permute-start | bytes 1572872 | tf_op jit(solution)/shard_map/ppermute | solution.py:471
  64.6 7.4 %collective-permute-start.22 = (bf16[128,2176]{1,0:T(8,128)(2,1)S(1)}, bf16[128,2176]{1,0:T(8,128)(2,1)S(1)}, u32[]{:S(2)}, u32[]{:S(2)}) collective-permute-start(bf16[128,2176]{1,0:T(8,128)(2,1)S(1)} %collective-permute-done.17.refs_0_), channel_id=1, source_target_pairs={{0,1},{1,0},{2,3},{3,2},{4,5},{5,4},{6,7},{7,6},{8,9},{9,8},{10,11... | collective-permute-start | bytes 1671176 | tf_op jit(solution)/shard_map/ppermute | solution.py:452
  69.3 13.8 %collective-permute-start.28 = (bf16[128,2048]{1,0:T(8,128)(2,1)S(1)}, bf16[128,2048]{1,0:T(8,128)(2,1)S(1)}, u32[]{:S(2)}, u32[]{:S(2)}) collective-permute-start(bf16[128,2048]{1,0:T(8,128)(2,1)S(1)} %add.17), channel_id=1, source_target_pairs={{0,4},{2,0},{4,8},{6,2},{8,12},{10,6},{12,14},{14,10},{5,1},{1,3},... | collective-permute-start | bytes 1572872 | tf_op jit(solution)/shard_map/ppermute | solution.py:475
  74.2 8.9 %collective-permute-start.24 = (bf16[112,1408]{1,0:T(8,128)(2,1)S(1)}, bf16[112,1408]{1,0:T(8,128)(2,1)S(1)}, u32[]{:S(2)}, u32[]{:S(2)}) collective-permute-start(bf16[112,1408]{1,0:T(8,128)(2,1)S(1)} %get-tuple-element.147.mine_ref), channel_id=1, source_target_pairs={{0,16},{16,0},{1,17},{17,1},{2,18},{18,2},{3,19},{19,3},{4,20},{20... | collective-permute-start | bytes 946184 | tf_op jit(solution)/shard_map/ppermute | solution.py:462
  80.2 2.9 %collective-permute-start.25 = (bf16[128,2048]{1,0:T(8,128)(2,1)S(1)}, bf16[128,2048]{1,0:T(8,128)(2,1)S(1)}, u32[]{:S(2)}, u32[]{:S(2)}) collective-permute-start(bf16[128,2048]{1,0:T(8,128)(2,1)S(1)} %get-tuple-element.149), channel_id=1, source_target_pairs={{0,1},{1,0},{2,3},{3,2},{4,5},{5,4},{6,7},{7,6},{8,9},{9,8},{10,11... | collective-permute-start | bytes 1572872 | tf_op jit(solution)/shard_map/ppermute | solution.py:471
  87.2 5.3 %collective-permute-start.29 = (bf16[128,2048]{1,0:T(8,128)(2,1)S(1)}, bf16[128,2048]{1,0:T(8,128)(2,1)S(1)}, u32[]{:S(2)}, u32[]{:S(2)}) collective-permute-start(bf16[128,2048]{1,0:T(8,128)(2,1)S(1)} %get-tuple-element.158), channel_id=1, source_target_pairs={{0,1},{1,0},{2,3},{3,2},{4,5},{5,4},{6,7},{7,6},{8,9},{9,8},{10,11... | collective-permute-start | bytes 1572872 | tf_op jit(solution)/shard_map/ppermute | solution.py:471
  87.3 9.2 %collective-permute-start.30 = (bf16[128,2048]{1,0:T(8,128)(2,1)S(1)}, bf16[128,2048]{1,0:T(8,128)(2,1)S(1)}, u32[]{:S(2)}, u32[]{:S(2)}) collective-permute-start(bf16[128,2048]{1,0:T(8,128)(2,1)S(1)} %add.18), channel_id=1, source_target_pairs={{0,4},{2,0},{4,8},{6,2},{8,12},{10,6},{12,14},{14,10},{5,1},{1,3},... | collective-permute-start | bytes 1572872 | tf_op jit(solution)/shard_map/ppermute | solution.py:475
  96.6 6.4 %collective-permute-start.35 = (bf16[128,1024]{1,0:T(8,128)(2,1)S(1)}, bf16[128,1024]{1,0:T(8,128)(2,1)S(1)}, u32[]{:S(2)}, u32[]{:S(2)}) collective-permute-start(bf16[128,1024]{1,0:T(8,128)(2,1)S(1)} %add.23), channel_id=1, source_target_pairs={{0,4},{2,0},{4,8},{6,2},{8,12},{10,6},{12,14},{14,10},{5,1},{1,3},... | collective-permute-start | bytes 786440 | tf_op jit(solution)/shard_map/ppermute | solution.py:475
  97.4 21.3 %collective-permute-start.19 = (bf16[128,2048]{1,0:T(8,128)(2,1)S(1)}, bf16[128,2048]{1,0:T(8,128)(2,1)S(1)}, u32[]{:S(2)}, u32[]{:S(2)}) collective-permute-start(bf16[128,2048]{1,0:T(8,128)(2,1)S(1)} %get-tuple-element.133), channel_id=1, source_target_pairs={{0,1},{1,0},{2,3},{3,2},{4,5},{5,4},{6,7},{7,6},{8,9},{9,8},{10,11... | collective-permute-start | bytes 1572872 | tf_op jit(solution)/shard_map/ppermute | solution.py:471
  97.4 14.8 %collective-permute-start.20 = (bf16[128,2048]{1,0:T(8,128)(2,1)S(1)}, bf16[128,2048]{1,0:T(8,128)(2,1)S(1)}, u32[]{:S(2)}, u32[]{:S(2)}) collective-permute-start(bf16[128,2048]{1,0:T(8,128)(2,1)S(1)} %get-tuple-element.135), channel_id=1, source_target_pairs={{0,1},{1,0},{2,3},{3,2},{4,5},{5,4},{6,7},{7,6},{8,9},{9,8},{10,11... | collective-permute-start | bytes 1572872 | tf_op jit(solution)/shard_map/ppermute | solution.py:471
  97.9 31.1 %collective-permute-start.18 = (bf16[128,2048]{1,0:T(8,128)(2,1)S(1)}, bf16[128,2048]{1,0:T(8,128)(2,1)S(1)}, u32[]{:S(2)}, u32[]{:S(2)}) collective-permute-start(bf16[128,2048]{1,0:T(8,128)(2,1)S(1)} %get-tuple-element.131), channel_id=1, source_target_pairs={{0,1},{1,0},{2,3},{3,2},{4,5},{5,4},{6,7},{7,6},{8,9},{9,8},{10,11... | collective-permute-start | bytes 1572872 | tf_op jit(solution)/shard_map/ppermute | solution.py:471
  97.9 5.9 %collective-permute-start.23 = (bf16[128,2048]{1,0:T(8,128)(2,1)S(1)}, bf16[128,2048]{1,0:T(8,128)(2,1)S(1)}, u32[]{:S(2)}, u32[]{:S(2)}) collective-permute-start(bf16[128,2048]{1,0:T(8,128)(2,1)S(1)} %get-tuple-element.146), channel_id=1, source_target_pairs={{0,1},{1,0},{2,3},{3,2},{4,5},{5,4},{6,7},{7,6},{8,9},{9,8},{10,11... | collective-permute-start | bytes 1572872 | tf_op jit(solution)/shard_map/ppermute | solution.py:471
  103.1 6.4 %collective-permute-start.31 = (bf16[128,1024]{1,0:T(8,128)(2,1)S(1)}, bf16[128,1024]{1,0:T(8,128)(2,1)S(1)}, u32[]{:S(2)}, u32[]{:S(2)}) collective-permute-start(bf16[128,1024]{1,0:T(8,128)(2,1)S(1)} %add.19), channel_id=1, source_target_pairs={{0,4},{2,0},{4,8},{6,2},{8,12},{10,6},{12,14},{14,10},{5,1},{1,3},... | collective-permute-start | bytes 786440 | tf_op jit(solution)/shard_map/ppermute | solution.py:475
  103.9 8.3 %collective-permute-start.36 = (bf16[128,1024]{1,0:T(8,128)(2,1)S(1)}, bf16[128,1024]{1,0:T(8,128)(2,1)S(1)}, u32[]{:S(2)}, u32[]{:S(2)}) collective-permute-start(bf16[128,1024]{1,0:T(8,128)(2,1)S(1)} %add.24), channel_id=1, source_target_pairs={{0,4},{2,0},{4,8},{6,2},{8,12},{10,6},{12,14},{14,10},{5,1},{1,3},... | collective-permute-start | bytes 786440 | tf_op jit(solution)/shard_map/ppermute | solution.py:475
  109.5 6.4 %collective-permute-start.32 = (bf16[128,1024]{1,0:T(8,128)(2,1)S(1)}, bf16[128,1024]{1,0:T(8,128)(2,1)S(1)}, u32[]{:S(2)}, u32[]{:S(2)}) collective-permute-start(bf16[128,1024]{1,0:T(8,128)(2,1)S(1)} %add.20), channel_id=1, source_target_pairs={{0,4},{2,0},{4,8},{6,2},{8,12},{10,6},{12,14},{14,10},{5,1},{1,3},... | collective-permute-start | bytes 786440 | tf_op jit(solution)/shard_map/ppermute | solution.py:475
  112.3 6.4 %collective-permute-start.37 = (bf16[128,1024]{1,0:T(8,128)(2,1)S(1)}, bf16[128,1024]{1,0:T(8,128)(2,1)S(1)}, u32[]{:S(2)}, u32[]{:S(2)}) collective-permute-start(bf16[128,1024]{1,0:T(8,128)(2,1)S(1)} %add.25), channel_id=1, source_target_pairs={{0,4},{2,0},{4,8},{6,2},{8,12},{10,6},{12,14},{14,10},{5,1},{1,3},... | collective-permute-start | bytes 786440 | tf_op jit(solution)/shard_map/ppermute | solution.py:475
  116.1 6.4 %collective-permute-start.33 = (bf16[128,1024]{1,0:T(8,128)(2,1)S(1)}, bf16[128,1024]{1,0:T(8,128)(2,1)S(1)}, u32[]{:S(2)}, u32[]{:S(2)}) collective-permute-start(bf16[128,1024]{1,0:T(8,128)(2,1)S(1)} %add.21), channel_id=1, source_target_pairs={{0,4},{2,0},{4,8},{6,2},{8,12},{10,6},{12,14},{14,10},{5,1},{1,3},... | collective-permute-start | bytes 786440 | tf_op jit(solution)/shard_map/ppermute | solution.py:475
  118.9 9.0 %collective-permute-start.38 = (bf16[128,1024]{1,0:T(8,128)(2,1)S(1)}, bf16[128,1024]{1,0:T(8,128)(2,1)S(1)}, u32[]{:S(2)}, u32[]{:S(2)}) collective-permute-start(bf16[128,1024]{1,0:T(8,128)(2,1)S(1)} %add.26), channel_id=1, source_target_pairs={{0,4},{2,0},{4,8},{6,2},{8,12},{10,6},{12,14},{14,10},{5,1},{1,3},... | collective-permute-start | bytes 786440 | tf_op jit(solution)/shard_map/ppermute | solution.py:532
  122.6 6.4 %collective-permute-start.34 = (bf16[128,1024]{1,0:T(8,128)(2,1)S(1)}, bf16[128,1024]{1,0:T(8,128)(2,1)S(1)}, u32[]{:S(2)}, u32[]{:S(2)}) collective-permute-start(bf16[128,1024]{1,0:T(8,128)(2,1)S(1)} %add.22.after_ref), channel_id=1, source_target_pairs={{0,4},{2,0},{4,8},{6,2},{8,12},{10,6},{12,14},{14,10},{5,1},{1,3},... | collective-permute-start | bytes 786440 | tf_op jit(solution)/shard_map/ppermute | solution.py:532

commit v2 on v1

--- a/solution.py
+++ b/solution.py
@@ -433,8 +433,7 @@
 
     payload = pack(grad_out, routing, gates, scales, groups)
     tiles = -(-saved_gate.shape[1] // LANES)
-    *factors, token = prep(ids, saved_gate[0], saved_up[0], capacity, (0, SPLIT))
-    wdown, _ = hold(w_down[0], token)
+    wdown, _ = hold(w_down[0], payload, ids)
 
     tie = lax.optimization_barrier
     rows, others = {0: payload}, {}
@@ -459,12 +458,13 @@
         return every
 
     def trade(stage):
-        theirs[stage] = mark(lax.ppermute(partial[stage], "dp", swap), 10.0)
-
-    def give(stage):
+        theirs[stage] = lax.ppermute(partial[stage], "dp", swap)
+
+    def give(stage, marked=False):
         first = 2 * steps.index(stage[0])
+        there = theirs[stage] if marked else mark(theirs[stage], 10.0)
         parts = give_rows(
-            first, partial[stage], theirs[stage], to_gate, to_up, *held, leads[stage]
+            first, partial[stage], there, to_gate, to_up, *held, leads[stage]
         )
         for i, s in enumerate(stage):
             own[s] = parts[2 * i]
@@ -472,7 +472,10 @@
 
     def collect(s, before):
         received = [] if before is None else totals[before]
-        received = [mark(lax.ppermute(part, "expert", ring), 8.0) for part in received]
+        estimate = 8.0 if s <= HALVES else 1.0
+        received = [mark(lax.ppermute(part, "expert", ring), estimate) for part in received]
+        if s == HALVES:
+            received = [mark(part, 8.0) for part in received]
         pieces = 2 if s >= HALVES else 1
         width = dcols // pieces
         totals[s] = []
@@ -490,7 +493,9 @@
     pass_on(stages[0])
     share(last)
     every = take(last)
-    trade(last)
+    ids, partial[last] = tie((ids, partial[last]))
+    *factors, token = prep(ids, saved_gate[0], saved_up[0], capacity, (0, SPLIT))
+    rows[1], early = tie((rows[1], token))
     after(rows, stages[0], partial, last)
     before = last
     for i, stage in enumerate(stages):
@@ -505,7 +510,7 @@
             to_gate, to_up, hidden, token = prep(
                 ids, saved_gate[0], saved_up[0], capacity, (SPLIT, tiles), factors
             )
-            wgate, token = hold(w_gate[0], token)
+            wgate, token = hold(w_gate[0], early, token)
             tokens = [token]
             after(rows, stages[1], tokens, 0)
         else:
@@ -513,23 +518,26 @@
                 wup, _ = hold(w_up[0], leads[stage][0], *tokens)
                 held = (wgate, wup)
             after(theirs, [before], partial, stage)
+            if i + 1 == len(stages):
+                grads = [grad_rows(hidden, every, leads[stage][0], 0, [])]
+                after(theirs, [before], grads, 0)
             give(before)
             if not final:
                 after(rows, stages[i + 1], own, before[0])
-            if i == 2:
-                after(theirs, [last], own, before[0])
-                give(last)
-                after(given, [before[0]], own, 0)
             collect(before[0], before[0] - 1 if before[0] > 1 else None)
         before = stage
     after(theirs, [before], totals[before[0] - 1], 0)
+    after(partial, [last], totals[before[0] - 1], 0)
+    trade(last)
     give(before)
-    grads = [grad_rows(hidden, every, own[before[0]], 0, [])]
-    after(given, [before[0]], grads, 0)
     for s in range(before[0], chips):
         collect(s, s - 1)
+        if s == before[0] + 1:
+            after(theirs, [last], totals[s], 1)
+            give(last)
+            after(given, [s + 1], own, 0)
     grads = [grad_rows(hidden, every, totals[chips - 1][0], 1, grads)]
-    received = [mark(lax.ppermute(part, "expert", ring), 8.0) for part in totals[chips - 1]]
+    received = [mark(lax.ppermute(part, "expert", ring), 1.0) for part in totals[chips - 1]]
     grad_x = add(slice(0, dcols), own[0], given[0], received)
     (grad_down,) = grads
     return (grad_x, grad_down[None])

time: 130 us -> 126 us (0.969)
  waiting for transfers between devices: 30.8 us -> 26.4 us
    ppermute x5, waiting for transfers between devices: 4.94 us -> 1.31 us  [trade(): theirs[stage] = lax.ppermute(partial[stage], 'dp', swap)]
    ppermute x9, waiting for transfers between devices: 21.8 us -> 18.7 us  [collect(): lax.ppermute(part, 'expert', ring)]
    ppermute x8, waiting for transfers between devices: 0.02 us -> 2.85 us  [give(): given[s] = lax.ppermute(parts[2 * i + 1], 'expert', sibling)]
    ppermute x4, waiting for transfers between devices: 2.02 us -> 0.52 us  [pass_on(): rows[s] = lax.ppermute(rows[s - 1], 'expert', ring)]
  transfers between devices with their start and end apart: 39 -> 39, of which waited for: 14 -> 17; matrix products, arithmetic and copies ran while one was open for 1% -> 1% of each run, Pallas kernels for 46% -> 51%
where the time goes in v2:
time: 126 us
  Pallas kernels  66.1 us (52%)
  starting transfers between devices  31.5 us (25%)
  waiting for transfers between devices  26.4 us (21%)
    pallas_call x5, Pallas kernels, give_rows(): pl.pallas_call(functools.partial(give_kernel, count, first), in_specs=[VM...  20.6 us
    ppermute x9, waiting for transfers between devices, collect(): lax.ppermute(part, 'expert', ring)  18.7 us
    pallas_call x2, Pallas kernels, prep(): pl.pallas_call(functools.partial(prep_kernel, capacity, tiles[0]), grid_s...  12 us
    pallas_call x5, Pallas kernels, take_rows(): pl.pallas_call(functools.partial(take_kernel, experts, count, first), in_...  11.7 us
    ppermute x9, starting transfers between devices, collect(): lax.ppermute(part, 'expert', ring)  10.5 us
    pallas_call x3, Pallas kernels, hold(): pl.pallas_call(hold_kernel, in_specs=[ANY] * (1 + len(after)), out_specs=...  9.12 us
    pallas_call x2, Pallas kernels, grad_rows(): pl.pallas_call(grad_kernel, grid=(2,), in_specs=[pl.BlockSpec((rows, slot...  8.9 us
    ppermute x5, starting transfers between devices, trade(): theirs[stage] = lax.ppermute(partial[stage], 'dp', swap)  7.73 us
  transfers between devices with their start and end apart: 39, of which 17 were waited for; matrix products, arithmetic and copies ran while one was open for 1% of the time, Pallas kernels for 51%

profile of v2, /device:TPU:0, one launch (start us, length us, event | category | flops | bytes accessed | tf_op | source)
XLA Modules:
  0.0 125.5 jit_solution(16213265655259043283)
XLA Ops:
  0.6 1.3 %pack.1.refs_0_ = bf16[128,2176]{1,0:T(8,128)(2,1)S(1)} custom-call(bf16[128,2048]{1,0:T(8,128)(2,1)} %rows_ref.1, s32[6,128]{1,0:T(8,128)} %bitcast.20, f32[6,128]{1,0:T(8,128)} %bitcast.21, f32[1,128]{1,0:T(1,128)} %bitcast.22), custom_call_target="tpu_custom_call" | custom-call | tf_op jit(solution)/shard_map/pack/pallas_call | solution.py:134
  2.0 0.5 collective-permute-start.1
  2.5 2.6 %collective-permute-start = (bf16[128,2176]{1,0:T(8,128)(2,1)S(1)}, bf16[128,2176]{1,0:T(8,128)(2,1)S(1)}, u32[]{:S(2)}, u32[]{:S(2)}) collective-permute-start(bf16[128,2176]{1,0:T(8,128)(2,1)S(1)} %pack.1.refs_0_), channel_id=1, source_target_pairs={{0,4},{2,0},{4,8},{6,2},{8,12},{10,6},{12,14},{14,10},{5,1},{1,3},... | collective-permute-start | bytes 1671176 | tf_op jit(solution)/shard_map/ppermute | solution.py:445
  5.1 0.7 dynamic-slice_bitcast_fusion.refs_1_.ids_ref
  5.8 3.2 %hold.3 = (bf16[1408,2048]{1,0:T(8,128)(2,1)S(1)}, f32[8,128]{1,0:T(8,128)}) custom-call(bf16[1408,2048]{1,0:T(8,128)(2,1)} %bitcast.17, bf16[128,2176]{1,0:T(8,128)(2,1)S(1)} %pack.1.refs_0_, s32[16]{0:T(128)S(1)} %dynamic-slice_bitcast_fusion.refs_1_.ids_ref), custom_call_target="tpu_custom_call" | custom-call | tf_op jit(solution)/shard_map/hold/pallas_call | solution.py:206
  9.1 2.3 %take.5 = (bf16[896,2048]{1,0:T(8,128)(2,1)S(1)}, bf16[112,1408]{1,0:T(8,128)(2,1)S(1)}, bf16[128,56]{1,0:T(8,128)(2,1)S(1)}, bf16[128,56]{1,0:T(8,128)(2,1)S(1)}) custom-call(s32[1]{0:T(128)} %bitcast.me_ref, bf16[1408,2048]{1,0:T(8,128)(2,1)S(1)} %get-tuple-element.89.wdown_ref, bf16[128,2176]{1,0:T(8,128)(2,1)S(1)} %pack.1.refs_0_, ...), custom_call_target="tpu_custom_call" | custom-call | tf_op jit(solution)/shard_map/take/pallas_call | solution.py:252
  11.3 6.4 %prep.2 = (bf16[896,1408]{1,0:T(8,128)(2,1)S(1)}, bf16[896,1408]{1,0:T(8,128)(2,1)S(1)}, bf16[1408,896]{1,0:T(8,128)(2,1)S(1)}, f32[8,128]{1,0:T(8,128)S(1)}) custom-call(s32[16]{0:T(128)S(1)} %dynamic-slice_bitcast_fusion.refs_1_.ids_ref, bf16[1408,896]{1,0:T(8,128)(2,1)} %bitcast.13, bf16[1408,896]{1,0:T(8,128)(2,1)} %bitcast.15), custom_call_target="tpu_custom_call" | custom-call | flops 6881280 | bytes 6881280 | tf_op jit(solution)/shard_map/prep/pallas_call | solution.py:173
  17.8 0.6 collective-permute-done.2.refs_2_
  18.5 0.4 collective-permute-start.4
  18.9 1.8 %collective-permute-start.6 = (bf16[128,2176]{1,0:T(8,128)(2,1)S(1)}, bf16[128,2176]{1,0:T(8,128)(2,1)S(1)}, u32[]{:S(2)}, u32[]{:S(2)}) collective-permute-start(bf16[128,2176]{1,0:T(8,128)(2,1)S(1)} %collective-permute-done.refs_0_), channel_id=1, source_target_pairs={{0,4},{2,0},{4,8},{6,2},{8,12},{10,6},{12,14},{14,10},{5,1},{1,3},... | collective-permute-start | bytes 1671176 | tf_op jit(solution)/shard_map/ppermute | solution.py:445
  20.6 0.3 collective-permute-start.7
  21.1 2.4 %take.6 = (bf16[896,2048]{1,0:T(8,128)(2,1)S(1)}, bf16[224,1408]{1,0:T(8,128)(2,1)S(1)}, bf16[128,56]{1,0:T(8,128)(2,1)S(1)}, bf16[128,56]{1,0:T(8,128)(2,1)S(1)...) custom-call(s32[1]{0:T(128)} %bitcast.me_ref, ...), custom_call_target="tpu_custom_call", output_to_operand_aliasing={{0}: (6, {})} | custom-call | tf_op jit(solution)/shard_map/take/pallas_call | solution.py:252
  23.5 1.7 %collective-permute-start.5 = (bf16[224,1408]{1,0:T(8,128)(2,1)S(1)}, bf16[224,1408]{1,0:T(8,128)(2,1)S(1)}, u32[]{:S(2)}, u32[]{:S(2)}) collective-permute-start(bf16[224,1408]{1,0:T(8,128)(2,1)S(1)} %get-tuple-element.111.mine_ref), channel_id=1, source_target_pairs={{0,16},{16,0},{1,17},{17,1},{2,18},{18,2},{3,19},{19,3},{4,20},{20... | collective-permute-start | bytes 1892360 | tf_op jit(solution)/shard_map/ppermute | solution.py:461
  25.2 5.6 %prep.3 = (bf16[896,1408]{1,0:T(8,128)(2,1)S(1)}, bf16[896,1408]{1,0:T(8,128)(2,1)S(1)}, bf16[1408,896]{1,0:T(8,128)(2,1)S(1)}, f32[8,128]{1,0:T(8,128)S(1)}) custom-call(s32[16]{0:T(128)S(1)} %dynamic-slice_bitcast_fusion.refs_1_.ids_ref, bf16[1408,896]{1,0:T(8,128)(2,1)} %bitcast.14, ...), custom_call_target="tpu_custom_call", output_to_operand_aliasing={{0}: (3, {}), {1}: (4, {}), {2}: (5, {})} | custom-call | flops 5734400 | bytes 5734400 | tf_op jit(solution)/shard_map/prep/pallas_call | solution.py:173
  30.9 2.6 %hold.4 = (bf16[2048,1408]{1,0:T(8,128)(2,1)S(1)}, f32[8,128]{1,0:T(8,128)S(1)}) custom-call(bf16[2048,1408]{1,0:T(8,128)(2,1)} %bitcast.18, f32[8,128]{1,0:T(8,128)S(1)} %get-tuple-element.99.refs_0_, f32[8,128]{1,0:T(8,128)S(1)} %get-tuple-element.104.refs_1_), custom_call_target="tpu_custom_call" | custom-call | tf_op jit(solution)/shard_map/hold/pallas_call | solution.py:206
  33.6 0.9 collective-permute-start.8
  34.5 1.5 %collective-permute-start.11 = (bf16[128,2176]{1,0:T(8,128)(2,1)S(1)}, bf16[128,2176]{1,0:T(8,128)(2,1)S(1)}, u32[]{:S(2)}, u32[]{:S(2)}) collective-permute-start(bf16[128,2176]{1,0:T(8,128)(2,1)S(1)} %collective-permute-done.6.refs_0_), channel_id=1, source_target_pairs={{0,4},{2,0},{4,8},{6,2},{8,12},{10,6},{12,14},{14,10},{5,1},{1,3},... | collective-permute-start | bytes 1671176 | tf_op jit(solution)/shard_map/ppermute | solution.py:445
  35.9 0.6 collective-permute-start.12
  36.5 0.3 collective-permute-done.9.refs_3_
  36.9 2.4 %take.7 = (bf16[896,2048]{1,0:T(8,128)(2,1)S(1)}, bf16[224,1408]{1,0:T(8,128)(2,1)S(1)}, bf16[128,56]{1,0:T(8,128)(2,1)S(1)}, bf16[128,56]{1,0:T(8,128)(2,1)S(1)...) custom-call(s32[1]{0:T(128)} %bitcast.me_ref, ...), custom_call_target="tpu_custom_call", output_to_operand_aliasing={{0}: (6, {})} | custom-call | tf_op jit(solution)/shard_map/take/pallas_call | solution.py:252
  39.3 1.7 %collective-permute-start.10 = (bf16[224,1408]{1,0:T(8,128)(2,1)S(1)}, bf16[224,1408]{1,0:T(8,128)(2,1)S(1)}, u32[]{:S(2)}, u32[]{:S(2)}) collective-permute-start(bf16[224,1408]{1,0:T(8,128)(2,1)S(1)} %get-tuple-element.110.mine_ref), channel_id=1, source_target_pairs={{0,16},{16,0},{1,17},{17,1},{2,18},{18,2},{3,19},{19,3},{4,20},{20... | collective-permute-start | bytes 1892360 | tf_op jit(solution)/shard_map/ppermute | solution.py:461
  41.0 3.2 %hold.5 = (bf16[2048,1408]{1,0:T(8,128)(2,1)S(1)}, f32[8,128]{1,0:T(8,128)}) custom-call(bf16[2048,1408]{1,0:T(8,128)(2,1)} %bitcast.19, bf16[128,56]{1,0:T(8,128)(2,1)S(1)} %get-tuple-element.116.refs_0_, f32[8,128]{1,0:T(8,128)S(1)} %get-tuple-element.117.refs_1_), custom_call_target="tpu_custom_call" | custom-call | tf_op jit(solution)/shard_map/hold/pallas_call | solution.py:206
  44.3 4.3 %give.5 = (bf16[128,2048]{1,0:T(8,128)(2,1)S(1)}, bf16[128,2048]{1,0:T(8,128)(2,1)S(1)}, bf16[128,2048]{1,0:T(8,128)(2,1)S(1)}, bf16[128,2048]{1,0:T(8,128)(2,1)S(1)}) custom-call(bf16[224,1408]{1,0:T(8,128)(2,1)S(1)} %get-tuple-element.111.mine_ref, bf16[224,1408]{1,0:T(8,128)(2,1)S(1)} %mark.17.theirs_ref, ...), custom_call_target="tpu_custom_call" | custom-call | tf_op jit(solution)/shard_map/give/pallas_call | solution.py:292
  48.6 0.5 collective-permute-done.11.refs_0_
  49.0 0.5 collective-permute-done.12.refs_2_
  49.5 0.6 collective-permute-start.13
  50.1 0.5 collective-permute-start.22
  50.6 1.2 collective-permute-start.16
  51.8 1.4 %collective-permute-done.22.given_ref = bf16[128,2048]{1,0:T(8,128)(2,1)S(1)} collective-permute-done((bf16[128,2048]{1,0:T(8,128)(2,1)S(1)}, bf16[128,2048]{1,0:T(8,128)(2,1)S(1)}, u32[]{:S(2)}, u32[]{:S(2)}) %collective-permute-start.22) | collective-permute-done | bytes 524320 | tf_op jit(solution)/shard_map/ppermute | solution.py:471
  53.4 1.8 %collective-permute-start.23 = (bf16[128,2048]{1,0:T(8,128)(2,1)S(1)}, bf16[128,2048]{1,0:T(8,128)(2,1)S(1)}, u32[]{:S(2)}, u32[]{:S(2)}) collective-permute-start(bf16[128,2048]{1,0:T(8,128)(2,1)S(1)} %add.16), channel_id=1, source_target_pairs={{0,4},{2,0},{4,8},{6,2},{8,12},{10,6},{12,14},{14,10},{5,1},{1,3},... | collective-permute-start | bytes 1572872 | tf_op jit(solution)/shard_map/ppermute | solution.py:476
  55.1 2.4 %take.8 = (bf16[896,2048]{1,0:T(8,128)(2,1)S(1)}, bf16[224,1408]{1,0:T(8,128)(2,1)S(1)}, bf16[128,56]{1,0:T(8,128)(2,1)S(1)}, bf16[128,56]{1,0:T(8,128)(2,1)S(1)...) custom-call(s32[1]{0:T(128)} %bitcast.me_ref, ...), custom_call_target="tpu_custom_call", output_to_operand_aliasing={{0}: (6, {})} | custom-call | tf_op jit(solution)/shard_map/take/pallas_call | solution.py:252
  57.6 1.7 %collective-permute-start.19 = (bf16[224,1408]{1,0:T(8,128)(2,1)S(1)}, bf16[224,1408]{1,0:T(8,128)(2,1)S(1)}, u32[]{:S(2)}, u32[]{:S(2)}) collective-permute-start(bf16[224,1408]{1,0:T(8,128)(2,1)S(1)} %get-tuple-element.138.mine_ref), channel_id=1, source_target_pairs={{0,16},{16,0},{1,17},{17,1},{2,18},{18,2},{3,19},{19,3},{4,20},{20... | collective-permute-start | bytes 1892360 | tf_op jit(solution)/shard_map/ppermute | solution.py:461
  59.3 4.3 %give.6 = (bf16[128,2048]{1,0:T(8,128)(2,1)S(1)}, bf16[128,2048]{1,0:T(8,128)(2,1)S(1)}, bf16[128,2048]{1,0:T(8,128)(2,1)S(1)}, bf16[128,2048]{1,0:T(8,128)(2,1)S(1)}) custom-call(bf16[224,1408]{1,0:T(8,128)(2,1)S(1)} %get-tuple-element.110.mine_ref, bf16[224,1408]{1,0:T(8,128)(2,1)S(1)} %mark.18.theirs_ref, ...), custom_call_target="tpu_custom_call" | custom-call | tf_op jit(solution)/shard_map/give/pallas_call | solution.py:292
  63.6 0.5 collective-permute-start.17
  64.1 1.6 %collective-permute-done.23.old_ref = bf16[128,2048]{1,0:T(8,128)(2,1)S(1)} collective-permute-done((bf16[128,2048]{1,0:T(8,128)(2,1)S(1)}, bf16[128,2048]{1,0:T(8,128)(2,1)S(1)}, u32[]{:S(2)}, u32[]{:S(2)}) %collective-permute-start.23) | collective-permute-done | bytes 524320 | tf_op jit(solution)/shard_map/ppermute | solution.py:476
  66.0 1.2 collective-permute-start.24
  67.2 2.2 %take.9 = (bf16[896,2048]{1,0:T(8,128)(2,1)S(1)}, bf16[112,1408]{1,0:T(8,128)(2,1)S(1)}, bf16[128,56]{1,0:T(8,128)(2,1)S(1)}, bf16[128,56]{1,0:T(8,128)(2,1)S(1)}) custom-call(s32[1]{0:T(128)} %bitcast.me_ref, bf16[1408,2048]{1,0:T(8,128)(2,1)S(1)} %get-tuple-element.89.wdown_ref, ...), custom_call_target="tpu_custom_call", output_to_operand_aliasing={{0}: (4, {})} | custom-call | tf_op jit(solution)/shard_map/take/pallas_call | solution.py:252
  69.4 1.7 %collective-permute-start.18 = (bf16[112,1408]{1,0:T(8,128)(2,1)S(1)}, bf16[112,1408]{1,0:T(8,128)(2,1)S(1)}, u32[]{:S(2)}, u32[]{:S(2)}) collective-permute-start(bf16[112,1408]{1,0:T(8,128)(2,1)S(1)} %get-tuple-element.158.mine_ref), channel_id=1, source_target_pairs={{0,16},{16,0},{1,17},{17,1},{2,18},{18,2},{3,19},{19,3},{4,20},{20... | collective-permute-start | bytes 946184 | tf_op jit(solution)/shard_map/ppermute | solution.py:461
  71.2 4.4 %grad_down.2.refs_0_ = bf16[1408,2048]{1,0:T(8,128)(2,1)} custom-call(bf16[1408,896]{1,0:T(8,128)(2,1)S(1)} %get-tuple-element.140.hidden_ref, bf16[896,2048]{1,0:T(8,128)(2,1)S(1)} %get-tuple-element.141.every_ref, bf16[128,56]{1,0:T(8,128)(2,1)S(1)} %get-tuple-element.142.after_ref.refs_0_), custom_call_target="tpu_custom_call" | custom-call | tf_op jit(solution)/shard_map/grad_down/pallas_call | solution.py:336
  75.6 4.3 %give.7 = (bf16[128,2048]{1,0:T(8,128)(2,1)S(1)}, bf16[128,2048]{1,0:T(8,128)(2,1)S(1)}, bf16[128,2048]{1,0:T(8,128)(2,1)S(1)}, bf16[128,2048]{1,0:T(8,128)(2,1)S(1)}) custom-call(bf16[224,1408]{1,0:T(8,128)(2,1)S(1)} %get-tuple-element.138.mine_ref, bf16[224,1408]{1,0:T(8,128)(2,1)S(1)} %mark.19.theirs_ref, ...), custom_call_target="tpu_custom_call" | custom-call | tf_op jit(solution)/shard_map/give/pallas_call | solution.py:292
  80.0 0.5 collective-permute-start.26
  80.5 1.4 %collective-permute-done.20.given_ref = bf16[128,2048]{1,0:T(8,128)(2,1)S(1)} collective-permute-done((bf16[128,2048]{1,0:T(8,128)(2,1)S(1)}, bf16[128,2048]{1,0:T(8,128)(2,1)S(1)}, u32[]{:S(2)}, u32[]{:S(2)}) %collective-permute-start.20) | collective-permute-done | bytes 524320 | tf_op jit(solution)/shard_map/ppermute | solution.py:471
  82.1 1.3 %collective-permute-start.28 = (bf16[128,2048]{1,0:T(8,128)(2,1)S(1)}, bf16[128,2048]{1,0:T(8,128)(2,1)S(1)}, u32[]{:S(2)}, u32[]{:S(2)}) collective-permute-start(bf16[128,2048]{1,0:T(8,128)(2,1)S(1)} %add.18), channel_id=1, source_target_pairs={{0,4},{2,0},{4,8},{6,2},{8,12},{10,6},{12,14},{14,10},{5,1},{1,3},... | collective-permute-start | bytes 1572872 | tf_op jit(solution)/shard_map/ppermute | solution.py:476
  83.4 3.9 %give.8 = (bf16[128,2048]{1,0:T(8,128)(2,1)S(1)}, bf16[128,2048]{1,0:T(8,128)(2,1)S(1)}) custom-call(bf16[112,1408]{1,0:T(8,128)(2,1)S(1)} %get-tuple-element.158.mine_ref, bf16[112,1408]{1,0:T(8,128)(2,1)S(1)} %mark.22.theirs_ref, bf16[896,1408]{1,0:T(8,128)(2,1)S(1)} %get-tuple-element.113.to_gate_ref, bf16[896,1408]{1,0:T(8,128)(2,1)S(1)} %get-tuple-element.114.to_up_ref, ...), custom_call_target="tpu_custom_call" | custom-call | tf_op jit(solution)/shard_map/give/pallas_call | solution.py:292
  87.4 4.2 %collective-permute-done.28.old_ref = bf16[128,2048]{1,0:T(8,128)(2,1)S(1)} collective-permute-done((bf16[128,2048]{1,0:T(8,128)(2,1)S(1)}, bf16[128,2048]{1,0:T(8,128)(2,1)S(1)}, u32[]{:S(2)}, u32[]{:S(2)}) %collective-permute-start.28) | collective-permute-done | bytes 524320 | tf_op jit(solution)/shard_map/ppermute | solution.py:476
  91.7 1.1 collective-permute-start.32
  92.8 1.5 %collective-permute-start.29 = (bf16[128,1024]{1,0:T(8,128)(2,1)S(1)}, bf16[128,1024]{1,0:T(8,128)(2,1)S(1)}, u32[]{:S(2)}, u32[]{:S(2)}) collective-permute-start(bf16[128,1024]{1,0:T(8,128)(2,1)S(1)} %add.19), channel_id=1, source_target_pairs={{0,4},{2,0},{4,8},{6,2},{8,12},{10,6},{12,14},{14,10},{5,1},{1,3},... | collective-permute-start | bytes 786440 | tf_op jit(solution)/shard_map/ppermute | solution.py:476
  94.3 0.8 collective-permute-start.25
  95.1 3.0 %collective-permute-done.32.old_ref = bf16[128,1024]{1,0:T(8,128)(2,1)S(1)} collective-permute-done((bf16[128,1024]{1,0:T(8,128)(2,1)S(1)}, bf16[128,1024]{1,0:T(8,128)(2,1)S(1)}, u32[]{:S(2)}, u32[]{:S(2)}) %collective-permute-start.32) | collective-permute-done | bytes 262176 | tf_op jit(solution)/shard_map/ppermute | solution.py:476
  98.2 1.1 collective-permute-start.33
  99.3 1.6 %collective-permute-done.29.old_ref = bf16[128,1024]{1,0:T(8,128)(2,1)S(1)} collective-permute-done((bf16[128,1024]{1,0:T(8,128)(2,1)S(1)}, bf16[128,1024]{1,0:T(8,128)(2,1)S(1)}, u32[]{:S(2)}, u32[]{:S(2)}) %collective-permute-start.29) | collective-permute-done | bytes 262176 | tf_op jit(solution)/shard_map/ppermute | solution.py:476
  101.0 1.3 %collective-permute-done.25.old_ref = bf16[112,1408]{1,0:T(8,128)(2,1)S(1)} collective-permute-done((bf16[112,1408]{1,0:T(8,128)(2,1)S(1)}, bf16[112,1408]{1,0:T(8,128)(2,1)S(1)}, u32[]{:S(2)}, u32[]{:S(2)}) %collective-permute-start.25) | collective-permute-done | bytes 315424 | tf_op jit(solution)/shard_map/ppermute | solution.py:461
  102.3 0.5 collective-permute-start.36
  102.8 3.9 %give.9 = (bf16[128,2048]{1,0:T(8,128)(2,1)S(1)}, bf16[128,2048]{1,0:T(8,128)(2,1)S(1)}) custom-call(bf16[112,1408]{1,0:T(8,128)(2,1)S(1)} %get-tuple-element.155.mine_ref, bf16[112,1408]{1,0:T(8,128)(2,1)S(1)} %mark.26.theirs_ref, bf16[896,1408]{1,0:T(8,128)(2,1)S(1)} %get-tuple-element.113.to_gate_ref, bf16[896,1408]{1,0:T(8,128)(2,1)S(1)} %get-tuple-element.114.to_up_ref, ...), custom_call_target="tpu_custom_call" | custom-call | tf_op jit(solution)/shard_map/give/pallas_call | solution.py:292
  106.7 1.9 %collective-permute-done.36.old_ref = bf16[128,1024]{1,0:T(8,128)(2,1)S(1)} collective-permute-done((bf16[128,1024]{1,0:T(8,128)(2,1)S(1)}, bf16[128,1024]{1,0:T(8,128)(2,1)S(1)}, u32[]{:S(2)}, u32[]{:S(2)}) %collective-permute-start.36) | collective-permute-done | bytes 262176 | tf_op jit(solution)/shard_map/ppermute | solution.py:476
  108.8 0.6 collective-permute-start.37
  109.4 1.6 %collective-permute-start.34 = (bf16[128,1024]{1,0:T(8,128)(2,1)S(1)}, bf16[128,1024]{1,0:T(8,128)(2,1)S(1)}, u32[]{:S(2)}, u32[]{:S(2)}) collective-permute-start(bf16[128,1024]{1,0:T(8,128)(2,1)S(1)} %add.23), channel_id=1, source_target_pairs={{0,4},{2,0},{4,8},{6,2},{8,12},{10,6},{12,14},{14,10},{5,1},{1,3},... | collective-permute-start | bytes 786440 | tf_op jit(solution)/shard_map/ppermute | solution.py:476
  111.0 4.2 %collective-permute-done.37.old_ref = bf16[128,1024]{1,0:T(8,128)(2,1)S(1)} collective-permute-done((bf16[128,1024]{1,0:T(8,128)(2,1)S(1)}, bf16[128,1024]{1,0:T(8,128)(2,1)S(1)}, u32[]{:S(2)}, u32[]{:S(2)}) %collective-permute-start.37) | collective-permute-done | bytes 262176 | tf_op jit(solution)/shard_map/ppermute | solution.py:476
  115.3 0.6 collective-permute-start.38
  115.9 2.1 %collective-permute-done.34.old_ref = bf16[128,1024]{1,0:T(8,128)(2,1)S(1)} collective-permute-done((bf16[128,1024]{1,0:T(8,128)(2,1)S(1)}, bf16[128,1024]{1,0:T(8,128)(2,1)S(1)}, u32[]{:S(2)}, u32[]{:S(2)}) %collective-permute-start.34) | collective-permute-done | bytes 262176 | tf_op jit(solution)/shard_map/ppermute | solution.py:476
  118.1 0.6 collective-permute-start.35
  118.7 4.4 %grad_down.3 = bf16[1408,2048]{1,0:T(8,128)(2,1)} custom-call(bf16[1408,896]{1,0:T(8,128)(2,1)S(1)} %get-tuple-element.140.hidden_ref, bf16[896,2048]{1,0:T(8,128)(2,1)S(1)} %get-tuple-element.141.every_ref, bf16[128,1024]{1,0:T(8,128)(2,1)S(1)} %add.24.after_ref, bf16[1408,2048]{1,0:T(8,128)(2,1)} %grad_down.2.refs_0_), custom_call_target="tpu_custom_call", output_to_operand_aliasing={{}: (3, {})} | custom-call | tf_op jit(solution)/shard_map/grad_down/pallas_call | solution.py:336
  123.1 1.4 %collective-permute-done.35.old_ref = bf16[128,1024]{1,0:T(8,128)(2,1)S(1)} collective-permute-done((bf16[128,1024]{1,0:T(8,128)(2,1)S(1)}, bf16[128,1024]{1,0:T(8,128)(2,1)S(1)}, u32[]{:S(2)}, u32[]{:S(2)}) %collective-permute-start.35) | collective-permute-done | bytes 262176 | tf_op jit(solution)/shard_map/ppermute | solution.py:540
  124.5 1.0 add.27
  (62 shorter events, 2.0 us)
Async XLA Ops:
  2.0 7.1 %collective-permute-start.1 = (bf16[128,2176]{1,0:T(8,128)(2,1)S(1)}, bf16[128,2176]{1,0:T(8,128)(2,1)S(1)}, u32[]{:S(2)}, u32[]{:S(2)}) collective-permute-start(bf16[128,2176]{1,0:T(8,128)(2,1)S(1)} %pack.1.refs_0_), channel_id=1, source_target_pairs={{0,1},{1,0},{2,3},{3,2},{4,5},{5,4},{6,7},{7,6},{8,9},{9,8},{10,11... | collective-permute-start | bytes 1671176 | tf_op jit(solution)/shard_map/ppermute | solution.py:451
  2.5 15.3 %collective-permute-start = (bf16[128,2176]{1,0:T(8,128)(2,1)S(1)}, bf16[128,2176]{1,0:T(8,128)(2,1)S(1)}, u32[]{:S(2)}, u32[]{:S(2)}) collective-permute-start(bf16[128,2176]{1,0:T(8,128)(2,1)S(1)} %pack.1.refs_0_), channel_id=1, source_target_pairs={{0,4},{2,0},{4,8},{6,2},{8,12},{10,6},{12,14},{14,10},{5,1},{1,3},... | collective-permute-start | bytes 1671176 | tf_op jit(solution)/shard_map/ppermute | solution.py:445
  5.1 13.2 %collective-permute-start.2 = (bf16[128,2176]{1,0:T(8,128)(2,1)S(1)}, bf16[128,2176]{1,0:T(8,128)(2,1)S(1)}, u32[]{:S(2)}, u32[]{:S(2)}) collective-permute-start(bf16[128,2176]{1,0:T(8,128)(2,1)S(1)} %pack.1.refs_0_), channel_id=1, source_target_pairs={{4,0},{0,2},{8,4},{2,6},{12,8},{6,10},{14,12},{10,14},{1,5},{3,1},... | collective-permute-start | bytes 1671176 | tf_op jit(solution)/shard_map/ppermute | solution.py:447
  18.4 2.5 %collective-permute-start.3 = (bf16[128,2176]{1,0:T(8,128)(2,1)S(1)}, bf16[128,2176]{1,0:T(8,128)(2,1)S(1)}, u32[]{:S(2)}, u32[]{:S(2)}) collective-permute-start(bf16[128,2176]{1,0:T(8,128)(2,1)S(1)} %collective-permute-done.refs_0_), channel_id=1, source_target_pairs={{0,1},{1,0},{2,3},{3,2},{4,5},{5,4},{6,7},{7,6},{8,9},{9,8},{10,11... | collective-permute-start | bytes 1671176 | tf_op jit(solution)/shard_map/ppermute | solution.py:451
  18.5 2.6 %collective-permute-start.4 = (bf16[128,2176]{1,0:T(8,128)(2,1)S(1)}, bf16[128,2176]{1,0:T(8,128)(2,1)S(1)}, u32[]{:S(2)}, u32[]{:S(2)}) collective-permute-start(bf16[128,2176]{1,0:T(8,128)(2,1)S(1)} %collective-permute-done.2.refs_2_), channel_id=1, source_target_pairs={{0,1},{1,0},{2,3},{3,2},{4,5},{5,4},{6,7},{7,6},{8,9},{9,8},{10,11... | collective-permute-start | bytes 1671176 | tf_op jit(solution)/shard_map/ppermute | solution.py:451
  18.9 14.7 %collective-permute-start.6 = (bf16[128,2176]{1,0:T(8,128)(2,1)S(1)}, bf16[128,2176]{1,0:T(8,128)(2,1)S(1)}, u32[]{:S(2)}, u32[]{:S(2)}) collective-permute-start(bf16[128,2176]{1,0:T(8,128)(2,1)S(1)} %collective-permute-done.refs_0_), channel_id=1, source_target_pairs={{0,4},{2,0},{4,8},{6,2},{8,12},{10,6},{12,14},{14,10},{5,1},{1,3},... | collective-permute-start | bytes 1671176 | tf_op jit(solution)/shard_map/ppermute | solution.py:445
  20.6 13.0 %collective-permute-start.7 = (bf16[128,2176]{1,0:T(8,128)(2,1)S(1)}, bf16[128,2176]{1,0:T(8,128)(2,1)S(1)}, u32[]{:S(2)}, u32[]{:S(2)}) collective-permute-start(bf16[128,2176]{1,0:T(8,128)(2,1)S(1)} %collective-permute-done.2.refs_2_), channel_id=1, source_target_pairs={{4,0},{0,2},{8,4},{2,6},{12,8},{6,10},{14,12},{10,14},{1,5},{3,1},... | collective-permute-start | bytes 1671176 | tf_op jit(solution)/shard_map/ppermute | solution.py:447
  23.5 20.8 %collective-permute-start.5 = (bf16[224,1408]{1,0:T(8,128)(2,1)S(1)}, bf16[224,1408]{1,0:T(8,128)(2,1)S(1)}, u32[]{:S(2)}, u32[]{:S(2)}) collective-permute-start(bf16[224,1408]{1,0:T(8,128)(2,1)S(1)} %get-tuple-element.111.mine_ref), channel_id=1, source_target_pairs={{0,16},{16,0},{1,17},{17,1},{2,18},{18,2},{3,19},{19,3},{4,20},{20... | collective-permute-start | bytes 1892360 | tf_op jit(solution)/shard_map/ppermute | solution.py:461
  33.6 2.9 %collective-permute-start.8 = (bf16[128,2176]{1,0:T(8,128)(2,1)S(1)}, bf16[128,2176]{1,0:T(8,128)(2,1)S(1)}, u32[]{:S(2)}, u32[]{:S(2)}) collective-permute-start(bf16[128,2176]{1,0:T(8,128)(2,1)S(1)} %collective-permute-done.6.refs_0_), channel_id=1, source_target_pairs={{0,1},{1,0},{2,3},{3,2},{4,5},{5,4},{6,7},{7,6},{8,9},{9,8},{10,11... | collective-permute-start | bytes 1671176 | tf_op jit(solution)/shard_map/ppermute | solution.py:451
  34.5 2.4 %collective-permute-start.9 = (bf16[128,2176]{1,0:T(8,128)(2,1)S(1)}, bf16[128,2176]{1,0:T(8,128)(2,1)S(1)}, u32[]{:S(2)}, u32[]{:S(2)}) collective-permute-start(bf16[128,2176]{1,0:T(8,128)(2,1)S(1)} %collective-permute-done.7.refs_2_), channel_id=1, source_target_pairs={{0,1},{1,0},{2,3},{3,2},{4,5},{5,4},{6,7},{7,6},{8,9},{9,8},{10,11... | collective-permute-start | bytes 1671176 | tf_op jit(solution)/shard_map/ppermute | solution.py:451
  34.5 14.6 %collective-permute-start.11 = (bf16[128,2176]{1,0:T(8,128)(2,1)S(1)}, bf16[128,2176]{1,0:T(8,128)(2,1)S(1)}, u32[]{:S(2)}, u32[]{:S(2)}) collective-permute-start(bf16[128,2176]{1,0:T(8,128)(2,1)S(1)} %collective-permute-done.6.refs_0_), channel_id=1, source_target_pairs={{0,4},{2,0},{4,8},{6,2},{8,12},{10,6},{12,14},{14,10},{5,1},{1,3},... | collective-permute-start | bytes 1671176 | tf_op jit(solution)/shard_map/ppermute | solution.py:445
  35.9 13.6 %collective-permute-start.12 = (bf16[128,2176]{1,0:T(8,128)(2,1)S(1)}, bf16[128,2176]{1,0:T(8,128)(2,1)S(1)}, u32[]{:S(2)}, u32[]{:S(2)}) collective-permute-start(bf16[128,2176]{1,0:T(8,128)(2,1)S(1)} %collective-permute-done.7.refs_2_), channel_id=1, source_target_pairs={{4,0},{0,2},{8,4},{2,6},{12,8},{6,10},{14,12},{10,14},{1,5},{3,1},... | collective-permute-start | bytes 1671176 | tf_op jit(solution)/shard_map/ppermute | solution.py:447
  39.3 20.0 %collective-permute-start.10 = (bf16[224,1408]{1,0:T(8,128)(2,1)S(1)}, bf16[224,1408]{1,0:T(8,128)(2,1)S(1)}, u32[]{:S(2)}, u32[]{:S(2)}) collective-permute-start(bf16[224,1408]{1,0:T(8,128)(2,1)S(1)} %get-tuple-element.110.mine_ref), channel_id=1, source_target_pairs={{0,16},{16,0},{1,17},{17,1},{2,18},{18,2},{3,19},{19,3},{4,20},{20... | collective-permute-start | bytes 1892360 | tf_op jit(solution)/shard_map/ppermute | solution.py:461
  49.5 5.6 %collective-permute-start.13 = (bf16[128,2176]{1,0:T(8,128)(2,1)S(1)}, bf16[128,2176]{1,0:T(8,128)(2,1)S(1)}, u32[]{:S(2)}, u32[]{:S(2)}) collective-permute-start(bf16[128,2176]{1,0:T(8,128)(2,1)S(1)} %collective-permute-done.11.refs_0_), channel_id=1, source_target_pairs={{0,1},{1,0},{2,3},{3,2},{4,5},{5,4},{6,7},{7,6},{8,9},{9,8},{10,11... | collective-permute-start | bytes 1671176 | tf_op jit(solution)/shard_map/ppermute | solution.py:451
  50.1 5.0 %collective-permute-start.14 = (bf16[128,2176]{1,0:T(8,128)(2,1)S(1)}, bf16[128,2176]{1,0:T(8,128)(2,1)S(1)}, u32[]{:S(2)}, u32[]{:S(2)}) collective-permute-start(bf16[128,2176]{1,0:T(8,128)(2,1)S(1)} %collective-permute-done.12.refs_2_), channel_id=1, source_target_pairs={{0,1},{1,0},{2,3},{3,2},{4,5},{5,4},{6,7},{7,6},{8,9},{9,8},{10,11... | collective-permute-start | bytes 1671176 | tf_op jit(solution)/shard_map/ppermute | solution.py:451
  50.1 3.1 %collective-permute-start.22 = (bf16[128,2048]{1,0:T(8,128)(2,1)S(1)}, bf16[128,2048]{1,0:T(8,128)(2,1)S(1)}, u32[]{:S(2)}, u32[]{:S(2)}) collective-permute-start(bf16[128,2048]{1,0:T(8,128)(2,1)S(1)} %get-tuple-element.153), channel_id=1, source_target_pairs={{0,1},{1,0},{2,3},{3,2},{4,5},{5,4},{6,7},{7,6},{8,9},{9,8},{10,11... | collective-permute-start | bytes 1572872 | tf_op jit(solution)/shard_map/ppermute | solution.py:471
  50.6 12.9 %collective-permute-start.16 = (bf16[128,2176]{1,0:T(8,128)(2,1)S(1)}, bf16[128,2176]{1,0:T(8,128)(2,1)S(1)}, u32[]{:S(2)}, u32[]{:S(2)}) collective-permute-start(bf16[128,2176]{1,0:T(8,128)(2,1)S(1)} %collective-permute-done.11.refs_0_), channel_id=1, source_target_pairs={{0,4},{2,0},{4,8},{6,2},{8,12},{10,6},{12,14},{14,10},{5,1},{1,3},... | collective-permute-start | bytes 1671176 | tf_op jit(solution)/shard_map/ppermute | solution.py:445
  53.4 12.4 %collective-permute-start.23 = (bf16[128,2048]{1,0:T(8,128)(2,1)S(1)}, bf16[128,2048]{1,0:T(8,128)(2,1)S(1)}, u32[]{:S(2)}, u32[]{:S(2)}) collective-permute-start(bf16[128,2048]{1,0:T(8,128)(2,1)S(1)} %add.16), channel_id=1, source_target_pairs={{0,4},{2,0},{4,8},{6,2},{8,12},{10,6},{12,14},{14,10},{5,1},{1,3},... | collective-permute-start | bytes 1572872 | tf_op jit(solution)/shard_map/ppermute | solution.py:476
  57.6 18.1 %collective-permute-start.19 = (bf16[224,1408]{1,0:T(8,128)(2,1)S(1)}, bf16[224,1408]{1,0:T(8,128)(2,1)S(1)}, u32[]{:S(2)}, u32[]{:S(2)}) collective-permute-start(bf16[224,1408]{1,0:T(8,128)(2,1)S(1)} %get-tuple-element.138.mine_ref), channel_id=1, source_target_pairs={{0,16},{16,0},{1,17},{17,1},{2,18},{18,2},{3,19},{19,3},{4,20},{20... | collective-permute-start | bytes 1892360 | tf_op jit(solution)/shard_map/ppermute | solution.py:461
  63.6 2.2 %collective-permute-start.21 = (bf16[128,2048]{1,0:T(8,128)(2,1)S(1)}, bf16[128,2048]{1,0:T(8,128)(2,1)S(1)}, u32[]{:S(2)}, u32[]{:S(2)}) collective-permute-start(bf16[128,2048]{1,0:T(8,128)(2,1)S(1)} %get-tuple-element.151), channel_id=1, source_target_pairs={{0,1},{1,0},{2,3},{3,2},{4,5},{5,4},{6,7},{7,6},{8,9},{9,8},{10,11... | collective-permute-start | bytes 1572872 | tf_op jit(solution)/shard_map/ppermute | solution.py:471
  63.6 3.5 %collective-permute-start.17 = (bf16[128,2176]{1,0:T(8,128)(2,1)S(1)}, bf16[128,2176]{1,0:T(8,128)(2,1)S(1)}, u32[]{:S(2)}, u32[]{:S(2)}) collective-permute-start(bf16[128,2176]{1,0:T(8,128)(2,1)S(1)} %collective-permute-done.16.refs_0_), channel_id=1, source_target_pairs={{0,1},{1,0},{2,3},{3,2},{4,5},{5,4},{6,7},{7,6},{8,9},{9,8},{10,11... | collective-permute-start | bytes 1671176 | tf_op jit(solution)/shard_map/ppermute | solution.py:451
  66.0 14.5 %collective-permute-start.24 = (bf16[128,2048]{1,0:T(8,128)(2,1)S(1)}, bf16[128,2048]{1,0:T(8,128)(2,1)S(1)}, u32[]{:S(2)}, u32[]{:S(2)}) collective-permute-start(bf16[128,2048]{1,0:T(8,128)(2,1)S(1)} %add.17), channel_id=1, source_target_pairs={{0,4},{2,0},{4,8},{6,2},{8,12},{10,6},{12,14},{14,10},{5,1},{1,3},... | collective-permute-start | bytes 1572872 | tf_op jit(solution)/shard_map/ppermute | solution.py:476
  69.4 12.7 %collective-permute-start.18 = (bf16[112,1408]{1,0:T(8,128)(2,1)S(1)}, bf16[112,1408]{1,0:T(8,128)(2,1)S(1)}, u32[]{:S(2)}, u32[]{:S(2)}) collective-permute-start(bf16[112,1408]{1,0:T(8,128)(2,1)S(1)} %get-tuple-element.158.mine_ref), channel_id=1, source_target_pairs={{0,16},{16,0},{1,17},{17,1},{2,18},{18,2},{3,19},{19,3},{4,20},{20... | collective-permute-start | bytes 946184 | tf_op jit(solution)/shard_map/ppermute | solution.py:461
  79.9 2.0 %collective-permute-start.20 = (bf16[128,2048]{1,0:T(8,128)(2,1)S(1)}, bf16[128,2048]{1,0:T(8,128)(2,1)S(1)}, u32[]{:S(2)}, u32[]{:S(2)}) collective-permute-start(bf16[128,2048]{1,0:T(8,128)(2,1)S(1)} %get-tuple-element.149), channel_id=1, source_target_pairs={{0,1},{1,0},{2,3},{3,2},{4,5},{5,4},{6,7},{7,6},{8,9},{9,8},{10,11... | collective-permute-start | bytes 1572872 | tf_op jit(solution)/shard_map/ppermute | solution.py:471
  80.0 18.1 %collective-permute-start.26 = (bf16[128,2048]{1,0:T(8,128)(2,1)S(1)}, bf16[128,2048]{1,0:T(8,128)(2,1)S(1)}, u32[]{:S(2)}, u32[]{:S(2)}) collective-permute-start(bf16[128,2048]{1,0:T(8,128)(2,1)S(1)} %get-tuple-element.157), channel_id=1, source_target_pairs={{0,1},{1,0},{2,3},{3,2},{4,5},{5,4},{6,7},{7,6},{8,9},{9,8},{10,11... | collective-permute-start | bytes 1572872 | tf_op jit(solution)/shard_map/ppermute | solution.py:471
  82.1 9.5 %collective-permute-start.28 = (bf16[128,2048]{1,0:T(8,128)(2,1)S(1)}, bf16[128,2048]{1,0:T(8,128)(2,1)S(1)}, u32[]{:S(2)}, u32[]{:S(2)}) collective-permute-start(bf16[128,2048]{1,0:T(8,128)(2,1)S(1)} %add.18), channel_id=1, source_target_pairs={{0,4},{2,0},{4,8},{6,2},{8,12},{10,6},{12,14},{14,10},{5,1},{1,3},... | collective-permute-start | bytes 1572872 | tf_op jit(solution)/shard_map/ppermute | solution.py:476
  87.3 4.3 %collective-permute-start.27 = (bf16[128,2048]{1,0:T(8,128)(2,1)S(1)}, bf16[128,2048]{1,0:T(8,128)(2,1)S(1)}, u32[]{:S(2)}, u32[]{:S(2)}) collective-permute-start(bf16[128,2048]{1,0:T(8,128)(2,1)S(1)} %get-tuple-element.162), channel_id=1, source_target_pairs={{0,1},{1,0},{2,3},{3,2},{4,5},{5,4},{6,7},{7,6},{8,9},{9,8},{10,11... | collective-permute-start | bytes 1572872 | tf_op jit(solution)/shard_map/ppermute | solution.py:471
  91.7 6.4 %collective-permute-start.32 = (bf16[128,1024]{1,0:T(8,128)(2,1)S(1)}, bf16[128,1024]{1,0:T(8,128)(2,1)S(1)}, u32[]{:S(2)}, u32[]{:S(2)}) collective-permute-start(bf16[128,1024]{1,0:T(8,128)(2,1)S(1)} %add.21), channel_id=1, source_target_pairs={{0,4},{2,0},{4,8},{6,2},{8,12},{10,6},{12,14},{14,10},{5,1},{1,3},... | collective-permute-start | bytes 786440 | tf_op jit(solution)/shard_map/ppermute | solution.py:476
  92.8 8.1 %collective-permute-start.29 = (bf16[128,1024]{1,0:T(8,128)(2,1)S(1)}, bf16[128,1024]{1,0:T(8,128)(2,1)S(1)}, u32[]{:S(2)}, u32[]{:S(2)}) collective-permute-start(bf16[128,1024]{1,0:T(8,128)(2,1)S(1)} %add.19), channel_id=1, source_target_pairs={{0,4},{2,0},{4,8},{6,2},{8,12},{10,6},{12,14},{14,10},{5,1},{1,3},... | collective-permute-start | bytes 786440 | tf_op jit(solution)/shard_map/ppermute | solution.py:476
  94.3 8.0 %collective-permute-start.25 = (bf16[112,1408]{1,0:T(8,128)(2,1)S(1)}, bf16[112,1408]{1,0:T(8,128)(2,1)S(1)}, u32[]{:S(2)}, u32[]{:S(2)}) collective-permute-start(bf16[112,1408]{1,0:T(8,128)(2,1)S(1)} %get-tuple-element.155.mine_ref), channel_id=1, source_target_pairs={{0,16},{16,0},{1,17},{17,1},{2,18},{18,2},{3,19},{19,3},{4,20},{20... | collective-permute-start | bytes 946184 | tf_op jit(solution)/shard_map/ppermute | solution.py:461
  95.1 20.1 %collective-permute-start.31 = (bf16[128,2048]{1,0:T(8,128)(2,1)S(1)}, bf16[128,2048]{1,0:T(8,128)(2,1)S(1)}, u32[]{:S(2)}, u32[]{:S(2)}) collective-permute-start(bf16[128,2048]{1,0:T(8,128)(2,1)S(1)} %get-tuple-element.171), channel_id=1, source_target_pairs={{0,1},{1,0},{2,3},{3,2},{4,5},{5,4},{6,7},{7,6},{8,9},{9,8},{10,11... | collective-permute-start | bytes 1572872 | tf_op jit(solution)/shard_map/ppermute | solution.py:471
  98.1 8.7 %collective-permute-start.15 = (bf16[128,2048]{1,0:T(8,128)(2,1)S(1)}, bf16[128,2048]{1,0:T(8,128)(2,1)S(1)}, u32[]{:S(2)}, u32[]{:S(2)}) collective-permute-start(bf16[128,2048]{1,0:T(8,128)(2,1)S(1)} %get-tuple-element.132), channel_id=1, source_target_pairs={{0,1},{1,0},{2,3},{3,2},{4,5},{5,4},{6,7},{7,6},{8,9},{9,8},{10,11... | collective-permute-start | bytes 1572872 | tf_op jit(solution)/shard_map/ppermute | solution.py:471
  98.2 11.1 %collective-permute-start.33 = (bf16[128,1024]{1,0:T(8,128)(2,1)S(1)}, bf16[128,1024]{1,0:T(8,128)(2,1)S(1)}, u32[]{:S(2)}, u32[]{:S(2)}) collective-permute-start(bf16[128,1024]{1,0:T(8,128)(2,1)S(1)} %add.22), channel_id=1, source_target_pairs={{0,4},{2,0},{4,8},{6,2},{8,12},{10,6},{12,14},{14,10},{5,1},{1,3},... | collective-permute-start | bytes 786440 | tf_op jit(solution)/shard_map/ppermute | solution.py:476
  102.3 6.4 %collective-permute-start.36 = (bf16[128,1024]{1,0:T(8,128)(2,1)S(1)}, bf16[128,1024]{1,0:T(8,128)(2,1)S(1)}, u32[]{:S(2)}, u32[]{:S(2)}) collective-permute-start(bf16[128,1024]{1,0:T(8,128)(2,1)S(1)} %add.20), channel_id=1, source_target_pairs={{0,4},{2,0},{4,8},{6,2},{8,12},{10,6},{12,14},{14,10},{5,1},{1,3},... | collective-permute-start | bytes 786440 | tf_op jit(solution)/shard_map/ppermute | solution.py:476
  108.8 6.4 %collective-permute-start.37 = (bf16[128,1024]{1,0:T(8,128)(2,1)S(1)}, bf16[128,1024]{1,0:T(8,128)(2,1)S(1)}, u32[]{:S(2)}, u32[]{:S(2)}) collective-permute-start(bf16[128,1024]{1,0:T(8,128)(2,1)S(1)} %add.25), channel_id=1, source_target_pairs={{0,4},{2,0},{4,8},{6,2},{8,12},{10,6},{12,14},{14,10},{5,1},{1,3},... | collective-permute-start | bytes 786440 | tf_op jit(solution)/shard_map/ppermute | solution.py:476
  109.4 8.6 %collective-permute-start.34 = (bf16[128,1024]{1,0:T(8,128)(2,1)S(1)}, bf16[128,1024]{1,0:T(8,128)(2,1)S(1)}, u32[]{:S(2)}, u32[]{:S(2)}) collective-permute-start(bf16[128,1024]{1,0:T(8,128)(2,1)S(1)} %add.23), channel_id=1, source_target_pairs={{0,4},{2,0},{4,8},{6,2},{8,12},{10,6},{12,14},{14,10},{5,1},{1,3},... | collective-permute-start | bytes 786440 | tf_op jit(solution)/shard_map/ppermute | solution.py:476
  111.0 13.5 %collective-permute-start.30 = (bf16[128,2048]{1,0:T(8,128)(2,1)S(1)}, bf16[128,2048]{1,0:T(8,128)(2,1)S(1)}, u32[]{:S(2)}, u32[]{:S(2)}) collective-permute-start(bf16[128,2048]{1,0:T(8,128)(2,1)S(1)} %get-tuple-element.169), channel_id=1, source_target_pairs={{0,1},{1,0},{2,3},{3,2},{4,5},{5,4},{6,7},{7,6},{8,9},{9,8},{10,11... | collective-permute-start | bytes 1572872 | tf_op jit(solution)/shard_map/ppermute | solution.py:471
  115.3 7.8 %collective-permute-start.38 = (bf16[128,1024]{1,0:T(8,128)(2,1)S(1)}, bf16[128,1024]{1,0:T(8,128)(2,1)S(1)}, u32[]{:S(2)}, u32[]{:S(2)}) collective-permute-start(bf16[128,1024]{1,0:T(8,128)(2,1)S(1)} %add.26), channel_id=1, source_target_pairs={{0,4},{2,0},{4,8},{6,2},{8,12},{10,6},{12,14},{14,10},{5,1},{1,3},... | collective-permute-start | bytes 786440 | tf_op jit(solution)/shard_map/ppermute | solution.py:540
  118.1 6.4 %collective-permute-start.35 = (bf16[128,1024]{1,0:T(8,128)(2,1)S(1)}, bf16[128,1024]{1,0:T(8,128)(2,1)S(1)}, u32[]{:S(2)}, u32[]{:S(2)}) collective-permute-start(bf16[128,1024]{1,0:T(8,128)(2,1)S(1)} %add.24.after_ref), channel_id=1, source_target_pairs={{0,4},{2,0},{4,8},{6,2},{8,12},{10,6},{12,14},{14,10},{5,1},{1,3},... | collective-permute-start | bytes 786440 | tf_op jit(solution)/shard_map/ppermute | solution.py:540

commit v3 on v2

--- a/solution.py
+++ b/solution.py
@@ -505,6 +505,9 @@
         share(stage)
         every = take(stage, every)
         trade(stage)
+        if i == 2:
+            after(own, [1], partial, stage)
+            collect(1, None)
         if i == 0:
             ids, partial[stage] = tie((ids, partial[stage]))
             to_gate, to_up, hidden, token = prep(
@@ -518,13 +521,11 @@
                 wup, _ = hold(w_up[0], leads[stage][0], *tokens)
                 held = (wgate, wup)
             after(theirs, [before], partial, stage)
-            if i + 1 == len(stages):
-                grads = [grad_rows(hidden, every, leads[stage][0], 0, [])]
-                after(theirs, [before], grads, 0)
             give(before)
             if not final:
                 after(rows, stages[i + 1], own, before[0])
-            collect(before[0], before[0] - 1 if before[0] > 1 else None)
+            if i > 1:
+                collect(before[0], before[0] - 1)
         before = stage
     after(theirs, [before], totals[before[0] - 1], 0)
     after(partial, [last], totals[before[0] - 1], 0)
@@ -532,10 +533,13 @@
     give(before)
     for s in range(before[0], chips):
         collect(s, s - 1)
+        if s == before[0]:
+            grads = [grad_rows(hidden, every, totals[s][1], 0, [])]
+            after(given, [s + 1], grads, 0)
         if s == before[0] + 1:
             after(theirs, [last], totals[s], 1)
             give(last)
-            after(given, [s + 1], own, 0)
+            after(given, [s + 2], own, 0)
     grads = [grad_rows(hidden, every, totals[chips - 1][0], 1, grads)]
     received = [mark(lax.ppermute(part, "expert", ring), 1.0) for part in totals[chips - 1]]
     grad_x = add(slice(0, dcols), own[0], given[0], received)

time: 126 us -> 123 us (0.976)
  waiting for transfers between devices: 26.4 us -> 16.9 us
  starting transfers between devices: 31.5 us -> 38 us
    ppermute x9, waiting for transfers between devices: 18.7 us -> 10.2 us  [collect(): lax.ppermute(part, 'expert', ring)]
    ppermute x9, starting transfers between devices: 10.5 us -> 14 us  [collect(): lax.ppermute(part, 'expert', ring)]
    ppermute x2, starting transfers between devices: 1.12 us -> 3.67 us  [ring_local(): lax.ppermute(part, 'expert', ring)]
    ppermute x8, waiting for transfers between devices: 2.85 us -> 1.41 us  [give(): given[s] = lax.ppermute(parts[2 * i + 1], 'expert', sibling)]
  transfers between devices with their start and end apart: 39 -> 39, of which waited for: 17 -> 17; matrix products, arithmetic and copies ran while one was open for 1% -> 1% of each run, Pallas kernels for 51% -> 52%
where the time goes in v3:
time: 123 us
  Pallas kernels  66.1 us (54%)
  starting transfers between devices  38 us (31%)
  waiting for transfers between devices  16.9 us (14%)
    pallas_call x5, Pallas kernels, give_rows(): pl.pallas_call(functools.partial(give_kernel, count, first), in_specs=[VM...  20.7 us
    ppermute x9, starting transfers between devices, collect(): lax.ppermute(part, 'expert', ring)  14 us
    pallas_call x2, Pallas kernels, prep(): pl.pallas_call(functools.partial(prep_kernel, capacity, tiles[0]), grid_s...  12 us
    pallas_call x5, Pallas kernels, take_rows(): pl.pallas_call(functools.partial(take_kernel, experts, count, first), in_...  11.7 us
    ppermute x9, waiting for transfers between devices, collect(): lax.ppermute(part, 'expert', ring)  10.2 us
    pallas_call x3, Pallas kernels, hold(): pl.pallas_call(hold_kernel, in_specs=[ANY] * (1 + len(after)), out_specs=...  9.12 us
    pallas_call x2, Pallas kernels, grad_rows(): pl.pallas_call(grad_kernel, grid=(2,), in_specs=[pl.BlockSpec((rows, slot...  8.9 us
    ppermute x5, starting transfers between devices, trade(): theirs[stage] = lax.ppermute(partial[stage], 'dp', swap)  8.03 us
  transfers between devices with their start and end apart: 39, of which 17 were waited for; matrix products, arithmetic and copies ran while one was open for 1% of the time, Pallas kernels for 52%

profile of v3, /device:TPU:0, one launch (start us, length us, event | category | flops | bytes accessed | tf_op | source)
XLA Modules:
  0.0 122.6 jit_solution(15577457580993537126)
XLA Ops:
  0.6 1.3 %pack.1.refs_0_ = bf16[128,2176]{1,0:T(8,128)(2,1)S(1)} custom-call(bf16[128,2048]{1,0:T(8,128)(2,1)} %rows_ref.1, s32[6,128]{1,0:T(8,128)} %bitcast.20, f32[6,128]{1,0:T(8,128)} %bitcast.21, f32[1,128]{1,0:T(1,128)} %bitcast.22), custom_call_target="tpu_custom_call" | custom-call | tf_op jit(solution)/shard_map/pack/pallas_call | solution.py:134
  2.0 0.5 collective-permute-start
  2.5 2.6 %collective-permute-start.1 = (bf16[128,2176]{1,0:T(8,128)(2,1)S(1)}, bf16[128,2176]{1,0:T(8,128)(2,1)S(1)}, u32[]{:S(2)}, u32[]{:S(2)}) collective-permute-start(bf16[128,2176]{1,0:T(8,128)(2,1)S(1)} %pack.1.refs_0_), channel_id=1, source_target_pairs={{0,4},{2,0},{4,8},{6,2},{8,12},{10,6},{12,14},{14,10},{5,1},{1,3},... | collective-permute-start | bytes 1671176 | tf_op jit(solution)/shard_map/ppermute | solution.py:445
  5.1 0.7 dynamic-slice_bitcast_fusion.refs_1_.ids_ref
  5.8 3.2 %hold.3 = (bf16[1408,2048]{1,0:T(8,128)(2,1)S(1)}, f32[8,128]{1,0:T(8,128)}) custom-call(bf16[1408,2048]{1,0:T(8,128)(2,1)} %bitcast.17, bf16[128,2176]{1,0:T(8,128)(2,1)S(1)} %pack.1.refs_0_, s32[16]{0:T(128)S(1)} %dynamic-slice_bitcast_fusion.refs_1_.ids_ref), custom_call_target="tpu_custom_call" | custom-call | tf_op jit(solution)/shard_map/hold/pallas_call | solution.py:206
  9.1 2.3 %take.5 = (bf16[896,2048]{1,0:T(8,128)(2,1)S(1)}, bf16[112,1408]{1,0:T(8,128)(2,1)S(1)}, bf16[128,56]{1,0:T(8,128)(2,1)S(1)}, bf16[128,56]{1,0:T(8,128)(2,1)S(1)}) custom-call(s32[1]{0:T(128)} %bitcast.1.me_ref, bf16[1408,2048]{1,0:T(8,128)(2,1)S(1)} %get-tuple-element.91.wdown_ref, bf16[128,2176]{1,0:T(8,128)(2,1)S(1)} %pack.1.refs_0_, ...), custom_call_target="tpu_custom_call" | custom-call | tf_op jit(solution)/shard_map/take/pallas_call | solution.py:252
  11.3 6.4 %prep.2 = (bf16[896,1408]{1,0:T(8,128)(2,1)S(1)}, bf16[896,1408]{1,0:T(8,128)(2,1)S(1)}, bf16[1408,896]{1,0:T(8,128)(2,1)S(1)}, f32[8,128]{1,0:T(8,128)S(1)}) custom-call(s32[16]{0:T(128)S(1)} %dynamic-slice_bitcast_fusion.refs_1_.ids_ref, bf16[1408,896]{1,0:T(8,128)(2,1)} %bitcast.13, bf16[1408,896]{1,0:T(8,128)(2,1)} %bitcast.15), custom_call_target="tpu_custom_call" | custom-call | flops 6881280 | bytes 6881280 | tf_op jit(solution)/shard_map/prep/pallas_call | solution.py:173
  17.8 0.6 collective-permute-done.2.refs_2_
  18.5 0.4 collective-permute-start.4
  18.9 1.8 %collective-permute-start.6 = (bf16[128,2176]{1,0:T(8,128)(2,1)S(1)}, bf16[128,2176]{1,0:T(8,128)(2,1)S(1)}, u32[]{:S(2)}, u32[]{:S(2)}) collective-permute-start(bf16[128,2176]{1,0:T(8,128)(2,1)S(1)} %collective-permute-done.1.refs_0_), channel_id=1, source_target_pairs={{0,4},{2,0},{4,8},{6,2},{8,12},{10,6},{12,14},{14,10},{5,1},{1,3},... | collective-permute-start | bytes 1671176 | tf_op jit(solution)/shard_map/ppermute | solution.py:445
  20.6 0.3 collective-permute-start.7
  21.1 2.4 %take.6 = (bf16[896,2048]{1,0:T(8,128)(2,1)S(1)}, bf16[224,1408]{1,0:T(8,128)(2,1)S(1)}, bf16[128,56]{1,0:T(8,128)(2,1)S(1)}, bf16[128,56]{1,0:T(8,128)(2,1)S(1)...) custom-call(s32[1]{0:T(128)} %bitcast.1.me_ref, ...), custom_call_target="tpu_custom_call", output_to_operand_aliasing={{0}: (6, {})} | custom-call | tf_op jit(solution)/shard_map/take/pallas_call | solution.py:252
  23.5 1.7 %collective-permute-start.5 = (bf16[224,1408]{1,0:T(8,128)(2,1)S(1)}, bf16[224,1408]{1,0:T(8,128)(2,1)S(1)}, u32[]{:S(2)}, u32[]{:S(2)}) collective-permute-start(bf16[224,1408]{1,0:T(8,128)(2,1)S(1)} %get-tuple-element.101.mine_ref), channel_id=1, source_target_pairs={{0,16},{16,0},{1,17},{17,1},{2,18},{18,2},{3,19},{19,3},{4,20},{20... | collective-permute-start | bytes 1892360 | tf_op jit(solution)/shard_map/ppermute | solution.py:461
  25.2 5.6 %prep.3 = (bf16[896,1408]{1,0:T(8,128)(2,1)S(1)}, bf16[896,1408]{1,0:T(8,128)(2,1)S(1)}, bf16[1408,896]{1,0:T(8,128)(2,1)S(1)}, f32[8,128]{1,0:T(8,128)S(1)}) custom-call(s32[16]{0:T(128)S(1)} %dynamic-slice_bitcast_fusion.refs_1_.ids_ref, bf16[1408,896]{1,0:T(8,128)(2,1)} %bitcast.14, ...), custom_call_target="tpu_custom_call", output_to_operand_aliasing={{0}: (3, {}), {1}: (4, {}), {2}: (5, {})} | custom-call | flops 5734400 | bytes 5734400 | tf_op jit(solution)/shard_map/prep/pallas_call | solution.py:173
  30.9 2.6 %hold.4 = (bf16[2048,1408]{1,0:T(8,128)(2,1)S(1)}, f32[8,128]{1,0:T(8,128)S(1)}) custom-call(bf16[2048,1408]{1,0:T(8,128)(2,1)} %bitcast.18, f32[8,128]{1,0:T(8,128)S(1)} %get-tuple-element.102.refs_0_, f32[8,128]{1,0:T(8,128)S(1)} %get-tuple-element.107.refs_1_), custom_call_target="tpu_custom_call" | custom-call | tf_op jit(solution)/shard_map/hold/pallas_call | solution.py:206
  33.6 0.9 collective-permute-start.8
  34.5 1.5 %collective-permute-start.11 = (bf16[128,2176]{1,0:T(8,128)(2,1)S(1)}, bf16[128,2176]{1,0:T(8,128)(2,1)S(1)}, u32[]{:S(2)}, u32[]{:S(2)}) collective-permute-start(bf16[128,2176]{1,0:T(8,128)(2,1)S(1)} %collective-permute-done.6.refs_0_), channel_id=1, source_target_pairs={{0,4},{2,0},{4,8},{6,2},{8,12},{10,6},{12,14},{14,10},{5,1},{1,3},... | collective-permute-start | bytes 1671176 | tf_op jit(solution)/shard_map/ppermute | solution.py:445
  35.9 0.6 collective-permute-start.12
  36.5 0.3 collective-permute-done.9.refs_3_
  36.9 2.4 %take.7 = (bf16[896,2048]{1,0:T(8,128)(2,1)S(1)}, bf16[224,1408]{1,0:T(8,128)(2,1)S(1)}, bf16[128,56]{1,0:T(8,128)(2,1)S(1)}, bf16[128,56]{1,0:T(8,128)(2,1)S(1)...) custom-call(s32[1]{0:T(128)} %bitcast.1.me_ref, ...), custom_call_target="tpu_custom_call", output_to_operand_aliasing={{0}: (6, {})} | custom-call | tf_op jit(solution)/shard_map/take/pallas_call | solution.py:252
  39.3 1.7 %collective-permute-start.14 = (bf16[224,1408]{1,0:T(8,128)(2,1)S(1)}, bf16[224,1408]{1,0:T(8,128)(2,1)S(1)}, u32[]{:S(2)}, u32[]{:S(2)}) collective-permute-start(bf16[224,1408]{1,0:T(8,128)(2,1)S(1)} %get-tuple-element.128.mine_ref), channel_id=1, source_target_pairs={{0,16},{16,0},{1,17},{17,1},{2,18},{18,2},{3,19},{19,3},{4,20},{20... | collective-permute-start | bytes 1892360 | tf_op jit(solution)/shard_map/ppermute | solution.py:461
  41.0 3.2 %hold.5 = (bf16[2048,1408]{1,0:T(8,128)(2,1)S(1)}, f32[8,128]{1,0:T(8,128)}) custom-call(bf16[2048,1408]{1,0:T(8,128)(2,1)} %bitcast.19, bf16[128,56]{1,0:T(8,128)(2,1)S(1)} %get-tuple-element.117.refs_0_, f32[8,128]{1,0:T(8,128)S(1)} %get-tuple-element.118.refs_1_), custom_call_target="tpu_custom_call" | custom-call | tf_op jit(solution)/shard_map/hold/pallas_call | solution.py:206
  44.3 4.3 %give.5 = (bf16[128,2048]{1,0:T(8,128)(2,1)S(1)}, bf16[128,2048]{1,0:T(8,128)(2,1)S(1)}, bf16[128,2048]{1,0:T(8,128)(2,1)S(1)}, bf16[128,2048]{1,0:T(8,128)(2,1)S(1)}) custom-call(bf16[224,1408]{1,0:T(8,128)(2,1)S(1)} %get-tuple-element.101.mine_ref, bf16[224,1408]{1,0:T(8,128)(2,1)S(1)} %mark.17.theirs_ref, ...), custom_call_target="tpu_custom_call" | custom-call | tf_op jit(solution)/shard_map/give/pallas_call | solution.py:292
  48.6 0.5 collective-permute-done.11.refs_0_
  49.0 0.5 collective-permute-done.12.refs_2_
  49.5 0.6 collective-permute-start.15
  50.1 0.5 collective-permute-start.22
  50.6 1.2 collective-permute-start.13
  51.8 0.7 collective-permute-done.16.refs_3_
  52.5 2.4 %take.8 = (bf16[896,2048]{1,0:T(8,128)(2,1)S(1)}, bf16[224,1408]{1,0:T(8,128)(2,1)S(1)}, bf16[128,56]{1,0:T(8,128)(2,1)S(1)}, bf16[128,56]{1,0:T(8,128)(2,1)S(1)...) custom-call(s32[1]{0:T(128)} %bitcast.1.me_ref, ...), custom_call_target="tpu_custom_call", output_to_operand_aliasing={{0}: (6, {})} | custom-call | tf_op jit(solution)/shard_map/take/pallas_call | solution.py:252
  54.9 1.7 %collective-permute-start.19 = (bf16[224,1408]{1,0:T(8,128)(2,1)S(1)}, bf16[224,1408]{1,0:T(8,128)(2,1)S(1)}, u32[]{:S(2)}, u32[]{:S(2)}) collective-permute-start(bf16[224,1408]{1,0:T(8,128)(2,1)S(1)} %get-tuple-element.142.mine_ref), channel_id=1, source_target_pairs={{0,16},{16,0},{1,17},{17,1},{2,18},{18,2},{3,19},{19,3},{4,20},{20... | collective-permute-start | bytes 1892360 | tf_op jit(solution)/shard_map/ppermute | solution.py:461
  56.8 1.6 %collective-permute-start.23 = (bf16[128,2048]{1,0:T(8,128)(2,1)S(1)}, bf16[128,2048]{1,0:T(8,128)(2,1)S(1)}, u32[]{:S(2)}, u32[]{:S(2)}) collective-permute-start(bf16[128,2048]{1,0:T(8,128)(2,1)S(1)} %add.16), channel_id=1, source_target_pairs={{0,4},{2,0},{4,8},{6,2},{8,12},{10,6},{12,14},{14,10},{5,1},{1,3},... | collective-permute-start | bytes 1572872 | tf_op jit(solution)/shard_map/ppermute | solution.py:476
  58.4 4.3 %give.6 = (bf16[128,2048]{1,0:T(8,128)(2,1)S(1)}, bf16[128,2048]{1,0:T(8,128)(2,1)S(1)}, bf16[128,2048]{1,0:T(8,128)(2,1)S(1)}, bf16[128,2048]{1,0:T(8,128)(2,1)S(1)}) custom-call(bf16[224,1408]{1,0:T(8,128)(2,1)S(1)} %get-tuple-element.128.mine_ref, bf16[224,1408]{1,0:T(8,128)(2,1)S(1)} %mark.18.theirs_ref, ...), custom_call_target="tpu_custom_call" | custom-call | tf_op jit(solution)/shard_map/give/pallas_call | solution.py:292
  62.8 0.5 collective-permute-start.17
  63.2 2.8 %collective-permute-done.23.old_ref = bf16[128,2048]{1,0:T(8,128)(2,1)S(1)} collective-permute-done((bf16[128,2048]{1,0:T(8,128)(2,1)S(1)}, bf16[128,2048]{1,0:T(8,128)(2,1)S(1)}, u32[]{:S(2)}, u32[]{:S(2)}) %collective-permute-start.23) | collective-permute-done | bytes 524320 | tf_op jit(solution)/shard_map/ppermute | solution.py:476
  66.2 1.6 %collective-permute-start.24 = (bf16[128,2048]{1,0:T(8,128)(2,1)S(1)}, bf16[128,2048]{1,0:T(8,128)(2,1)S(1)}, u32[]{:S(2)}, u32[]{:S(2)}) collective-permute-start(bf16[128,2048]{1,0:T(8,128)(2,1)S(1)} %add.17), channel_id=1, source_target_pairs={{0,4},{2,0},{4,8},{6,2},{8,12},{10,6},{12,14},{14,10},{5,1},{1,3},... | collective-permute-start | bytes 1572872 | tf_op jit(solution)/shard_map/ppermute | solution.py:476
  67.8 2.2 %take.9 = (bf16[896,2048]{1,0:T(8,128)(2,1)S(1)}, bf16[112,1408]{1,0:T(8,128)(2,1)S(1)}, bf16[128,56]{1,0:T(8,128)(2,1)S(1)}, bf16[128,56]{1,0:T(8,128)(2,1)S(1)}) custom-call(s32[1]{0:T(128)} %bitcast.1.me_ref, bf16[1408,2048]{1,0:T(8,128)(2,1)S(1)} %get-tuple-element.91.wdown_ref, ...), custom_call_target="tpu_custom_call", output_to_operand_aliasing={{0}: (4, {})} | custom-call | tf_op jit(solution)/shard_map/take/pallas_call | solution.py:252
  70.0 1.1 collective-permute-start.18
  71.2 0.3 collective-permute-done.19.old_ref
  71.5 4.3 %give.7 = (bf16[128,2048]{1,0:T(8,128)(2,1)S(1)}, bf16[128,2048]{1,0:T(8,128)(2,1)S(1)}, bf16[128,2048]{1,0:T(8,128)(2,1)S(1)}, bf16[128,2048]{1,0:T(8,128)(2,1)S(1)}) custom-call(bf16[224,1408]{1,0:T(8,128)(2,1)S(1)} %get-tuple-element.142.mine_ref, bf16[224,1408]{1,0:T(8,128)(2,1)S(1)} %mark.19.theirs_ref, ...), custom_call_target="tpu_custom_call" | custom-call | tf_op jit(solution)/shard_map/give/pallas_call | solution.py:292
  75.8 0.5 collective-permute-start.26
  76.3 1.4 %collective-permute-done.20.given_ref = bf16[128,2048]{1,0:T(8,128)(2,1)S(1)} collective-permute-done((bf16[128,2048]{1,0:T(8,128)(2,1)S(1)}, bf16[128,2048]{1,0:T(8,128)(2,1)S(1)}, u32[]{:S(2)}, u32[]{:S(2)}) %collective-permute-start.20) | collective-permute-done | bytes 524320 | tf_op jit(solution)/shard_map/ppermute | solution.py:471
  77.9 0.5 collective-permute-done.18.old_ref
  78.4 1.7 %collective-permute-start.28 = (bf16[128,2048]{1,0:T(8,128)(2,1)S(1)}, bf16[128,2048]{1,0:T(8,128)(2,1)S(1)}, u32[]{:S(2)}, u32[]{:S(2)}) collective-permute-start(bf16[128,2048]{1,0:T(8,128)(2,1)S(1)} %add.18), channel_id=1, source_target_pairs={{0,4},{2,0},{4,8},{6,2},{8,12},{10,6},{12,14},{14,10},{5,1},{1,3},... | collective-permute-start | bytes 1572872 | tf_op jit(solution)/shard_map/ppermute | solution.py:476
  80.1 3.9 %give.8 = (bf16[128,2048]{1,0:T(8,128)(2,1)S(1)}, bf16[128,2048]{1,0:T(8,128)(2,1)S(1)}) custom-call(bf16[112,1408]{1,0:T(8,128)(2,1)S(1)} %get-tuple-element.160.mine_ref, bf16[112,1408]{1,0:T(8,128)(2,1)S(1)} %mark.22.theirs_ref, bf16[896,1408]{1,0:T(8,128)(2,1)S(1)} %get-tuple-element.114.to_gate_ref, bf16[896,1408]{1,0:T(8,128)(2,1)S(1)} %get-tuple-element.115.to_up_ref, ...), custom_call_target="tpu_custom_call" | custom-call | tf_op jit(solution)/shard_map/give/pallas_call | solution.py:292
  84.1 3.5 %collective-permute-done.28.old_ref = bf16[128,2048]{1,0:T(8,128)(2,1)S(1)} collective-permute-done((bf16[128,2048]{1,0:T(8,128)(2,1)S(1)}, bf16[128,2048]{1,0:T(8,128)(2,1)S(1)}, u32[]{:S(2)}, u32[]{:S(2)}) %collective-permute-start.28) | collective-permute-done | bytes 524320 | tf_op jit(solution)/shard_map/ppermute | solution.py:476
  87.7 1.7 %collective-permute-start.32 = (bf16[128,1024]{1,0:T(8,128)(2,1)S(1)}, bf16[128,1024]{1,0:T(8,128)(2,1)S(1)}, u32[]{:S(2)}, u32[]{:S(2)}) collective-permute-start(bf16[128,1024]{1,0:T(8,128)(2,1)S(1)} %add.21), channel_id=1, source_target_pairs={{0,4},{2,0},{4,8},{6,2},{8,12},{10,6},{12,14},{14,10},{5,1},{1,3},... | collective-permute-start | bytes 786440 | tf_op jit(solution)/shard_map/ppermute | solution.py:476
  89.5 0.7 collective-permute-start.29
  90.2 1.7 %collective-permute-start.25 = (bf16[112,1408]{1,0:T(8,128)(2,1)S(1)}, bf16[112,1408]{1,0:T(8,128)(2,1)S(1)}, u32[]{:S(2)}, u32[]{:S(2)}) collective-permute-start(bf16[112,1408]{1,0:T(8,128)(2,1)S(1)} %get-tuple-element.155.mine_ref), channel_id=1, source_target_pairs={{0,16},{16,0},{1,17},{17,1},{2,18},{18,2},{3,19},{19,3},{4,20},{20... | collective-permute-start | bytes 946184 | tf_op jit(solution)/shard_map/ppermute | solution.py:461
  91.9 4.4 %grad_down.2.refs_0_ = bf16[1408,2048]{1,0:T(8,128)(2,1)} custom-call(bf16[1408,896]{1,0:T(8,128)(2,1)S(1)} %get-tuple-element.158.hidden_ref, bf16[896,2048]{1,0:T(8,128)(2,1)S(1)} %get-tuple-element.159.every_ref, bf16[128,1024]{1,0:T(8,128)(2,1)S(1)} %add.19.after_ref), custom_call_target="tpu_custom_call" | custom-call | tf_op jit(solution)/shard_map/grad_down/pallas_call | solution.py:336
  96.5 1.8 %collective-permute-start.33 = (bf16[128,1024]{1,0:T(8,128)(2,1)S(1)}, bf16[128,1024]{1,0:T(8,128)(2,1)S(1)}, u32[]{:S(2)}, u32[]{:S(2)}) collective-permute-start(bf16[128,1024]{1,0:T(8,128)(2,1)S(1)} %add.22), channel_id=1, source_target_pairs={{0,4},{2,0},{4,8},{6,2},{8,12},{10,6},{12,14},{14,10},{5,1},{1,3},... | collective-permute-start | bytes 786440 | tf_op jit(solution)/shard_map/ppermute | solution.py:476
  98.4 0.6 collective-permute-done.25.old_ref
  99.0 1.2 collective-permute-start.36
  100.4 2.5 %collective-permute-done.33.old_ref = bf16[128,1024]{1,0:T(8,128)(2,1)S(1)} collective-permute-done((bf16[128,1024]{1,0:T(8,128)(2,1)S(1)}, bf16[128,1024]{1,0:T(8,128)(2,1)S(1)}, u32[]{:S(2)}, u32[]{:S(2)}) %collective-permute-start.33) | collective-permute-done | bytes 262176 | tf_op jit(solution)/shard_map/ppermute | solution.py:476
  103.0 1.8 %collective-permute-start.34 = (bf16[128,1024]{1,0:T(8,128)(2,1)S(1)}, bf16[128,1024]{1,0:T(8,128)(2,1)S(1)}, u32[]{:S(2)}, u32[]{:S(2)}) collective-permute-start(bf16[128,1024]{1,0:T(8,128)(2,1)S(1)} %add.23), channel_id=1, source_target_pairs={{0,4},{2,0},{4,8},{6,2},{8,12},{10,6},{12,14},{14,10},{5,1},{1,3},... | collective-permute-start | bytes 786440 | tf_op jit(solution)/shard_map/ppermute | solution.py:476
  104.8 0.9 collective-permute-done.36.old_ref
  105.8 1.8 %collective-permute-start.37 = (bf16[128,1024]{1,0:T(8,128)(2,1)S(1)}, bf16[128,1024]{1,0:T(8,128)(2,1)S(1)}, u32[]{:S(2)}, u32[]{:S(2)}) collective-permute-start(bf16[128,1024]{1,0:T(8,128)(2,1)S(1)} %add.25), channel_id=1, source_target_pairs={{0,4},{2,0},{4,8},{6,2},{8,12},{10,6},{12,14},{14,10},{5,1},{1,3},... | collective-permute-start | bytes 786440 | tf_op jit(solution)/shard_map/ppermute | solution.py:476
  107.6 3.9 %give.9 = (bf16[128,2048]{1,0:T(8,128)(2,1)S(1)}, bf16[128,2048]{1,0:T(8,128)(2,1)S(1)}) custom-call(bf16[112,1408]{1,0:T(8,128)(2,1)S(1)} %get-tuple-element.155.mine_ref, bf16[112,1408]{1,0:T(8,128)(2,1)S(1)} %mark.26.theirs_ref, bf16[896,1408]{1,0:T(8,128)(2,1)S(1)} %get-tuple-element.114.to_gate_ref, bf16[896,1408]{1,0:T(8,128)(2,1)S(1)} %get-tuple-element.115.to_up_ref, ...), custom_call_target="tpu_custom_call" | custom-call | tf_op jit(solution)/shard_map/give/pallas_call | solution.py:292
  111.6 0.6 collective-permute-done.37.old_ref
  112.3 1.8 %collective-permute-start.38 = (bf16[128,1024]{1,0:T(8,128)(2,1)S(1)}, bf16[128,1024]{1,0:T(8,128)(2,1)S(1)}, u32[]{:S(2)}, u32[]{:S(2)}) collective-permute-start(bf16[128,1024]{1,0:T(8,128)(2,1)S(1)} %add.26), channel_id=1, source_target_pairs={{0,4},{2,0},{4,8},{6,2},{8,12},{10,6},{12,14},{14,10},{5,1},{1,3},... | collective-permute-start | bytes 786440 | tf_op jit(solution)/shard_map/ppermute | solution.py:544
  114.3 1.9 %collective-permute-start.35 = (bf16[128,1024]{1,0:T(8,128)(2,1)S(1)}, bf16[128,1024]{1,0:T(8,128)(2,1)S(1)}, u32[]{:S(2)}, u32[]{:S(2)}) collective-permute-start(bf16[128,1024]{1,0:T(8,128)(2,1)S(1)} %add.24.after_ref), channel_id=1, source_target_pairs={{0,4},{2,0},{4,8},{6,2},{8,12},{10,6},{12,14},{14,10},{5,1},{1,3},... | collective-permute-start | bytes 786440 | tf_op jit(solution)/shard_map/ppermute | solution.py:544
  116.1 4.4 %grad_down.3 = bf16[1408,2048]{1,0:T(8,128)(2,1)} custom-call(bf16[1408,896]{1,0:T(8,128)(2,1)S(1)} %get-tuple-element.158.hidden_ref, bf16[896,2048]{1,0:T(8,128)(2,1)S(1)} %get-tuple-element.159.every_ref, bf16[128,1024]{1,0:T(8,128)(2,1)S(1)} %add.24.after_ref, bf16[1408,2048]{1,0:T(8,128)(2,1)} %grad_down.2.refs_0_), custom_call_target="tpu_custom_call", output_to_operand_aliasing={{}: (3, {})} | custom-call | tf_op jit(solution)/shard_map/grad_down/pallas_call | solution.py:336
  120.6 1.0 collective-permute-done.35.old_ref
  121.6 1.0 add.27
  (62 shorter events, 2.2 us)
Async XLA Ops:
  2.0 7.1 %collective-permute-start = (bf16[128,2176]{1,0:T(8,128)(2,1)S(1)}, bf16[128,2176]{1,0:T(8,128)(2,1)S(1)}, u32[]{:S(2)}, u32[]{:S(2)}) collective-permute-start(bf16[128,2176]{1,0:T(8,128)(2,1)S(1)} %pack.1.refs_0_), channel_id=1, source_target_pairs={{0,1},{1,0},{2,3},{3,2},{4,5},{5,4},{6,7},{7,6},{8,9},{9,8},{10,11... | collective-permute-start | bytes 1671176 | tf_op jit(solution)/shard_map/ppermute | solution.py:451
  2.5 15.3 %collective-permute-start.1 = (bf16[128,2176]{1,0:T(8,128)(2,1)S(1)}, bf16[128,2176]{1,0:T(8,128)(2,1)S(1)}, u32[]{:S(2)}, u32[]{:S(2)}) collective-permute-start(bf16[128,2176]{1,0:T(8,128)(2,1)S(1)} %pack.1.refs_0_), channel_id=1, source_target_pairs={{0,4},{2,0},{4,8},{6,2},{8,12},{10,6},{12,14},{14,10},{5,1},{1,3},... | collective-permute-start | bytes 1671176 | tf_op jit(solution)/shard_map/ppermute | solution.py:445
  5.1 13.2 %collective-permute-start.2 = (bf16[128,2176]{1,0:T(8,128)(2,1)S(1)}, bf16[128,2176]{1,0:T(8,128)(2,1)S(1)}, u32[]{:S(2)}, u32[]{:S(2)}) collective-permute-start(bf16[128,2176]{1,0:T(8,128)(2,1)S(1)} %pack.1.refs_0_), channel_id=1, source_target_pairs={{4,0},{0,2},{8,4},{2,6},{12,8},{6,10},{14,12},{10,14},{1,5},{3,1},... | collective-permute-start | bytes 1671176 | tf_op jit(solution)/shard_map/ppermute | solution.py:447
  18.4 2.5 %collective-permute-start.3 = (bf16[128,2176]{1,0:T(8,128)(2,1)S(1)}, bf16[128,2176]{1,0:T(8,128)(2,1)S(1)}, u32[]{:S(2)}, u32[]{:S(2)}) collective-permute-start(bf16[128,2176]{1,0:T(8,128)(2,1)S(1)} %collective-permute-done.1.refs_0_), channel_id=1, source_target_pairs={{0,1},{1,0},{2,3},{3,2},{4,5},{5,4},{6,7},{7,6},{8,9},{9,8},{10,11... | collective-permute-start | bytes 1671176 | tf_op jit(solution)/shard_map/ppermute | solution.py:451
  18.5 2.6 %collective-permute-start.4 = (bf16[128,2176]{1,0:T(8,128)(2,1)S(1)}, bf16[128,2176]{1,0:T(8,128)(2,1)S(1)}, u32[]{:S(2)}, u32[]{:S(2)}) collective-permute-start(bf16[128,2176]{1,0:T(8,128)(2,1)S(1)} %collective-permute-done.2.refs_2_), channel_id=1, source_target_pairs={{0,1},{1,0},{2,3},{3,2},{4,5},{5,4},{6,7},{7,6},{8,9},{9,8},{10,11... | collective-permute-start | bytes 1671176 | tf_op jit(solution)/shard_map/ppermute | solution.py:451
  18.9 14.7 %collective-permute-start.6 = (bf16[128,2176]{1,0:T(8,128)(2,1)S(1)}, bf16[128,2176]{1,0:T(8,128)(2,1)S(1)}, u32[]{:S(2)}, u32[]{:S(2)}) collective-permute-start(bf16[128,2176]{1,0:T(8,128)(2,1)S(1)} %collective-permute-done.1.refs_0_), channel_id=1, source_target_pairs={{0,4},{2,0},{4,8},{6,2},{8,12},{10,6},{12,14},{14,10},{5,1},{1,3},... | collective-permute-start | bytes 1671176 | tf_op jit(solution)/shard_map/ppermute | solution.py:445
  20.6 13.0 %collective-permute-start.7 = (bf16[128,2176]{1,0:T(8,128)(2,1)S(1)}, bf16[128,2176]{1,0:T(8,128)(2,1)S(1)}, u32[]{:S(2)}, u32[]{:S(2)}) collective-permute-start(bf16[128,2176]{1,0:T(8,128)(2,1)S(1)} %collective-permute-done.2.refs_2_), channel_id=1, source_target_pairs={{4,0},{0,2},{8,4},{2,6},{12,8},{6,10},{14,12},{10,14},{1,5},{3,1},... | collective-permute-start | bytes 1671176 | tf_op jit(solution)/shard_map/ppermute | solution.py:447
  23.5 20.8 %collective-permute-start.5 = (bf16[224,1408]{1,0:T(8,128)(2,1)S(1)}, bf16[224,1408]{1,0:T(8,128)(2,1)S(1)}, u32[]{:S(2)}, u32[]{:S(2)}) collective-permute-start(bf16[224,1408]{1,0:T(8,128)(2,1)S(1)} %get-tuple-element.101.mine_ref), channel_id=1, source_target_pairs={{0,16},{16,0},{1,17},{17,1},{2,18},{18,2},{3,19},{19,3},{4,20},{20... | collective-permute-start | bytes 1892360 | tf_op jit(solution)/shard_map/ppermute | solution.py:461
  33.6 2.9 %collective-permute-start.8 = (bf16[128,2176]{1,0:T(8,128)(2,1)S(1)}, bf16[128,2176]{1,0:T(8,128)(2,1)S(1)}, u32[]{:S(2)}, u32[]{:S(2)}) collective-permute-start(bf16[128,2176]{1,0:T(8,128)(2,1)S(1)} %collective-permute-done.6.refs_0_), channel_id=1, source_target_pairs={{0,1},{1,0},{2,3},{3,2},{4,5},{5,4},{6,7},{7,6},{8,9},{9,8},{10,11... | collective-permute-start | bytes 1671176 | tf_op jit(solution)/shard_map/ppermute | solution.py:451
  34.5 2.4 %collective-permute-start.9 = (bf16[128,2176]{1,0:T(8,128)(2,1)S(1)}, bf16[128,2176]{1,0:T(8,128)(2,1)S(1)}, u32[]{:S(2)}, u32[]{:S(2)}) collective-permute-start(bf16[128,2176]{1,0:T(8,128)(2,1)S(1)} %collective-permute-done.7.refs_2_), channel_id=1, source_target_pairs={{0,1},{1,0},{2,3},{3,2},{4,5},{5,4},{6,7},{7,6},{8,9},{9,8},{10,11... | collective-permute-start | bytes 1671176 | tf_op jit(solution)/shard_map/ppermute | solution.py:451
  34.5 14.6 %collective-permute-start.11 = (bf16[128,2176]{1,0:T(8,128)(2,1)S(1)}, bf16[128,2176]{1,0:T(8,128)(2,1)S(1)}, u32[]{:S(2)}, u32[]{:S(2)}) collective-permute-start(bf16[128,2176]{1,0:T(8,128)(2,1)S(1)} %collective-permute-done.6.refs_0_), channel_id=1, source_target_pairs={{0,4},{2,0},{4,8},{6,2},{8,12},{10,6},{12,14},{14,10},{5,1},{1,3},... | collective-permute-start | bytes 1671176 | tf_op jit(solution)/shard_map/ppermute | solution.py:445
  35.9 13.6 %collective-permute-start.12 = (bf16[128,2176]{1,0:T(8,128)(2,1)S(1)}, bf16[128,2176]{1,0:T(8,128)(2,1)S(1)}, u32[]{:S(2)}, u32[]{:S(2)}) collective-permute-start(bf16[128,2176]{1,0:T(8,128)(2,1)S(1)} %collective-permute-done.7.refs_2_), channel_id=1, source_target_pairs={{4,0},{0,2},{8,4},{2,6},{12,8},{6,10},{14,12},{10,14},{1,5},{3,1},... | collective-permute-start | bytes 1671176 | tf_op jit(solution)/shard_map/ppermute | solution.py:447
  39.3 19.1 %collective-permute-start.14 = (bf16[224,1408]{1,0:T(8,128)(2,1)S(1)}, bf16[224,1408]{1,0:T(8,128)(2,1)S(1)}, u32[]{:S(2)}, u32[]{:S(2)}) collective-permute-start(bf16[224,1408]{1,0:T(8,128)(2,1)S(1)} %get-tuple-element.128.mine_ref), channel_id=1, source_target_pairs={{0,16},{16,0},{1,17},{17,1},{2,18},{18,2},{3,19},{19,3},{4,20},{20... | collective-permute-start | bytes 1892360 | tf_op jit(solution)/shard_map/ppermute | solution.py:461
  49.5 2.3 %collective-permute-start.15 = (bf16[128,2176]{1,0:T(8,128)(2,1)S(1)}, bf16[128,2176]{1,0:T(8,128)(2,1)S(1)}, u32[]{:S(2)}, u32[]{:S(2)}) collective-permute-start(bf16[128,2176]{1,0:T(8,128)(2,1)S(1)} %collective-permute-done.11.refs_0_), channel_id=1, source_target_pairs={{0,1},{1,0},{2,3},{3,2},{4,5},{5,4},{6,7},{7,6},{8,9},{9,8},{10,11... | collective-permute-start | bytes 1671176 | tf_op jit(solution)/shard_map/ppermute | solution.py:451
  50.1 2.4 %collective-permute-start.16 = (bf16[128,2176]{1,0:T(8,128)(2,1)S(1)}, bf16[128,2176]{1,0:T(8,128)(2,1)S(1)}, u32[]{:S(2)}, u32[]{:S(2)}) collective-permute-start(bf16[128,2176]{1,0:T(8,128)(2,1)S(1)} %collective-permute-done.12.refs_2_), channel_id=1, source_target_pairs={{0,1},{1,0},{2,3},{3,2},{4,5},{5,4},{6,7},{7,6},{8,9},{9,8},{10,11... | collective-permute-start | bytes 1671176 | tf_op jit(solution)/shard_map/ppermute | solution.py:451
  50.1 6.5 %collective-permute-start.22 = (bf16[128,2048]{1,0:T(8,128)(2,1)S(1)}, bf16[128,2048]{1,0:T(8,128)(2,1)S(1)}, u32[]{:S(2)}, u32[]{:S(2)}) collective-permute-start(bf16[128,2048]{1,0:T(8,128)(2,1)S(1)} %get-tuple-element.153), channel_id=1, source_target_pairs={{0,1},{1,0},{2,3},{3,2},{4,5},{5,4},{6,7},{7,6},{8,9},{9,8},{10,11... | collective-permute-start | bytes 1572872 | tf_op jit(solution)/shard_map/ppermute | solution.py:471
  50.6 12.1 %collective-permute-start.13 = (bf16[128,2176]{1,0:T(8,128)(2,1)S(1)}, bf16[128,2176]{1,0:T(8,128)(2,1)S(1)}, u32[]{:S(2)}, u32[]{:S(2)}) collective-permute-start(bf16[128,2176]{1,0:T(8,128)(2,1)S(1)} %collective-permute-done.11.refs_0_), channel_id=1, source_target_pairs={{0,4},{2,0},{4,8},{6,2},{8,12},{10,6},{12,14},{14,10},{5,1},{1,3},... | collective-permute-start | bytes 1671176 | tf_op jit(solution)/shard_map/ppermute | solution.py:445
  54.9 16.6 %collective-permute-start.19 = (bf16[224,1408]{1,0:T(8,128)(2,1)S(1)}, bf16[224,1408]{1,0:T(8,128)(2,1)S(1)}, u32[]{:S(2)}, u32[]{:S(2)}) collective-permute-start(bf16[224,1408]{1,0:T(8,128)(2,1)S(1)} %get-tuple-element.142.mine_ref), channel_id=1, source_target_pairs={{0,16},{16,0},{1,17},{17,1},{2,18},{18,2},{3,19},{19,3},{4,20},{20... | collective-permute-start | bytes 1892360 | tf_op jit(solution)/shard_map/ppermute | solution.py:461
  56.8 9.2 %collective-permute-start.23 = (bf16[128,2048]{1,0:T(8,128)(2,1)S(1)}, bf16[128,2048]{1,0:T(8,128)(2,1)S(1)}, u32[]{:S(2)}, u32[]{:S(2)}) collective-permute-start(bf16[128,2048]{1,0:T(8,128)(2,1)S(1)} %add.16), channel_id=1, source_target_pairs={{0,4},{2,0},{4,8},{6,2},{8,12},{10,6},{12,14},{14,10},{5,1},{1,3},... | collective-permute-start | bytes 1572872 | tf_op jit(solution)/shard_map/ppermute | solution.py:476
  62.7 3.3 %collective-permute-start.21 = (bf16[128,2048]{1,0:T(8,128)(2,1)S(1)}, bf16[128,2048]{1,0:T(8,128)(2,1)S(1)}, u32[]{:S(2)}, u32[]{:S(2)}) collective-permute-start(bf16[128,2048]{1,0:T(8,128)(2,1)S(1)} %get-tuple-element.151), channel_id=1, source_target_pairs={{0,1},{1,0},{2,3},{3,2},{4,5},{5,4},{6,7},{7,6},{8,9},{9,8},{10,11... | collective-permute-start | bytes 1572872 | tf_op jit(solution)/shard_map/ppermute | solution.py:471
  62.8 5.0 %collective-permute-start.17 = (bf16[128,2176]{1,0:T(8,128)(2,1)S(1)}, bf16[128,2176]{1,0:T(8,128)(2,1)S(1)}, u32[]{:S(2)}, u32[]{:S(2)}) collective-permute-start(bf16[128,2176]{1,0:T(8,128)(2,1)S(1)} %collective-permute-done.13.refs_0_), channel_id=1, source_target_pairs={{0,1},{1,0},{2,3},{3,2},{4,5},{5,4},{6,7},{7,6},{8,9},{9,8},{10,11... | collective-permute-start | bytes 1671176 | tf_op jit(solution)/shard_map/ppermute | solution.py:451
  66.2 10.1 %collective-permute-start.24 = (bf16[128,2048]{1,0:T(8,128)(2,1)S(1)}, bf16[128,2048]{1,0:T(8,128)(2,1)S(1)}, u32[]{:S(2)}, u32[]{:S(2)}) collective-permute-start(bf16[128,2048]{1,0:T(8,128)(2,1)S(1)} %add.17), channel_id=1, source_target_pairs={{0,4},{2,0},{4,8},{6,2},{8,12},{10,6},{12,14},{14,10},{5,1},{1,3},... | collective-permute-start | bytes 1572872 | tf_op jit(solution)/shard_map/ppermute | solution.py:476
  70.0 8.3 %collective-permute-start.18 = (bf16[112,1408]{1,0:T(8,128)(2,1)S(1)}, bf16[112,1408]{1,0:T(8,128)(2,1)S(1)}, u32[]{:S(2)}, u32[]{:S(2)}) collective-permute-start(bf16[112,1408]{1,0:T(8,128)(2,1)S(1)} %get-tuple-element.160.mine_ref), channel_id=1, source_target_pairs={{0,16},{16,0},{1,17},{17,1},{2,18},{18,2},{3,19},{19,3},{4,20},{20... | collective-permute-start | bytes 946184 | tf_op jit(solution)/shard_map/ppermute | solution.py:461
  75.7 2.0 %collective-permute-start.20 = (bf16[128,2048]{1,0:T(8,128)(2,1)S(1)}, bf16[128,2048]{1,0:T(8,128)(2,1)S(1)}, u32[]{:S(2)}, u32[]{:S(2)}) collective-permute-start(bf16[128,2048]{1,0:T(8,128)(2,1)S(1)} %get-tuple-element.149), channel_id=1, source_target_pairs={{0,1},{1,0},{2,3},{3,2},{4,5},{5,4},{6,7},{7,6},{8,9},{9,8},{10,11... | collective-permute-start | bytes 1572872 | tf_op jit(solution)/shard_map/ppermute | solution.py:471
  75.8 20.5 %collective-permute-start.26 = (bf16[128,2048]{1,0:T(8,128)(2,1)S(1)}, bf16[128,2048]{1,0:T(8,128)(2,1)S(1)}, u32[]{:S(2)}, u32[]{:S(2)}) collective-permute-start(bf16[128,2048]{1,0:T(8,128)(2,1)S(1)} %get-tuple-element.157), channel_id=1, source_target_pairs={{0,1},{1,0},{2,3},{3,2},{4,5},{5,4},{6,7},{7,6},{8,9},{9,8},{10,11... | collective-permute-start | bytes 1572872 | tf_op jit(solution)/shard_map/ppermute | solution.py:471
  78.4 9.2 %collective-permute-start.28 = (bf16[128,2048]{1,0:T(8,128)(2,1)S(1)}, bf16[128,2048]{1,0:T(8,128)(2,1)S(1)}, u32[]{:S(2)}, u32[]{:S(2)}) collective-permute-start(bf16[128,2048]{1,0:T(8,128)(2,1)S(1)} %add.18), channel_id=1, source_target_pairs={{0,4},{2,0},{4,8},{6,2},{8,12},{10,6},{12,14},{14,10},{5,1},{1,3},... | collective-permute-start | bytes 1572872 | tf_op jit(solution)/shard_map/ppermute | solution.py:476
  84.0 3.6 %collective-permute-start.27 = (bf16[128,2048]{1,0:T(8,128)(2,1)S(1)}, bf16[128,2048]{1,0:T(8,128)(2,1)S(1)}, u32[]{:S(2)}, u32[]{:S(2)}) collective-permute-start(bf16[128,2048]{1,0:T(8,128)(2,1)S(1)} %get-tuple-element.165), channel_id=1, source_target_pairs={{0,1},{1,0},{2,3},{3,2},{4,5},{5,4},{6,7},{7,6},{8,9},{9,8},{10,11... | collective-permute-start | bytes 1572872 | tf_op jit(solution)/shard_map/ppermute | solution.py:471
  87.7 8.7 %collective-permute-start.32 = (bf16[128,1024]{1,0:T(8,128)(2,1)S(1)}, bf16[128,1024]{1,0:T(8,128)(2,1)S(1)}, u32[]{:S(2)}, u32[]{:S(2)}) collective-permute-start(bf16[128,1024]{1,0:T(8,128)(2,1)S(1)} %add.21), channel_id=1, source_target_pairs={{0,4},{2,0},{4,8},{6,2},{8,12},{10,6},{12,14},{14,10},{5,1},{1,3},... | collective-permute-start | bytes 786440 | tf_op jit(solution)/shard_map/ppermute | solution.py:476
  89.5 8.8 %collective-permute-start.29 = (bf16[128,1024]{1,0:T(8,128)(2,1)S(1)}, bf16[128,1024]{1,0:T(8,128)(2,1)S(1)}, u32[]{:S(2)}, u32[]{:S(2)}) collective-permute-start(bf16[128,1024]{1,0:T(8,128)(2,1)S(1)} %add.19.after_ref), channel_id=1, source_target_pairs={{0,4},{2,0},{4,8},{6,2},{8,12},{10,6},{12,14},{14,10},{5,1},{1,3},... | collective-permute-start | bytes 786440 | tf_op jit(solution)/shard_map/ppermute | solution.py:476
  90.2 8.8 %collective-permute-start.25 = (bf16[112,1408]{1,0:T(8,128)(2,1)S(1)}, bf16[112,1408]{1,0:T(8,128)(2,1)S(1)}, u32[]{:S(2)}, u32[]{:S(2)}) collective-permute-start(bf16[112,1408]{1,0:T(8,128)(2,1)S(1)} %get-tuple-element.155.mine_ref), channel_id=1, source_target_pairs={{0,16},{16,0},{1,17},{17,1},{2,18},{18,2},{3,19},{19,3},{4,20},{20... | collective-permute-start | bytes 946184 | tf_op jit(solution)/shard_map/ppermute | solution.py:461
  91.9 11.0 %collective-permute-start.31 = (bf16[128,2048]{1,0:T(8,128)(2,1)S(1)}, bf16[128,2048]{1,0:T(8,128)(2,1)S(1)}, u32[]{:S(2)}, u32[]{:S(2)}) collective-permute-start(bf16[128,2048]{1,0:T(8,128)(2,1)S(1)} %get-tuple-element.177), channel_id=1, source_target_pairs={{0,1},{1,0},{2,3},{3,2},{4,5},{5,4},{6,7},{7,6},{8,9},{9,8},{10,11... | collective-permute-start | bytes 1572872 | tf_op jit(solution)/shard_map/ppermute | solution.py:471
  96.5 6.4 %collective-permute-start.33 = (bf16[128,1024]{1,0:T(8,128)(2,1)S(1)}, bf16[128,1024]{1,0:T(8,128)(2,1)S(1)}, u32[]{:S(2)}, u32[]{:S(2)}) collective-permute-start(bf16[128,1024]{1,0:T(8,128)(2,1)S(1)} %add.22), channel_id=1, source_target_pairs={{0,4},{2,0},{4,8},{6,2},{8,12},{10,6},{12,14},{14,10},{5,1},{1,3},... | collective-permute-start | bytes 786440 | tf_op jit(solution)/shard_map/ppermute | solution.py:476
  99.0 6.7 %collective-permute-start.36 = (bf16[128,1024]{1,0:T(8,128)(2,1)S(1)}, bf16[128,1024]{1,0:T(8,128)(2,1)S(1)}, u32[]{:S(2)}, u32[]{:S(2)}) collective-permute-start(bf16[128,1024]{1,0:T(8,128)(2,1)S(1)} %add.20), channel_id=1, source_target_pairs={{0,4},{2,0},{4,8},{6,2},{8,12},{10,6},{12,14},{14,10},{5,1},{1,3},... | collective-permute-start | bytes 786440 | tf_op jit(solution)/shard_map/ppermute | solution.py:476
  100.3 11.3 %collective-permute-start.10 = (bf16[128,2048]{1,0:T(8,128)(2,1)S(1)}, bf16[128,2048]{1,0:T(8,128)(2,1)S(1)}, u32[]{:S(2)}, u32[]{:S(2)}) collective-permute-start(bf16[128,2048]{1,0:T(8,128)(2,1)S(1)} %get-tuple-element.124), channel_id=1, source_target_pairs={{0,1},{1,0},{2,3},{3,2},{4,5},{5,4},{6,7},{7,6},{8,9},{9,8},{10,11... | collective-permute-start | bytes 1572872 | tf_op jit(solution)/shard_map/ppermute | solution.py:471
  103.0 11.2 %collective-permute-start.34 = (bf16[128,1024]{1,0:T(8,128)(2,1)S(1)}, bf16[128,1024]{1,0:T(8,128)(2,1)S(1)}, u32[]{:S(2)}, u32[]{:S(2)}) collective-permute-start(bf16[128,1024]{1,0:T(8,128)(2,1)S(1)} %add.23), channel_id=1, source_target_pairs={{0,4},{2,0},{4,8},{6,2},{8,12},{10,6},{12,14},{14,10},{5,1},{1,3},... | collective-permute-start | bytes 786440 | tf_op jit(solution)/shard_map/ppermute | solution.py:476
  105.8 6.4 %collective-permute-start.37 = (bf16[128,1024]{1,0:T(8,128)(2,1)S(1)}, bf16[128,1024]{1,0:T(8,128)(2,1)S(1)}, u32[]{:S(2)}, u32[]{:S(2)}) collective-permute-start(bf16[128,1024]{1,0:T(8,128)(2,1)S(1)} %add.25), channel_id=1, source_target_pairs={{0,4},{2,0},{4,8},{6,2},{8,12},{10,6},{12,14},{14,10},{5,1},{1,3},... | collective-permute-start | bytes 786440 | tf_op jit(solution)/shard_map/ppermute | solution.py:476
  111.6 10.0 %collective-permute-start.30 = (bf16[128,2048]{1,0:T(8,128)(2,1)S(1)}, bf16[128,2048]{1,0:T(8,128)(2,1)S(1)}, u32[]{:S(2)}, u32[]{:S(2)}) collective-permute-start(bf16[128,2048]{1,0:T(8,128)(2,1)S(1)} %get-tuple-element.173), channel_id=1, source_target_pairs={{0,1},{1,0},{2,3},{3,2},{4,5},{5,4},{6,7},{7,6},{8,9},{9,8},{10,11... | collective-permute-start | bytes 1572872 | tf_op jit(solution)/shard_map/ppermute | solution.py:471
  112.3 8.2 %collective-permute-start.38 = (bf16[128,1024]{1,0:T(8,128)(2,1)S(1)}, bf16[128,1024]{1,0:T(8,128)(2,1)S(1)}, u32[]{:S(2)}, u32[]{:S(2)}) collective-permute-start(bf16[128,1024]{1,0:T(8,128)(2,1)S(1)} %add.26), channel_id=1, source_target_pairs={{0,4},{2,0},{4,8},{6,2},{8,12},{10,6},{12,14},{14,10},{5,1},{1,3},... | collective-permute-start | bytes 786440 | tf_op jit(solution)/shard_map/ppermute | solution.py:544
  114.3 7.3 %collective-permute-start.35 = (bf16[128,1024]{1,0:T(8,128)(2,1)S(1)}, bf16[128,1024]{1,0:T(8,128)(2,1)S(1)}, u32[]{:S(2)}, u32[]{:S(2)}) collective-permute-start(bf16[128,1024]{1,0:T(8,128)(2,1)S(1)} %add.24.after_ref), channel_id=1, source_target_pairs={{0,4},{2,0},{4,8},{6,2},{8,12},{10,6},{12,14},{14,10},{5,1},{1,3},... | collective-permute-start | bytes 786440 | tf_op jit(solution)/shard_map/ppermute | solution.py:544

commit v4 on v3

--- a/solution.py
+++ b/solution.py
@@ -491,6 +491,7 @@
 
     last = (0,)
     pass_on(stages[0])
+    rows[0], ids = tie((rows[0], ids))
     share(last)
     every = take(last)
     ids, partial[last] = tie((ids, partial[last]))

time: 123 us -> 124 us (level)
  transfers between devices with their start and end apart: 39 -> 39, of which waited for: 17 -> 17; matrix products, arithmetic and copies ran while one was open for 1% -> 0% of each run, Pallas kernels for 52% -> 52%
where the time goes in v4:
time: 124 us; the launch traced here: 123 us
  Pallas kernels  66.1 us (53%)
  starting transfers between devices  38.1 us (31%)
  waiting for transfers between devices  17.5 us (14%)
    pallas_call x5, Pallas kernels, give_rows(): pl.pallas_call(functools.partial(give_kernel, count, first), in_specs=[VM...  20.6 us
    ppermute x9, starting transfers between devices, collect(): lax.ppermute(part, 'expert', ring)  14.1 us
    pallas_call x2, Pallas kernels, prep(): pl.pallas_call(functools.partial(prep_kernel, capacity, tiles[0]), grid_s...  12 us
    pallas_call x5, Pallas kernels, take_rows(): pl.pallas_call(functools.partial(take_kernel, experts, count, first), in_...  11.8 us
    ppermute x9, waiting for transfers between devices, collect(): lax.ppermute(part, 'expert', ring)  10.2 us
    pallas_call x3, Pallas kernels, hold(): pl.pallas_call(hold_kernel, in_specs=[ANY] * (1 + len(after)), out_specs=...  9.12 us
    pallas_call x2, Pallas kernels, grad_rows(): pl.pallas_call(grad_kernel, grid=(2,), in_specs=[pl.BlockSpec((rows, slot...  8.9 us
    ppermute x5, starting transfers between devices, trade(): theirs[stage] = lax.ppermute(partial[stage], 'dp', swap)  8.01 us
  transfers between devices with their start and end apart: 39, of which 17 were waited for; matrix products, arithmetic and copies ran while one was open for 0% of the time, Pallas kernels for 52%

profile of v4, /device:TPU:0, one launch (start us, length us, event | category | flops | bytes accessed | tf_op | source)
XLA Modules:
  0.0 123.3 jit_solution(10877999060716159806)
XLA Ops:
  0.6 0.7 dynamic-slice_bitcast_fusion.refs_1_.ids_ref
  1.3 1.3 %pack.1.refs_0_ = bf16[128,2176]{1,0:T(8,128)(2,1)S(1)} custom-call(bf16[128,2048]{1,0:T(8,128)(2,1)} %rows_ref.1, s32[6,128]{1,0:T(8,128)} %bitcast.20, f32[6,128]{1,0:T(8,128)} %bitcast.21, f32[1,128]{1,0:T(1,128)} %bitcast.22), custom_call_target="tpu_custom_call" | custom-call | tf_op jit(solution)/shard_map/pack/pallas_call | solution.py:134
  2.7 0.5 collective-permute-start
  3.2 2.6 %collective-permute-start.1 = (bf16[128,2176]{1,0:T(8,128)(2,1)S(1)}, bf16[128,2176]{1,0:T(8,128)(2,1)S(1)}, u32[]{:S(2)}, u32[]{:S(2)}) collective-permute-start(bf16[128,2176]{1,0:T(8,128)(2,1)S(1)} %pack.1.refs_0_), channel_id=1, source_target_pairs={{0,4},{2,0},{4,8},{6,2},{8,12},{10,6},{12,14},{14,10},{5,1},{1,3},... | collective-permute-start | bytes 1671176 | tf_op jit(solution)/shard_map/ppermute | solution.py:445
  5.8 3.2 %hold.3 = (bf16[1408,2048]{1,0:T(8,128)(2,1)S(1)}, f32[8,128]{1,0:T(8,128)}) custom-call(bf16[1408,2048]{1,0:T(8,128)(2,1)} %bitcast.17, bf16[128,2176]{1,0:T(8,128)(2,1)S(1)} %pack.1.refs_0_, s32[16]{0:T(128)S(1)} %dynamic-slice_bitcast_fusion.refs_1_.ids_ref), custom_call_target="tpu_custom_call" | custom-call | tf_op jit(solution)/shard_map/hold/pallas_call | solution.py:206
  9.1 2.2 %take.5 = (bf16[896,2048]{1,0:T(8,128)(2,1)S(1)}, bf16[112,1408]{1,0:T(8,128)(2,1)S(1)}, bf16[128,56]{1,0:T(8,128)(2,1)S(1)}, bf16[128,56]{1,0:T(8,128)(2,1)S(1)}) custom-call(s32[1]{0:T(128)} %bitcast.4.me_ref, bf16[1408,2048]{1,0:T(8,128)(2,1)S(1)} %get-tuple-element.94.wdown_ref, bf16[128,2176]{1,0:T(8,128)(2,1)S(1)} %pack.1.refs_0_, ...), custom_call_target="tpu_custom_call" | custom-call | tf_op jit(solution)/shard_map/take/pallas_call | solution.py:252
  11.4 6.4 %prep.2 = (bf16[896,1408]{1,0:T(8,128)(2,1)S(1)}, bf16[896,1408]{1,0:T(8,128)(2,1)S(1)}, bf16[1408,896]{1,0:T(8,128)(2,1)S(1)}, f32[8,128]{1,0:T(8,128)S(1)}) custom-call(s32[16]{0:T(128)S(1)} %dynamic-slice_bitcast_fusion.refs_1_.ids_ref, bf16[1408,896]{1,0:T(8,128)(2,1)} %bitcast.13, bf16[1408,896]{1,0:T(8,128)(2,1)} %bitcast.15), custom_call_target="tpu_custom_call" | custom-call | flops 6881280 | bytes 6881280 | tf_op jit(solution)/shard_map/prep/pallas_call | solution.py:173
  17.8 0.6 collective-permute-done.1.refs_0_
  18.3 0.7 collective-permute-done.2.refs_2_
  19.2 0.4 collective-permute-start.4
  19.6 1.8 %collective-permute-start.6 = (bf16[128,2176]{1,0:T(8,128)(2,1)S(1)}, bf16[128,2176]{1,0:T(8,128)(2,1)S(1)}, u32[]{:S(2)}, u32[]{:S(2)}) collective-permute-start(bf16[128,2176]{1,0:T(8,128)(2,1)S(1)} %collective-permute-done.1.refs_0_), channel_id=1, source_target_pairs={{0,4},{2,0},{4,8},{6,2},{8,12},{10,6},{12,14},{14,10},{5,1},{1,3},... | collective-permute-start | bytes 1671176 | tf_op jit(solution)/shard_map/ppermute | solution.py:445
  21.8 2.4 %take.6 = (bf16[896,2048]{1,0:T(8,128)(2,1)S(1)}, bf16[224,1408]{1,0:T(8,128)(2,1)S(1)}, bf16[128,56]{1,0:T(8,128)(2,1)S(1)}, bf16[128,56]{1,0:T(8,128)(2,1)S(1)...) custom-call(s32[1]{0:T(128)} %bitcast.4.me_ref, ...), custom_call_target="tpu_custom_call", output_to_operand_aliasing={{0}: (6, {})} | custom-call | tf_op jit(solution)/shard_map/take/pallas_call | solution.py:252
  24.2 1.7 %collective-permute-start.5 = (bf16[224,1408]{1,0:T(8,128)(2,1)S(1)}, bf16[224,1408]{1,0:T(8,128)(2,1)S(1)}, u32[]{:S(2)}, u32[]{:S(2)}) collective-permute-start(bf16[224,1408]{1,0:T(8,128)(2,1)S(1)} %get-tuple-element.105.mine_ref), channel_id=1, source_target_pairs={{0,16},{16,0},{1,17},{17,1},{2,18},{18,2},{3,19},{19,3},{4,20},{20... | collective-permute-start | bytes 1892360 | tf_op jit(solution)/shard_map/ppermute | solution.py:461
  26.0 5.6 %prep.3 = (bf16[896,1408]{1,0:T(8,128)(2,1)S(1)}, bf16[896,1408]{1,0:T(8,128)(2,1)S(1)}, bf16[1408,896]{1,0:T(8,128)(2,1)S(1)}, f32[8,128]{1,0:T(8,128)S(1)}) custom-call(s32[16]{0:T(128)S(1)} %dynamic-slice_bitcast_fusion.refs_1_.ids_ref, bf16[1408,896]{1,0:T(8,128)(2,1)} %bitcast.14, ...), custom_call_target="tpu_custom_call", output_to_operand_aliasing={{0}: (3, {}), {1}: (4, {}), {2}: (5, {})} | custom-call | flops 5734400 | bytes 5734400 | tf_op jit(solution)/shard_map/prep/pallas_call | solution.py:173
  31.6 2.6 %hold.4 = (bf16[2048,1408]{1,0:T(8,128)(2,1)S(1)}, f32[8,128]{1,0:T(8,128)S(1)}) custom-call(bf16[2048,1408]{1,0:T(8,128)(2,1)} %bitcast.18, f32[8,128]{1,0:T(8,128)S(1)} %get-tuple-element.106.refs_0_, f32[8,128]{1,0:T(8,128)S(1)} %get-tuple-element.111.refs_1_), custom_call_target="tpu_custom_call" | custom-call | tf_op jit(solution)/shard_map/hold/pallas_call | solution.py:206
  34.3 0.9 collective-permute-start.8
  35.2 1.5 %collective-permute-start.11 = (bf16[128,2176]{1,0:T(8,128)(2,1)S(1)}, bf16[128,2176]{1,0:T(8,128)(2,1)S(1)}, u32[]{:S(2)}, u32[]{:S(2)}) collective-permute-start(bf16[128,2176]{1,0:T(8,128)(2,1)S(1)} %collective-permute-done.6.refs_0_), channel_id=1, source_target_pairs={{0,4},{2,0},{4,8},{6,2},{8,12},{10,6},{12,14},{14,10},{5,1},{1,3},... | collective-permute-start | bytes 1671176 | tf_op jit(solution)/shard_map/ppermute | solution.py:445
  36.6 0.6 collective-permute-start.12
  37.2 0.3 collective-permute-done.9.refs_3_
  37.6 2.4 %take.7 = (bf16[896,2048]{1,0:T(8,128)(2,1)S(1)}, bf16[224,1408]{1,0:T(8,128)(2,1)S(1)}, bf16[128,56]{1,0:T(8,128)(2,1)S(1)}, bf16[128,56]{1,0:T(8,128)(2,1)S(1)...) custom-call(s32[1]{0:T(128)} %bitcast.4.me_ref, ...), custom_call_target="tpu_custom_call", output_to_operand_aliasing={{0}: (6, {})} | custom-call | tf_op jit(solution)/shard_map/take/pallas_call | solution.py:252
  40.0 1.7 %collective-permute-start.14 = (bf16[224,1408]{1,0:T(8,128)(2,1)S(1)}, bf16[224,1408]{1,0:T(8,128)(2,1)S(1)}, u32[]{:S(2)}, u32[]{:S(2)}) collective-permute-start(bf16[224,1408]{1,0:T(8,128)(2,1)S(1)} %get-tuple-element.132.mine_ref), channel_id=1, source_target_pairs={{0,16},{16,0},{1,17},{17,1},{2,18},{18,2},{3,19},{19,3},{4,20},{20... | collective-permute-start | bytes 1892360 | tf_op jit(solution)/shard_map/ppermute | solution.py:461
  41.7 3.2 %hold.5 = (bf16[2048,1408]{1,0:T(8,128)(2,1)S(1)}, f32[8,128]{1,0:T(8,128)}) custom-call(bf16[2048,1408]{1,0:T(8,128)(2,1)} %bitcast.19, bf16[128,56]{1,0:T(8,128)(2,1)S(1)} %get-tuple-element.121.refs_0_, f32[8,128]{1,0:T(8,128)S(1)} %get-tuple-element.122.refs_1_), custom_call_target="tpu_custom_call" | custom-call | tf_op jit(solution)/shard_map/hold/pallas_call | solution.py:206
  45.0 4.3 %give.5 = (bf16[128,2048]{1,0:T(8,128)(2,1)S(1)}, bf16[128,2048]{1,0:T(8,128)(2,1)S(1)}, bf16[128,2048]{1,0:T(8,128)(2,1)S(1)}, bf16[128,2048]{1,0:T(8,128)(2,1)S(1)}) custom-call(bf16[224,1408]{1,0:T(8,128)(2,1)S(1)} %get-tuple-element.105.mine_ref, bf16[224,1408]{1,0:T(8,128)(2,1)S(1)} %mark.17.theirs_ref, ...), custom_call_target="tpu_custom_call" | custom-call | tf_op jit(solution)/shard_map/give/pallas_call | solution.py:292
  49.3 0.5 collective-permute-done.11.refs_0_
  49.7 0.5 collective-permute-done.12.refs_2_
  50.2 0.6 collective-permute-start.15
  50.8 0.5 collective-permute-start.22
  51.3 1.2 collective-permute-start.13
  52.5 0.7 collective-permute-done.16.refs_3_
  53.2 2.4 %take.8 = (bf16[896,2048]{1,0:T(8,128)(2,1)S(1)}, bf16[224,1408]{1,0:T(8,128)(2,1)S(1)}, bf16[128,56]{1,0:T(8,128)(2,1)S(1)}, bf16[128,56]{1,0:T(8,128)(2,1)S(1)...) custom-call(s32[1]{0:T(128)} %bitcast.4.me_ref, ...), custom_call_target="tpu_custom_call", output_to_operand_aliasing={{0}: (6, {})} | custom-call | tf_op jit(solution)/shard_map/take/pallas_call | solution.py:252
  55.6 1.7 %collective-permute-start.19 = (bf16[224,1408]{1,0:T(8,128)(2,1)S(1)}, bf16[224,1408]{1,0:T(8,128)(2,1)S(1)}, u32[]{:S(2)}, u32[]{:S(2)}) collective-permute-start(bf16[224,1408]{1,0:T(8,128)(2,1)S(1)} %get-tuple-element.146.mine_ref), channel_id=1, source_target_pairs={{0,16},{16,0},{1,17},{17,1},{2,18},{18,2},{3,19},{19,3},{4,20},{20... | collective-permute-start | bytes 1892360 | tf_op jit(solution)/shard_map/ppermute | solution.py:461
  57.5 1.6 %collective-permute-start.23 = (bf16[128,2048]{1,0:T(8,128)(2,1)S(1)}, bf16[128,2048]{1,0:T(8,128)(2,1)S(1)}, u32[]{:S(2)}, u32[]{:S(2)}) collective-permute-start(bf16[128,2048]{1,0:T(8,128)(2,1)S(1)} %add.16), channel_id=1, source_target_pairs={{0,4},{2,0},{4,8},{6,2},{8,12},{10,6},{12,14},{14,10},{5,1},{1,3},... | collective-permute-start | bytes 1572872 | tf_op jit(solution)/shard_map/ppermute | solution.py:476
  59.1 4.3 %give.6 = (bf16[128,2048]{1,0:T(8,128)(2,1)S(1)}, bf16[128,2048]{1,0:T(8,128)(2,1)S(1)}, bf16[128,2048]{1,0:T(8,128)(2,1)S(1)}, bf16[128,2048]{1,0:T(8,128)(2,1)S(1)}) custom-call(bf16[224,1408]{1,0:T(8,128)(2,1)S(1)} %get-tuple-element.132.mine_ref, bf16[224,1408]{1,0:T(8,128)(2,1)S(1)} %mark.18.theirs_ref, ...), custom_call_target="tpu_custom_call" | custom-call | tf_op jit(solution)/shard_map/give/pallas_call | solution.py:292
  63.4 0.5 collective-permute-start.17
  63.9 2.8 %collective-permute-done.23.old_ref = bf16[128,2048]{1,0:T(8,128)(2,1)S(1)} collective-permute-done((bf16[128,2048]{1,0:T(8,128)(2,1)S(1)}, bf16[128,2048]{1,0:T(8,128)(2,1)S(1)}, u32[]{:S(2)}, u32[]{:S(2)}) %collective-permute-start.23) | collective-permute-done | bytes 524320 | tf_op jit(solution)/shard_map/ppermute | solution.py:476
  66.9 1.6 %collective-permute-start.24 = (bf16[128,2048]{1,0:T(8,128)(2,1)S(1)}, bf16[128,2048]{1,0:T(8,128)(2,1)S(1)}, u32[]{:S(2)}, u32[]{:S(2)}) collective-permute-start(bf16[128,2048]{1,0:T(8,128)(2,1)S(1)} %add.17), channel_id=1, source_target_pairs={{0,4},{2,0},{4,8},{6,2},{8,12},{10,6},{12,14},{14,10},{5,1},{1,3},... | collective-permute-start | bytes 1572872 | tf_op jit(solution)/shard_map/ppermute | solution.py:476
  68.5 2.2 %take.9 = (bf16[896,2048]{1,0:T(8,128)(2,1)S(1)}, bf16[112,1408]{1,0:T(8,128)(2,1)S(1)}, bf16[128,56]{1,0:T(8,128)(2,1)S(1)}, bf16[128,56]{1,0:T(8,128)(2,1)S(1)}) custom-call(s32[1]{0:T(128)} %bitcast.4.me_ref, bf16[1408,2048]{1,0:T(8,128)(2,1)S(1)} %get-tuple-element.94.wdown_ref, ...), custom_call_target="tpu_custom_call", output_to_operand_aliasing={{0}: (4, {})} | custom-call | tf_op jit(solution)/shard_map/take/pallas_call | solution.py:252
  70.7 1.1 collective-permute-start.18
  71.9 0.3 collective-permute-done.19.old_ref
  72.2 4.3 %give.7 = (bf16[128,2048]{1,0:T(8,128)(2,1)S(1)}, bf16[128,2048]{1,0:T(8,128)(2,1)S(1)}, bf16[128,2048]{1,0:T(8,128)(2,1)S(1)}, bf16[128,2048]{1,0:T(8,128)(2,1)S(1)}) custom-call(bf16[224,1408]{1,0:T(8,128)(2,1)S(1)} %get-tuple-element.146.mine_ref, bf16[224,1408]{1,0:T(8,128)(2,1)S(1)} %mark.19.theirs_ref, ...), custom_call_target="tpu_custom_call" | custom-call | tf_op jit(solution)/shard_map/give/pallas_call | solution.py:292
  76.5 0.5 collective-permute-start.26
  77.0 1.4 %collective-permute-done.20.given_ref = bf16[128,2048]{1,0:T(8,128)(2,1)S(1)} collective-permute-done((bf16[128,2048]{1,0:T(8,128)(2,1)S(1)}, bf16[128,2048]{1,0:T(8,128)(2,1)S(1)}, u32[]{:S(2)}, u32[]{:S(2)}) %collective-permute-start.20) | collective-permute-done | bytes 524320 | tf_op jit(solution)/shard_map/ppermute | solution.py:471
  78.6 0.5 collective-permute-done.18.old_ref
  79.1 1.7 %collective-permute-start.28 = (bf16[128,2048]{1,0:T(8,128)(2,1)S(1)}, bf16[128,2048]{1,0:T(8,128)(2,1)S(1)}, u32[]{:S(2)}, u32[]{:S(2)}) collective-permute-start(bf16[128,2048]{1,0:T(8,128)(2,1)S(1)} %add.18), channel_id=1, source_target_pairs={{0,4},{2,0},{4,8},{6,2},{8,12},{10,6},{12,14},{14,10},{5,1},{1,3},... | collective-permute-start | bytes 1572872 | tf_op jit(solution)/shard_map/ppermute | solution.py:476
  80.8 3.9 %give.8 = (bf16[128,2048]{1,0:T(8,128)(2,1)S(1)}, bf16[128,2048]{1,0:T(8,128)(2,1)S(1)}) custom-call(bf16[112,1408]{1,0:T(8,128)(2,1)S(1)} %get-tuple-element.164.mine_ref, bf16[112,1408]{1,0:T(8,128)(2,1)S(1)} %mark.22.theirs_ref, bf16[896,1408]{1,0:T(8,128)(2,1)S(1)} %get-tuple-element.118.to_gate_ref, bf16[896,1408]{1,0:T(8,128)(2,1)S(1)} %get-tuple-element.119.to_up_ref, ...), custom_call_target="tpu_custom_call" | custom-call | tf_op jit(solution)/shard_map/give/pallas_call | solution.py:292
  84.8 3.5 %collective-permute-done.28.old_ref = bf16[128,2048]{1,0:T(8,128)(2,1)S(1)} collective-permute-done((bf16[128,2048]{1,0:T(8,128)(2,1)S(1)}, bf16[128,2048]{1,0:T(8,128)(2,1)S(1)}, u32[]{:S(2)}, u32[]{:S(2)}) %collective-permute-start.28) | collective-permute-done | bytes 524320 | tf_op jit(solution)/shard_map/ppermute | solution.py:476
  88.4 1.7 %collective-permute-start.32 = (bf16[128,1024]{1,0:T(8,128)(2,1)S(1)}, bf16[128,1024]{1,0:T(8,128)(2,1)S(1)}, u32[]{:S(2)}, u32[]{:S(2)}) collective-permute-start(bf16[128,1024]{1,0:T(8,128)(2,1)S(1)} %add.21), channel_id=1, source_target_pairs={{0,4},{2,0},{4,8},{6,2},{8,12},{10,6},{12,14},{14,10},{5,1},{1,3},... | collective-permute-start | bytes 786440 | tf_op jit(solution)/shard_map/ppermute | solution.py:476
  90.2 0.7 collective-permute-start.29
  90.9 1.7 %collective-permute-start.25 = (bf16[112,1408]{1,0:T(8,128)(2,1)S(1)}, bf16[112,1408]{1,0:T(8,128)(2,1)S(1)}, u32[]{:S(2)}, u32[]{:S(2)}) collective-permute-start(bf16[112,1408]{1,0:T(8,128)(2,1)S(1)} %get-tuple-element.159.mine_ref), channel_id=1, source_target_pairs={{0,16},{16,0},{1,17},{17,1},{2,18},{18,2},{3,19},{19,3},{4,20},{20... | collective-permute-start | bytes 946184 | tf_op jit(solution)/shard_map/ppermute | solution.py:461
  92.6 4.4 %grad_down.2.refs_0_ = bf16[1408,2048]{1,0:T(8,128)(2,1)} custom-call(bf16[1408,896]{1,0:T(8,128)(2,1)S(1)} %get-tuple-element.162.hidden_ref, bf16[896,2048]{1,0:T(8,128)(2,1)S(1)} %get-tuple-element.163.every_ref, bf16[128,1024]{1,0:T(8,128)(2,1)S(1)} %add.19.after_ref), custom_call_target="tpu_custom_call" | custom-call | tf_op jit(solution)/shard_map/grad_down/pallas_call | solution.py:336
  97.2 1.9 %collective-permute-start.33 = (bf16[128,1024]{1,0:T(8,128)(2,1)S(1)}, bf16[128,1024]{1,0:T(8,128)(2,1)S(1)}, u32[]{:S(2)}, u32[]{:S(2)}) collective-permute-start(bf16[128,1024]{1,0:T(8,128)(2,1)S(1)} %add.22), channel_id=1, source_target_pairs={{0,4},{2,0},{4,8},{6,2},{8,12},{10,6},{12,14},{14,10},{5,1},{1,3},... | collective-permute-start | bytes 786440 | tf_op jit(solution)/shard_map/ppermute | solution.py:476
  99.1 0.6 collective-permute-done.25.old_ref
  99.7 1.2 %collective-permute-start.36 = (bf16[128,1024]{1,0:T(8,128)(2,1)S(1)}, bf16[128,1024]{1,0:T(8,128)(2,1)S(1)}, u32[]{:S(2)}, u32[]{:S(2)}) collective-permute-start(bf16[128,1024]{1,0:T(8,128)(2,1)S(1)} %add.20), channel_id=1, source_target_pairs={{0,4},{2,0},{4,8},{6,2},{8,12},{10,6},{12,14},{14,10},{5,1},{1,3},... | collective-permute-start | bytes 786440 | tf_op jit(solution)/shard_map/ppermute | solution.py:476
  101.1 2.5 %collective-permute-done.33.old_ref = bf16[128,1024]{1,0:T(8,128)(2,1)S(1)} collective-permute-done((bf16[128,1024]{1,0:T(8,128)(2,1)S(1)}, bf16[128,1024]{1,0:T(8,128)(2,1)S(1)}, u32[]{:S(2)}, u32[]{:S(2)}) %collective-permute-start.33) | collective-permute-done | bytes 262176 | tf_op jit(solution)/shard_map/ppermute | solution.py:476
  103.7 1.9 %collective-permute-start.34 = (bf16[128,1024]{1,0:T(8,128)(2,1)S(1)}, bf16[128,1024]{1,0:T(8,128)(2,1)S(1)}, u32[]{:S(2)}, u32[]{:S(2)}) collective-permute-start(bf16[128,1024]{1,0:T(8,128)(2,1)S(1)} %add.23), channel_id=1, source_target_pairs={{0,4},{2,0},{4,8},{6,2},{8,12},{10,6},{12,14},{14,10},{5,1},{1,3},... | collective-permute-start | bytes 786440 | tf_op jit(solution)/shard_map/ppermute | solution.py:476
  105.5 0.8 collective-permute-done.36.old_ref
  106.5 1.9 %collective-permute-start.37 = (bf16[128,1024]{1,0:T(8,128)(2,1)S(1)}, bf16[128,1024]{1,0:T(8,128)(2,1)S(1)}, u32[]{:S(2)}, u32[]{:S(2)}) collective-permute-start(bf16[128,1024]{1,0:T(8,128)(2,1)S(1)} %add.25), channel_id=1, source_target_pairs={{0,4},{2,0},{4,8},{6,2},{8,12},{10,6},{12,14},{14,10},{5,1},{1,3},... | collective-permute-start | bytes 786440 | tf_op jit(solution)/shard_map/ppermute | solution.py:476
  108.4 3.9 %give.9 = (bf16[128,2048]{1,0:T(8,128)(2,1)S(1)}, bf16[128,2048]{1,0:T(8,128)(2,1)S(1)}) custom-call(bf16[112,1408]{1,0:T(8,128)(2,1)S(1)} %get-tuple-element.159.mine_ref, bf16[112,1408]{1,0:T(8,128)(2,1)S(1)} %mark.26.theirs_ref, bf16[896,1408]{1,0:T(8,128)(2,1)S(1)} %get-tuple-element.118.to_gate_ref, bf16[896,1408]{1,0:T(8,128)(2,1)S(1)} %get-tuple-element.119.to_up_ref, ...), custom_call_target="tpu_custom_call" | custom-call | tf_op jit(solution)/shard_map/give/pallas_call | solution.py:292
  112.4 0.6 collective-permute-done.37.old_ref
  113.0 1.9 %collective-permute-start.38 = (bf16[128,1024]{1,0:T(8,128)(2,1)S(1)}, bf16[128,1024]{1,0:T(8,128)(2,1)S(1)}, u32[]{:S(2)}, u32[]{:S(2)}) collective-permute-start(bf16[128,1024]{1,0:T(8,128)(2,1)S(1)} %add.26), channel_id=1, source_target_pairs={{0,4},{2,0},{4,8},{6,2},{8,12},{10,6},{12,14},{14,10},{5,1},{1,3},... | collective-permute-start | bytes 786440 | tf_op jit(solution)/shard_map/ppermute | solution.py:545
  115.0 1.8 %collective-permute-start.35 = (bf16[128,1024]{1,0:T(8,128)(2,1)S(1)}, bf16[128,1024]{1,0:T(8,128)(2,1)S(1)}, u32[]{:S(2)}, u32[]{:S(2)}) collective-permute-start(bf16[128,1024]{1,0:T(8,128)(2,1)S(1)} %add.24.after_ref), channel_id=1, source_target_pairs={{0,4},{2,0},{4,8},{6,2},{8,12},{10,6},{12,14},{14,10},{5,1},{1,3},... | collective-permute-start | bytes 786440 | tf_op jit(solution)/shard_map/ppermute | solution.py:545
  116.8 4.4 %grad_down.3 = bf16[1408,2048]{1,0:T(8,128)(2,1)} custom-call(bf16[1408,896]{1,0:T(8,128)(2,1)S(1)} %get-tuple-element.162.hidden_ref, bf16[896,2048]{1,0:T(8,128)(2,1)S(1)} %get-tuple-element.163.every_ref, bf16[128,1024]{1,0:T(8,128)(2,1)S(1)} %add.24.after_ref, bf16[1408,2048]{1,0:T(8,128)(2,1)} %grad_down.2.refs_0_), custom_call_target="tpu_custom_call", output_to_operand_aliasing={{}: (3, {})} | custom-call | tf_op jit(solution)/shard_map/grad_down/pallas_call | solution.py:336
  121.3 1.0 collective-permute-done.35.old_ref
  122.3 1.0 add.27
  (62 shorter events, 2.5 us)
Async XLA Ops:
  2.7 6.4 %collective-permute-start = (bf16[128,2176]{1,0:T(8,128)(2,1)S(1)}, bf16[128,2176]{1,0:T(8,128)(2,1)S(1)}, u32[]{:S(2)}, u32[]{:S(2)}) collective-permute-start(bf16[128,2176]{1,0:T(8,128)(2,1)S(1)} %pack.1.refs_0_), channel_id=1, source_target_pairs={{0,1},{1,0},{2,3},{3,2},{4,5},{5,4},{6,7},{7,6},{8,9},{9,8},{10,11... | collective-permute-start | bytes 1671176 | tf_op jit(solution)/shard_map/ppermute | solution.py:451
  3.2 15.1 %collective-permute-start.1 = (bf16[128,2176]{1,0:T(8,128)(2,1)S(1)}, bf16[128,2176]{1,0:T(8,128)(2,1)S(1)}, u32[]{:S(2)}, u32[]{:S(2)}) collective-permute-start(bf16[128,2176]{1,0:T(8,128)(2,1)S(1)} %pack.1.refs_0_), channel_id=1, source_target_pairs={{0,4},{2,0},{4,8},{6,2},{8,12},{10,6},{12,14},{14,10},{5,1},{1,3},... | collective-permute-start | bytes 1671176 | tf_op jit(solution)/shard_map/ppermute | solution.py:445
  5.8 13.2 %collective-permute-start.2 = (bf16[128,2176]{1,0:T(8,128)(2,1)S(1)}, bf16[128,2176]{1,0:T(8,128)(2,1)S(1)}, u32[]{:S(2)}, u32[]{:S(2)}) collective-permute-start(bf16[128,2176]{1,0:T(8,128)(2,1)S(1)} %pack.1.refs_0_), channel_id=1, source_target_pairs={{4,0},{0,2},{8,4},{2,6},{12,8},{6,10},{14,12},{10,14},{1,5},{3,1},... | collective-permute-start | bytes 1671176 | tf_op jit(solution)/shard_map/ppermute | solution.py:447
  19.1 2.5 %collective-permute-start.3 = (bf16[128,2176]{1,0:T(8,128)(2,1)S(1)}, bf16[128,2176]{1,0:T(8,128)(2,1)S(1)}, u32[]{:S(2)}, u32[]{:S(2)}) collective-permute-start(bf16[128,2176]{1,0:T(8,128)(2,1)S(1)} %collective-permute-done.1.refs_0_), channel_id=1, source_target_pairs={{0,1},{1,0},{2,3},{3,2},{4,5},{5,4},{6,7},{7,6},{8,9},{9,8},{10,11... | collective-permute-start | bytes 1671176 | tf_op jit(solution)/shard_map/ppermute | solution.py:451
  19.2 2.6 %collective-permute-start.4 = (bf16[128,2176]{1,0:T(8,128)(2,1)S(1)}, bf16[128,2176]{1,0:T(8,128)(2,1)S(1)}, u32[]{:S(2)}, u32[]{:S(2)}) collective-permute-start(bf16[128,2176]{1,0:T(8,128)(2,1)S(1)} %collective-permute-done.2.refs_2_), channel_id=1, source_target_pairs={{0,1},{1,0},{2,3},{3,2},{4,5},{5,4},{6,7},{7,6},{8,9},{9,8},{10,11... | collective-permute-start | bytes 1671176 | tf_op jit(solution)/shard_map/ppermute | solution.py:451
  19.6 14.7 %collective-permute-start.6 = (bf16[128,2176]{1,0:T(8,128)(2,1)S(1)}, bf16[128,2176]{1,0:T(8,128)(2,1)S(1)}, u32[]{:S(2)}, u32[]{:S(2)}) collective-permute-start(bf16[128,2176]{1,0:T(8,128)(2,1)S(1)} %collective-permute-done.1.refs_0_), channel_id=1, source_target_pairs={{0,4},{2,0},{4,8},{6,2},{8,12},{10,6},{12,14},{14,10},{5,1},{1,3},... | collective-permute-start | bytes 1671176 | tf_op jit(solution)/shard_map/ppermute | solution.py:445
  21.3 13.0 %collective-permute-start.7 = (bf16[128,2176]{1,0:T(8,128)(2,1)S(1)}, bf16[128,2176]{1,0:T(8,128)(2,1)S(1)}, u32[]{:S(2)}, u32[]{:S(2)}) collective-permute-start(bf16[128,2176]{1,0:T(8,128)(2,1)S(1)} %collective-permute-done.2.refs_2_), channel_id=1, source_target_pairs={{4,0},{0,2},{8,4},{2,6},{12,8},{6,10},{14,12},{10,14},{1,5},{3,1},... | collective-permute-start | bytes 1671176 | tf_op jit(solution)/shard_map/ppermute | solution.py:447
  24.2 20.7 %collective-permute-start.5 = (bf16[224,1408]{1,0:T(8,128)(2,1)S(1)}, bf16[224,1408]{1,0:T(8,128)(2,1)S(1)}, u32[]{:S(2)}, u32[]{:S(2)}) collective-permute-start(bf16[224,1408]{1,0:T(8,128)(2,1)S(1)} %get-tuple-element.105.mine_ref), channel_id=1, source_target_pairs={{0,16},{16,0},{1,17},{17,1},{2,18},{18,2},{3,19},{19,3},{4,20},{20... | collective-permute-start | bytes 1892360 | tf_op jit(solution)/shard_map/ppermute | solution.py:461
  34.3 2.9 %collective-permute-start.8 = (bf16[128,2176]{1,0:T(8,128)(2,1)S(1)}, bf16[128,2176]{1,0:T(8,128)(2,1)S(1)}, u32[]{:S(2)}, u32[]{:S(2)}) collective-permute-start(bf16[128,2176]{1,0:T(8,128)(2,1)S(1)} %collective-permute-done.6.refs_0_), channel_id=1, source_target_pairs={{0,1},{1,0},{2,3},{3,2},{4,5},{5,4},{6,7},{7,6},{8,9},{9,8},{10,11... | collective-permute-start | bytes 1671176 | tf_op jit(solution)/shard_map/ppermute | solution.py:451
  35.2 2.4 %collective-permute-start.9 = (bf16[128,2176]{1,0:T(8,128)(2,1)S(1)}, bf16[128,2176]{1,0:T(8,128)(2,1)S(1)}, u32[]{:S(2)}, u32[]{:S(2)}) collective-permute-start(bf16[128,2176]{1,0:T(8,128)(2,1)S(1)} %collective-permute-done.7.refs_2_), channel_id=1, source_target_pairs={{0,1},{1,0},{2,3},{3,2},{4,5},{5,4},{6,7},{7,6},{8,9},{9,8},{10,11... | collective-permute-start | bytes 1671176 | tf_op jit(solution)/shard_map/ppermute | solution.py:451
  35.2 14.6 %collective-permute-start.11 = (bf16[128,2176]{1,0:T(8,128)(2,1)S(1)}, bf16[128,2176]{1,0:T(8,128)(2,1)S(1)}, u32[]{:S(2)}, u32[]{:S(2)}) collective-permute-start(bf16[128,2176]{1,0:T(8,128)(2,1)S(1)} %collective-permute-done.6.refs_0_), channel_id=1, source_target_pairs={{0,4},{2,0},{4,8},{6,2},{8,12},{10,6},{12,14},{14,10},{5,1},{1,3},... | collective-permute-start | bytes 1671176 | tf_op jit(solution)/shard_map/ppermute | solution.py:445
  36.6 13.6 %collective-permute-start.12 = (bf16[128,2176]{1,0:T(8,128)(2,1)S(1)}, bf16[128,2176]{1,0:T(8,128)(2,1)S(1)}, u32[]{:S(2)}, u32[]{:S(2)}) collective-permute-start(bf16[128,2176]{1,0:T(8,128)(2,1)S(1)} %collective-permute-done.7.refs_2_), channel_id=1, source_target_pairs={{4,0},{0,2},{8,4},{2,6},{12,8},{6,10},{14,12},{10,14},{1,5},{3,1},... | collective-permute-start | bytes 1671176 | tf_op jit(solution)/shard_map/ppermute | solution.py:447
  40.0 19.1 %collective-permute-start.14 = (bf16[224,1408]{1,0:T(8,128)(2,1)S(1)}, bf16[224,1408]{1,0:T(8,128)(2,1)S(1)}, u32[]{:S(2)}, u32[]{:S(2)}) collective-permute-start(bf16[224,1408]{1,0:T(8,128)(2,1)S(1)} %get-tuple-element.132.mine_ref), channel_id=1, source_target_pairs={{0,16},{16,0},{1,17},{17,1},{2,18},{18,2},{3,19},{19,3},{4,20},{20... | collective-permute-start | bytes 1892360 | tf_op jit(solution)/shard_map/ppermute | solution.py:461
  50.2 2.3 %collective-permute-start.15 = (bf16[128,2176]{1,0:T(8,128)(2,1)S(1)}, bf16[128,2176]{1,0:T(8,128)(2,1)S(1)}, u32[]{:S(2)}, u32[]{:S(2)}) collective-permute-start(bf16[128,2176]{1,0:T(8,128)(2,1)S(1)} %collective-permute-done.11.refs_0_), channel_id=1, source_target_pairs={{0,1},{1,0},{2,3},{3,2},{4,5},{5,4},{6,7},{7,6},{8,9},{9,8},{10,11... | collective-permute-start | bytes 1671176 | tf_op jit(solution)/shard_map/ppermute | solution.py:451
  50.8 2.4 %collective-permute-start.16 = (bf16[128,2176]{1,0:T(8,128)(2,1)S(1)}, bf16[128,2176]{1,0:T(8,128)(2,1)S(1)}, u32[]{:S(2)}, u32[]{:S(2)}) collective-permute-start(bf16[128,2176]{1,0:T(8,128)(2,1)S(1)} %collective-permute-done.12.refs_2_), channel_id=1, source_target_pairs={{0,1},{1,0},{2,3},{3,2},{4,5},{5,4},{6,7},{7,6},{8,9},{9,8},{10,11... | collective-permute-start | bytes 1671176 | tf_op jit(solution)/shard_map/ppermute | solution.py:451
  50.8 6.5 %collective-permute-start.22 = (bf16[128,2048]{1,0:T(8,128)(2,1)S(1)}, bf16[128,2048]{1,0:T(8,128)(2,1)S(1)}, u32[]{:S(2)}, u32[]{:S(2)}) collective-permute-start(bf16[128,2048]{1,0:T(8,128)(2,1)S(1)} %get-tuple-element.157), channel_id=1, source_target_pairs={{0,1},{1,0},{2,3},{3,2},{4,5},{5,4},{6,7},{7,6},{8,9},{9,8},{10,11... | collective-permute-start | bytes 1572872 | tf_op jit(solution)/shard_map/ppermute | solution.py:471
  51.3 12.1 %collective-permute-start.13 = (bf16[128,2176]{1,0:T(8,128)(2,1)S(1)}, bf16[128,2176]{1,0:T(8,128)(2,1)S(1)}, u32[]{:S(2)}, u32[]{:S(2)}) collective-permute-start(bf16[128,2176]{1,0:T(8,128)(2,1)S(1)} %collective-permute-done.11.refs_0_), channel_id=1, source_target_pairs={{0,4},{2,0},{4,8},{6,2},{8,12},{10,6},{12,14},{14,10},{5,1},{1,3},... | collective-permute-start | bytes 1671176 | tf_op jit(solution)/shard_map/ppermute | solution.py:445
  55.6 16.5 %collective-permute-start.19 = (bf16[224,1408]{1,0:T(8,128)(2,1)S(1)}, bf16[224,1408]{1,0:T(8,128)(2,1)S(1)}, u32[]{:S(2)}, u32[]{:S(2)}) collective-permute-start(bf16[224,1408]{1,0:T(8,128)(2,1)S(1)} %get-tuple-element.146.mine_ref), channel_id=1, source_target_pairs={{0,16},{16,0},{1,17},{17,1},{2,18},{18,2},{3,19},{19,3},{4,20},{20... | collective-permute-start | bytes 1892360 | tf_op jit(solution)/shard_map/ppermute | solution.py:461
  57.5 9.2 %collective-permute-start.23 = (bf16[128,2048]{1,0:T(8,128)(2,1)S(1)}, bf16[128,2048]{1,0:T(8,128)(2,1)S(1)}, u32[]{:S(2)}, u32[]{:S(2)}) collective-permute-start(bf16[128,2048]{1,0:T(8,128)(2,1)S(1)} %add.16), channel_id=1, source_target_pairs={{0,4},{2,0},{4,8},{6,2},{8,12},{10,6},{12,14},{14,10},{5,1},{1,3},... | collective-permute-start | bytes 1572872 | tf_op jit(solution)/shard_map/ppermute | solution.py:476
  63.4 3.4 %collective-permute-start.21 = (bf16[128,2048]{1,0:T(8,128)(2,1)S(1)}, bf16[128,2048]{1,0:T(8,128)(2,1)S(1)}, u32[]{:S(2)}, u32[]{:S(2)}) collective-permute-start(bf16[128,2048]{1,0:T(8,128)(2,1)S(1)} %get-tuple-element.155), channel_id=1, source_target_pairs={{0,1},{1,0},{2,3},{3,2},{4,5},{5,4},{6,7},{7,6},{8,9},{9,8},{10,11... | collective-permute-start | bytes 1572872 | tf_op jit(solution)/shard_map/ppermute | solution.py:471
  63.4 5.0 %collective-permute-start.17 = (bf16[128,2176]{1,0:T(8,128)(2,1)S(1)}, bf16[128,2176]{1,0:T(8,128)(2,1)S(1)}, u32[]{:S(2)}, u32[]{:S(2)}) collective-permute-start(bf16[128,2176]{1,0:T(8,128)(2,1)S(1)} %collective-permute-done.13.refs_0_), channel_id=1, source_target_pairs={{0,1},{1,0},{2,3},{3,2},{4,5},{5,4},{6,7},{7,6},{8,9},{9,8},{10,11... | collective-permute-start | bytes 1671176 | tf_op jit(solution)/shard_map/ppermute | solution.py:451
  66.9 10.1 %collective-permute-start.24 = (bf16[128,2048]{1,0:T(8,128)(2,1)S(1)}, bf16[128,2048]{1,0:T(8,128)(2,1)S(1)}, u32[]{:S(2)}, u32[]{:S(2)}) collective-permute-start(bf16[128,2048]{1,0:T(8,128)(2,1)S(1)} %add.17), channel_id=1, source_target_pairs={{0,4},{2,0},{4,8},{6,2},{8,12},{10,6},{12,14},{14,10},{5,1},{1,3},... | collective-permute-start | bytes 1572872 | tf_op jit(solution)/shard_map/ppermute | solution.py:476
  70.7 8.4 %collective-permute-start.18 = (bf16[112,1408]{1,0:T(8,128)(2,1)S(1)}, bf16[112,1408]{1,0:T(8,128)(2,1)S(1)}, u32[]{:S(2)}, u32[]{:S(2)}) collective-permute-start(bf16[112,1408]{1,0:T(8,128)(2,1)S(1)} %get-tuple-element.164.mine_ref), channel_id=1, source_target_pairs={{0,16},{16,0},{1,17},{17,1},{2,18},{18,2},{3,19},{19,3},{4,20},{20... | collective-permute-start | bytes 946184 | tf_op jit(solution)/shard_map/ppermute | solution.py:461
  76.4 2.0 %collective-permute-start.20 = (bf16[128,2048]{1,0:T(8,128)(2,1)S(1)}, bf16[128,2048]{1,0:T(8,128)(2,1)S(1)}, u32[]{:S(2)}, u32[]{:S(2)}) collective-permute-start(bf16[128,2048]{1,0:T(8,128)(2,1)S(1)} %get-tuple-element.153), channel_id=1, source_target_pairs={{0,1},{1,0},{2,3},{3,2},{4,5},{5,4},{6,7},{7,6},{8,9},{9,8},{10,11... | collective-permute-start | bytes 1572872 | tf_op jit(solution)/shard_map/ppermute | solution.py:471
  76.5 20.6 %collective-permute-start.26 = (bf16[128,2048]{1,0:T(8,128)(2,1)S(1)}, bf16[128,2048]{1,0:T(8,128)(2,1)S(1)}, u32[]{:S(2)}, u32[]{:S(2)}) collective-permute-start(bf16[128,2048]{1,0:T(8,128)(2,1)S(1)} %get-tuple-element.161), channel_id=1, source_target_pairs={{0,1},{1,0},{2,3},{3,2},{4,5},{5,4},{6,7},{7,6},{8,9},{9,8},{10,11... | collective-permute-start | bytes 1572872 | tf_op jit(solution)/shard_map/ppermute | solution.py:471
  79.1 9.2 %collective-permute-start.28 = (bf16[128,2048]{1,0:T(8,128)(2,1)S(1)}, bf16[128,2048]{1,0:T(8,128)(2,1)S(1)}, u32[]{:S(2)}, u32[]{:S(2)}) collective-permute-start(bf16[128,2048]{1,0:T(8,128)(2,1)S(1)} %add.18), channel_id=1, source_target_pairs={{0,4},{2,0},{4,8},{6,2},{8,12},{10,6},{12,14},{14,10},{5,1},{1,3},... | collective-permute-start | bytes 1572872 | tf_op jit(solution)/shard_map/ppermute | solution.py:476
  84.7 3.6 %collective-permute-start.27 = (bf16[128,2048]{1,0:T(8,128)(2,1)S(1)}, bf16[128,2048]{1,0:T(8,128)(2,1)S(1)}, u32[]{:S(2)}, u32[]{:S(2)}) collective-permute-start(bf16[128,2048]{1,0:T(8,128)(2,1)S(1)} %get-tuple-element.169), channel_id=1, source_target_pairs={{0,1},{1,0},{2,3},{3,2},{4,5},{5,4},{6,7},{7,6},{8,9},{9,8},{10,11... | collective-permute-start | bytes 1572872 | tf_op jit(solution)/shard_map/ppermute | solution.py:471
  88.4 8.7 %collective-permute-start.32 = (bf16[128,1024]{1,0:T(8,128)(2,1)S(1)}, bf16[128,1024]{1,0:T(8,128)(2,1)S(1)}, u32[]{:S(2)}, u32[]{:S(2)}) collective-permute-start(bf16[128,1024]{1,0:T(8,128)(2,1)S(1)} %add.21), channel_id=1, source_target_pairs={{0,4},{2,0},{4,8},{6,2},{8,12},{10,6},{12,14},{14,10},{5,1},{1,3},... | collective-permute-start | bytes 786440 | tf_op jit(solution)/shard_map/ppermute | solution.py:476
  90.2 8.8 %collective-permute-start.29 = (bf16[128,1024]{1,0:T(8,128)(2,1)S(1)}, bf16[128,1024]{1,0:T(8,128)(2,1)S(1)}, u32[]{:S(2)}, u32[]{:S(2)}) collective-permute-start(bf16[128,1024]{1,0:T(8,128)(2,1)S(1)} %add.19.after_ref), channel_id=1, source_target_pairs={{0,4},{2,0},{4,8},{6,2},{8,12},{10,6},{12,14},{14,10},{5,1},{1,3},... | collective-permute-start | bytes 786440 | tf_op jit(solution)/shard_map/ppermute | solution.py:476
  90.9 8.8 %collective-permute-start.25 = (bf16[112,1408]{1,0:T(8,128)(2,1)S(1)}, bf16[112,1408]{1,0:T(8,128)(2,1)S(1)}, u32[]{:S(2)}, u32[]{:S(2)}) collective-permute-start(bf16[112,1408]{1,0:T(8,128)(2,1)S(1)} %get-tuple-element.159.mine_ref), channel_id=1, source_target_pairs={{0,16},{16,0},{1,17},{17,1},{2,18},{18,2},{3,19},{19,3},{4,20},{20... | collective-permute-start | bytes 946184 | tf_op jit(solution)/shard_map/ppermute | solution.py:461
  92.6 11.0 %collective-permute-start.31 = (bf16[128,2048]{1,0:T(8,128)(2,1)S(1)}, bf16[128,2048]{1,0:T(8,128)(2,1)S(1)}, u32[]{:S(2)}, u32[]{:S(2)}) collective-permute-start(bf16[128,2048]{1,0:T(8,128)(2,1)S(1)} %get-tuple-element.181), channel_id=1, source_target_pairs={{0,1},{1,0},{2,3},{3,2},{4,5},{5,4},{6,7},{7,6},{8,9},{9,8},{10,11... | collective-permute-start | bytes 1572872 | tf_op jit(solution)/shard_map/ppermute | solution.py:471
  97.2 6.4 %collective-permute-start.33 = (bf16[128,1024]{1,0:T(8,128)(2,1)S(1)}, bf16[128,1024]{1,0:T(8,128)(2,1)S(1)}, u32[]{:S(2)}, u32[]{:S(2)}) collective-permute-start(bf16[128,1024]{1,0:T(8,128)(2,1)S(1)} %add.22), channel_id=1, source_target_pairs={{0,4},{2,0},{4,8},{6,2},{8,12},{10,6},{12,14},{14,10},{5,1},{1,3},... | collective-permute-start | bytes 786440 | tf_op jit(solution)/shard_map/ppermute | solution.py:476
  99.7 6.7 %collective-permute-start.36 = (bf16[128,1024]{1,0:T(8,128)(2,1)S(1)}, bf16[128,1024]{1,0:T(8,128)(2,1)S(1)}, u32[]{:S(2)}, u32[]{:S(2)}) collective-permute-start(bf16[128,1024]{1,0:T(8,128)(2,1)S(1)} %add.20), channel_id=1, source_target_pairs={{0,4},{2,0},{4,8},{6,2},{8,12},{10,6},{12,14},{14,10},{5,1},{1,3},... | collective-permute-start | bytes 786440 | tf_op jit(solution)/shard_map/ppermute | solution.py:476
  101.0 11.3 %collective-permute-start.10 = (bf16[128,2048]{1,0:T(8,128)(2,1)S(1)}, bf16[128,2048]{1,0:T(8,128)(2,1)S(1)}, u32[]{:S(2)}, u32[]{:S(2)}) collective-permute-start(bf16[128,2048]{1,0:T(8,128)(2,1)S(1)} %get-tuple-element.128), channel_id=1, source_target_pairs={{0,1},{1,0},{2,3},{3,2},{4,5},{5,4},{6,7},{7,6},{8,9},{9,8},{10,11... | collective-permute-start | bytes 1572872 | tf_op jit(solution)/shard_map/ppermute | solution.py:471
  103.7 11.2 %collective-permute-start.34 = (bf16[128,1024]{1,0:T(8,128)(2,1)S(1)}, bf16[128,1024]{1,0:T(8,128)(2,1)S(1)}, u32[]{:S(2)}, u32[]{:S(2)}) collective-permute-start(bf16[128,1024]{1,0:T(8,128)(2,1)S(1)} %add.23), channel_id=1, source_target_pairs={{0,4},{2,0},{4,8},{6,2},{8,12},{10,6},{12,14},{14,10},{5,1},{1,3},... | collective-permute-start | bytes 786440 | tf_op jit(solution)/shard_map/ppermute | solution.py:476
  106.5 6.4 %collective-permute-start.37 = (bf16[128,1024]{1,0:T(8,128)(2,1)S(1)}, bf16[128,1024]{1,0:T(8,128)(2,1)S(1)}, u32[]{:S(2)}, u32[]{:S(2)}) collective-permute-start(bf16[128,1024]{1,0:T(8,128)(2,1)S(1)} %add.25), channel_id=1, source_target_pairs={{0,4},{2,0},{4,8},{6,2},{8,12},{10,6},{12,14},{14,10},{5,1},{1,3},... | collective-permute-start | bytes 786440 | tf_op jit(solution)/shard_map/ppermute | solution.py:476
  112.3 10.0 %collective-permute-start.30 = (bf16[128,2048]{1,0:T(8,128)(2,1)S(1)}, bf16[128,2048]{1,0:T(8,128)(2,1)S(1)}, u32[]{:S(2)}, u32[]{:S(2)}) collective-permute-start(bf16[128,2048]{1,0:T(8,128)(2,1)S(1)} %get-tuple-element.177), channel_id=1, source_target_pairs={{0,1},{1,0},{2,3},{3,2},{4,5},{5,4},{6,7},{7,6},{8,9},{9,8},{10,11... | collective-permute-start | bytes 1572872 | tf_op jit(solution)/shard_map/ppermute | solution.py:471
  113.0 8.3 %collective-permute-start.38 = (bf16[128,1024]{1,0:T(8,128)(2,1)S(1)}, bf16[128,1024]{1,0:T(8,128)(2,1)S(1)}, u32[]{:S(2)}, u32[]{:S(2)}) collective-permute-start(bf16[128,1024]{1,0:T(8,128)(2,1)S(1)} %add.26), channel_id=1, source_target_pairs={{0,4},{2,0},{4,8},{6,2},{8,12},{10,6},{12,14},{14,10},{5,1},{1,3},... | collective-permute-start | bytes 786440 | tf_op jit(solution)/shard_map/ppermute | solution.py:545
  115.0 7.3 %collective-permute-start.35 = (bf16[128,1024]{1,0:T(8,128)(2,1)S(1)}, bf16[128,1024]{1,0:T(8,128)(2,1)S(1)}, u32[]{:S(2)}, u32[]{:S(2)}) collective-permute-start(bf16[128,1024]{1,0:T(8,128)(2,1)S(1)} %add.24.after_ref), channel_id=1, source_target_pairs={{0,4},{2,0},{4,8},{6,2},{8,12},{10,6},{12,14},{14,10},{5,1},{1,3},... | collective-permute-start | bytes 786440 | tf_op jit(solution)/shard_map/ppermute | solution.py:545
